TPU v7x, 32 devices: a whole 2x2x4 slice. The times are simulated.
32 devices in a mesh: row: 4 (over y, x), col: 8 (over z, core).
Axes of the slice: x: 2, y: 2, z: 4, core: 2. Of those that a mesh axis runs over, the one named last changes fastest.
Arguments:
- activations: bfloat16 [64, 8192], P('col', 'row'), may hold values from -6 to 6
- out_grad: bfloat16 [64, 8192], P('col', 'row'), may hold values from -6 to 6
- w_gate: bfloat16 [8192, 28672], P('row', 'col'), may hold values from -0.0625 to 0.0625
- w_up: bfloat16 [8192, 28672], P('row', 'col'), may hold values from -0.0625 to 0.0625
- w_down: bfloat16 [28672, 8192], P('col', 'row'), may hold values from -0.03125 to 0.03125
Outputs:
- grad_input: bfloat16 [64, 8192], P('col', 'row')
- grad_w_gate: bfloat16 [8192, 28672], P('row', 'col')
- grad_w_up: bfloat16 [8192, 28672], P('row', 'col')
- grad_w_down: bfloat16 [28672, 8192], P('col', 'row')
All inputs are finite; a program needn't handle non-finite values.
Results may differ from a plain program's by a relative error of at most 0.0049.
Values may be sent and summed in bfloat16 or wider, within the bound.
No kernel may reach another device: no remote copies, remote signals or barrier semaphores. Data moves between devices by JAX's collectives and lax.ppermute only.
A program may use at most 128 MiB of HBM per device.

v0:
```python
import jax
import jax.numpy as jnp
from jax import lax
from jax.sharding import PartitionSpec as P


def swiglu_backward(sums, width):
    gate = sums[:, :width]
    upward = sums[:, width : 2 * width]
    back = sums[:, 2 * width :]
    sigma = jax.nn.sigmoid(gate)
    hidden = (gate * sigma * upward).astype(jnp.bfloat16)
    grad_gate = (back * upward * sigma * (1.0 + gate * (1.0 - sigma))).astype(jnp.bfloat16)
    grad_up = (back * gate * sigma).astype(jnp.bfloat16)
    return (hidden, grad_gate, grad_up)


def per_device(activations, out_grad, w_gate, w_up, w_down):
    tokens_all, grads_all = (
        lax.all_gather(activations, "col", axis=0, tiled=True),
        lax.all_gather(out_grad, "col", axis=0, tiled=True),
    )
    width = w_gate.shape[1]
    contract_last = (((1,), (1,)), ((), ()))
    contract_first = (((0,), (0,)), ((), ()))
    gate = jnp.dot(tokens_all, w_gate, preferred_element_type=jnp.float32)
    upward = jnp.dot(tokens_all, w_up, preferred_element_type=jnp.float32)
    back = lax.dot_general(grads_all, w_down, contract_last, preferred_element_type=jnp.float32)
    shares = lax.psum_scatter(
        jnp.concatenate([gate, upward, back], axis=1), "row", scatter_dimension=0, tiled=True
    )
    hidden_part, gate_part, up_part = swiglu_backward(shares, width)
    hidden, grad_gate, grad_up = (
        lax.all_gather(hidden_part, "row", axis=0, tiled=True),
        lax.all_gather(gate_part, "row", axis=0, tiled=True),
        lax.all_gather(up_part, "row", axis=0, tiled=True),
    )
    result = lax.dot_general(grad_gate, w_gate, contract_last, preferred_element_type=jnp.float32)
    grad_input = lax.psum_scatter(
        result + lax.dot_general(grad_up, w_up, contract_last, preferred_element_type=jnp.float32),
        "col",
        scatter_dimension=0,
        tiled=True,
    ).astype(jnp.bfloat16)
    grad_w_gate = lax.dot_general(
        tokens_all, grad_gate, contract_first, preferred_element_type=jnp.float32
    ).astype(jnp.bfloat16)
    grad_w_up = lax.dot_general(
        tokens_all, grad_up, contract_first, preferred_element_type=jnp.float32
    ).astype(jnp.bfloat16)
    grad_w_down = lax.dot_general(
        hidden, grads_all, contract_first, preferred_element_type=jnp.float32
    ).astype(jnp.bfloat16)
    return (grad_input, grad_w_gate, grad_w_up, grad_w_down)


def solution(mesh):
    in_specs = (P("col", "row"), P("col", "row"), P("row", "col"), P("row", "col"), P("col", "row"))
    out_specs = (P("col", "row"), P("row", "col"), P("row", "col"), P("col", "row"))
    return jax.shard_map(
        per_device, mesh=mesh, in_specs=in_specs, out_specs=out_specs, check_vma=False
    )
```

profile of v0, /device:TPU:0, one launch (start us, length us, event | category | flops | bytes accessed | tf_op | source)
XLA Modules:
  0.0 219.7 jit_solution(9096483197858155633)
XLA Ops:
  7.2 0.0 reduce-scatter.3.cloned.1.call-start
  7.2 0.0 copy-start
  7.2 16.2 %all_gather.15 = bf16[64,2048]{1,0:T(8,128)(2,1)S(1)} all-gather(bf16[8,2048]{1,0:T(8,128)(2,1)} %param.5), channel_id=1, replica_groups=mesh['row'=4,'col'=8] {'col'}, dimensions={0}, use_global_device_ids=true | all-gather | bytes 294912 | tf_op jit(solution)/shard_map/all_gather | solution.py:20
  23.5 7.8 %fusion.2 = f32[64,3584]{1,0:T(8,128)S(1)} fusion(bf16[64,2048]{1,0:T(8,128)(2,1)S(1)} %all_gather.15, bf16[2048,3584]{1,0:T(8,128)(2,1)} %param.7), kind=kOutput, calls=%fused_computation.11 | convolution fusion | flops 939524096 | bytes 15859712 | tf_op jit(solution)/shard_map/dot_general | solution.py:26
  31.3 2.6 %fusion.3 = f32[64,3584]{1,0:T(8,128)S(1)} fusion(bf16[64,2048]{1,0:T(8,128)(2,1)S(1)} %all_gather.15, bf16[2048,3584]{1,0:T(8,128)(2,1)S(1)} %copy-done), kind=kOutput, calls=%fused_computation.12 | convolution fusion | flops 939524096 | bytes 15859712 | tf_op jit(solution)/shard_map/dot_general | solution.py:27
  33.9 14.2 %all_gather.16 = bf16[64,2048]{1,0:T(8,128)(2,1)S(1)} all-gather(bf16[8,2048]{1,0:T(8,128)(2,1)S(1)} %copy-done.1), channel_id=1, replica_groups=mesh['row'=4,'col'=8] {'col'}, dimensions={0}, use_global_device_ids=true | all-gather | bytes 294912 | tf_op jit(solution)/shard_map/all_gather | solution.py:21
  48.1 9.7 %fusion.4 = f32[64,3584]{1,0:T(8,128)S(1)} fusion(bf16[64,2048]{1,0:T(8,128)(2,1)S(1)} %all_gather.16, bf16[3584,2048]{1,0:T(8,128)(2,1)} %param.9), kind=kOutput, calls=%fused_computation.13 | convolution fusion | flops 939524096 | bytes 15859712 | tf_op jit(solution)/shard_map/dot_general | solution.py:28
  57.8 1.7 pad_maximum_fusion
  59.5 0.0 reduce-scatter.3.cloned.1.call-update
  59.5 0.0 reduce-scatter.5.cloned.1.call-start
  59.6 41.9 %reduce-scatter.3.cloned.1.call-done = f32[16,10752]{1,0:T(8,128)} async-done(((f32[64,10752]{1,0:T(8,128)}), f32[16,10752]{1,0:T(8,128)}) %reduce-scatter.3.cloned.1.call-update) | async-done | bytes 688144 | tf_op jit(solution)/shard_map/reduce_scatter | solution.py:29
  101.5 1.3 multiply_convert_fusion
  102.8 9.7 %all_gather.17 = bf16[64,3584]{1,0:T(8,128)(2,1)S(1)} all-gather(bf16[16,3584]{1,0:T(8,128)(2,1)S(1)} %get-tuple-element.9), channel_id=1, replica_groups=mesh['row'=4,'col'=8] {'row'}, dimensions={0}, use_global_device_ids=true | all-gather | bytes 573440 | tf_op jit(solution)/shard_map/all_gather | solution.py:35
  112.5 9.7 %fusion.5 = f32[64,2048]{1,0:T(8,128)S(1)} fusion(bf16[64,3584]{1,0:T(8,128)(2,1)S(1)} %all_gather.17, bf16[2048,3584]{1,0:T(8,128)(2,1)} %param.7), kind=kOutput, calls=%fused_computation.14 | convolution fusion | flops 939524096 | bytes 15663104 | tf_op jit(solution)/shard_map/dot_general | solution.py:38
  122.2 7.6 %fusion = bf16[2048,3584]{0,1:T(8,128)(2,1)} fusion(bf16[64,3584]{1,0:T(8,128)(2,1)S(1)} %all_gather.17, bf16[64,2048]{1,0:T(8,128)(2,1)S(1)} %all_gather.15), kind=kOutput, calls=%fused_computation.3 | convolution fusion | flops 946864128 | bytes 15400960 | tf_op jit(solution)/shard_map/dot_general | solution.py:45
  129.8 9.6 %all_gather.18 = bf16[64,3584]{1,0:T(8,128)(2,1)S(1)} all-gather(bf16[16,3584]{1,0:T(8,128)(2,1)S(1)} %get-tuple-element.10), channel_id=1, replica_groups=mesh['row'=4,'col'=8] {'row'}, dimensions={0}, use_global_device_ids=true | all-gather | bytes 573440 | tf_op jit(solution)/shard_map/all_gather | solution.py:36
  139.4 7.6 %fusion.1 = bf16[2048,3584]{0,1:T(8,128)(2,1)} fusion(bf16[64,3584]{1,0:T(8,128)(2,1)S(1)} %all_gather.18, bf16[64,2048]{1,0:T(8,128)(2,1)S(1)} %all_gather.15), kind=kOutput, calls=%fused_computation.4 | convolution fusion | flops 946864128 | bytes 15400960 | tf_op jit(solution)/shard_map/dot_general | solution.py:48
  146.9 10.5 %convolution_add_fusion = f32[64,2048]{1,0:T(8,128)} fusion(f32[64,2048]{1,0:T(8,128)S(1)} %fusion.5, bf16[64,3584]{1,0:T(8,128)(2,1)S(1)} %all_gather.18, bf16[2048,3584]{1,0:T(8,128)(2,1)} %param.8), kind=kOutput, calls=%fused_computation.6 | convolution fusion | flops 939655168 | bytes 16187392 | tf_op jit(solution)/shard_map/dot_general | solution.py:40
  157.4 0.0 reduce-scatter.5.cloned.1.call-update
  157.5 18.7 %copy.10 = bf16[2048,3584]{1,0:T(8,128)(2,1)} copy(bf16[2048,3584]{0,1:T(8,128)(2,1)} %fusion.1) | data formatting | bytes 29360128
  176.1 18.6 %copy.9 = bf16[2048,3584]{1,0:T(8,128)(2,1)} copy(bf16[2048,3584]{0,1:T(8,128)(2,1)} %fusion) | data formatting | bytes 29360128
  194.8 9.1 %all_gather.19 = bf16[64,3584]{1,0:T(8,128)(2,1)S(1)} all-gather(bf16[16,3584]{1,0:T(8,128)(2,1)S(1)} %get-tuple-element.8), channel_id=1, replica_groups=mesh['row'=4,'col'=8] {'row'}, dimensions={0}, use_global_device_ids=true | all-gather | bytes 573440 | tf_op jit(solution)/shard_map/all_gather | solution.py:34
  203.9 7.6 %convolution_convert_fusion = bf16[3584,2048]{1,0:T(8,128)(2,1)} fusion(bf16[64,3584]{1,0:T(8,128)(2,1)S(1)} %all_gather.19, bf16[64,2048]{1,0:T(8,128)(2,1)S(1)} %all_gather.16), kind=kOutput, calls=%fused_computation | convolution fusion | flops 946864128 | bytes 15400960 | tf_op jit(solution)/shard_map/dot_general | solution.py:51
  211.4 1.5 convert_element_type.29
  (4 shorter events, 0.0 us)
Async XLA Ops:
  7.2 94.4 %reduce-scatter.3.cloned.1.call-start = ((), (), s32[]{:S(2)}) async-start(), calls=%async_computation.2 | async-start | bytes 3440640 | tf_op jit(solution)/shard_map/reduce_scatter | solution.py:29
  7.2 24.0 %copy-start = (bf16[2048,3584]{1,0:T(8,128)(2,1)S(1)}, bf16[2048,3584]{1,0:T(8,128)(2,1)}, u32[]{:S(2)}) copy-start(bf16[2048,3584]{1,0:T(8,128)(2,1)} %param.8) | copy-start | bytes 44040196
  31.3 2.6 %copy-start.1 = (bf16[8,2048]{1,0:T(8,128)(2,1)S(1)}, bf16[8,2048]{1,0:T(8,128)(2,1)}, u32[]{:S(2)}) copy-start(bf16[8,2048]{1,0:T(8,128)(2,1)} %param.6) | copy-start | bytes 98308
  59.5 151.9 %reduce-scatter.5.cloned.1.call-start = ((), (), s32[]{:S(2)}) async-start(), calls=%async_computation.3 | async-start | bytes 589824 | tf_op jit(solution)/shard_map/reduce_scatter | solution.py:39
Sparse Core Ops, SparseCore 0:
  59.7 41.8 reduce-scatter.2
  157.6 30.8 reduce-scatter.4
where the time goes:
time: 221 us; the launch traced here: 220 us
  matrix products  63 us (29%)
  blocking collectives  58.8 us (27%)
  waiting for transfers between devices  42 us (19%)
  local copies, waits for them, and re-layouts  37.3 us (17%)
  between operations  14.1 us (6%)
  other arithmetic  4.46 us (2%)
    reduce_scatter x1, waiting for transfers between devices, per_device(): lax.psum_scatter(jnp.concatenate([gate, upward, back], axis=1), 'row', sc...  41.9 us
    unnamed x6, local copies, waits for them, and re-layouts  37.3 us
    all_gather x1, blocking collectives, per_device(): lax.all_gather(activations, 'col', axis=0, tiled=True)  16.2 us
    all_gather x1, blocking collectives, per_device(): lax.all_gather(out_grad, 'col', axis=0, tiled=True)  14.2 us
    dot_general x1, matrix products, per_device(): lax.dot_general(grad_up, w_up, contract_last, preferred_element_type=jnp....  10.5 us
    dot_general x1, matrix products, per_device(): lax.dot_general(grads_all, w_down, contract_last, preferred_element_type=...  9.71 us
    dot_general x1, matrix products, per_device(): lax.dot_general(grad_gate, w_gate, contract_last, preferred_element_type=...  9.68 us
    all_gather x1, blocking collectives, per_device(): lax.all_gather(gate_part, 'row', axis=0, tiled=True)  9.68 us
  transfers between devices with their start and end apart: 2, of which 1 were waited for; matrix products, arithmetic and copies ran while one was open for 20% of the time, Pallas kernels for 0%

commit v1 on v0

v1 whole, which is shorter than its diff:
```python
import functools

import jax
import jax.numpy as jnp
from jax import lax
from jax.experimental import pallas as pl
from jax.experimental.pallas import tpu as pltpu
from jax.sharding import PartitionSpec as P

BF16, F32 = jnp.bfloat16, jnp.float32
HBM = pl.BlockSpec(memory_space=pl.ANY)
VMEM = pl.BlockSpec(memory_space=pltpu.VMEM)
SMEM = pl.BlockSpec(memory_space=pltpu.SMEM)
CONTRACT_LAST = (((1,), (1,)), ((), ()))
CONTRACT_FIRST = (((0,), (0,)), ((), ()))
CHUNKS = 2


def params(mib):
    return pltpu.CompilerParams(vmem_limit_bytes=mib << 20)


def tiles(width, tile=512):
    return [(at, min(tile, width - at)) for at in range(0, width, tile)]


def exchange(x, axis, size, offset):
    return lax.ppermute(x, axis, [(i, i ^ offset) for i in range(size)])


def order_kernel(rows, me_ref, mine_ref, other_ref, tokens_ref, grads_ref, scratch):
    me = me_ref[0]
    share = rows // 2
    n = mine_ref.shape[0] // rows
    total = tokens_ref.shape[0]
    per_row = total // scratch.shape[1]
    for half, out in ((0, tokens_ref), (1, grads_ref)):
        for k in range(n):
            for c, ref in ((0, mine_ref), (1, other_ref)):
                block = ref[k * rows : (k + 1) * rows, :].astype(F32)
                at = (2 * k + c) * share
                scratch[half, at // per_row, at % per_row : at % per_row + share, :] = block[
                    half * share : (half + 1) * share
                ]
        parts = [scratch[half, k ^ me] for k in range(scratch.shape[1])]
        out[...] = jnp.concatenate(parts, axis=0).astype(BF16)


def forward_kernel(start, width, own, tokens_ref, grads_ref, gate_ref, up_ref, down_ref, keep_ref, *send_refs):
    tokens, grads = tokens_ref[...], grads_ref[...]
    for at, size in tiles(width):
        cols = slice(start + at, start + at + size)
        gate = jnp.dot(tokens, gate_ref[:, cols], preferred_element_type=F32)
        upward = jnp.dot(tokens, up_ref[:, cols], preferred_element_type=F32)
        back = lax.dot_general(grads, down_ref[cols, :], CONTRACT_LAST, preferred_element_type=F32)
        for i, part in enumerate((gate, upward, back)):
            to = slice(i * width + at, i * width + at + size)
            keep_ref[:, to] = part[:own]
            for s, ref in enumerate(send_refs):
                ref[:, to] = part[(s + 1) * own : (s + 2) * own].astype(BF16)


def swiglu_kernel(width, keep_ref, *refs):
    out_ref = refs[-1]
    sums = keep_ref[...]
    for ref in refs[:-1]:
        sums = sums + ref[...].astype(F32)
    gate, upward, back = (sums[:, i * width : (i + 1) * width] for i in range(3))
    sigma = 1.0 / (1.0 + jnp.exp(-gate))
    out_ref[:, :width] = (back * upward * sigma * (1.0 + gate * (1.0 - sigma))).astype(BF16)
    out_ref[:, width : 2 * width] = (back * gate * sigma).astype(BF16)
    out_ref[:, 2 * width :] = (gate * sigma * upward).astype(BF16)


def input_kernel(start, width, first, last, n, me_ref, *refs):
    pieces, refs = refs[:n], refs[n:]
    gate_ref, up_ref = refs[:2]
    out_ref = refs[-1]
    grads = jnp.concatenate([ref[:, : 2 * width] for ref in pieces], axis=0)
    own = pieces[0].shape[0]
    for at, size in tiles(gate_ref.shape[0]):
        rows = slice(at, at + size)
        part = lax.dot_general(grads[:, :width], gate_ref[rows, start : start + width], CONTRACT_LAST, preferred_element_type=F32)
        part += lax.dot_general(grads[:, width:], up_ref[rows, start : start + width], CONTRACT_LAST, preferred_element_type=F32)
        if not first:
            part += refs[2][:, rows]
        if last:
            for k in range(n):
                out_ref[pl.ds(pl.multiple_of((k ^ me_ref[0]) * own, 8), own), rows] = part[k * own : (k + 1) * own]
        else:
            out_ref[:, rows] = part


def weights_kernel(n, tokens_ref, grads_ref, *refs):
    pieces = refs[: 3 * n]
    g_gate_ref, g_up_ref, g_down_ref = refs[-3:]
    grad_gate, grad_up, hidden = (jnp.concatenate([r[...] for r in pieces[i * n : (i + 1) * n]], axis=0) for i in range(3))
    g_gate_ref[...] = lax.dot_general(tokens_ref[...], grad_gate, CONTRACT_FIRST, preferred_element_type=F32).astype(BF16)
    g_up_ref[...] = lax.dot_general(tokens_ref[...], grad_up, CONTRACT_FIRST, preferred_element_type=F32).astype(BF16)
    g_down_ref[...] = lax.dot_general(hidden, grads_ref[...], CONTRACT_FIRST, preferred_element_type=F32).astype(BF16)


def per_device(n_row, n_col, activations, out_grad, w_gate, w_up, w_down):
    share, depth = activations.shape
    hidden = w_gate.shape[1]
    total = share * n_col
    own = total // n_row
    me = lax.axis_index("row").astype(jnp.int32).reshape(1)
    shape = jax.ShapeDtypeStruct

    mine = jnp.concatenate([activations, out_grad], axis=0)
    near = jnp.concatenate([mine] + [exchange(mine, "col", n_col, 2 * k) for k in range(1, n_col // 2)], axis=0)
    far = exchange(near, "col", n_col, 1)
    tokens, grads = pl.pallas_call(
        functools.partial(order_kernel, 2 * share),
        out_shape=[pltpu.VMEM((total, depth), BF16)] * 2,
        in_specs=[SMEM, VMEM, VMEM],
        out_specs=[VMEM] * 2,
        scratch_shapes=[pltpu.VMEM((2, n_row, own, depth), F32)],
        compiler_params=params(6),
        name="order",
    )(me, near, far)

    w_gate, w_up, w_down = (pltpu.with_memory_space_constraint(w, pltpu.VMEM) for w in (w_gate, w_up, w_down))

    unit = 256 if hidden % 256 == 0 else 128
    cuts = [unit * (hidden // unit * i // CHUNKS) for i in range(CHUNKS + 1)]
    spans = [(a, b - a) for a, b in zip(cuts[:-1], cuts[1:])]

    partial = []
    for start, width in spans:
        keep, *sends = pl.pallas_call(
            functools.partial(forward_kernel, start, width, own),
            out_shape=[pltpu.VMEM((own, 3 * width), F32)] + [pltpu.VMEM((own, 3 * width), BF16)] * (n_row - 1),
            in_specs=[VMEM] * 5,
            out_specs=[VMEM] * n_row,
            compiler_params=params(8),
            name="forward",
        )(tokens, grads, w_gate, w_up, w_down)
        partial.append([keep] + [exchange(x, "row", n_row, s + 1) for s, x in enumerate(sends)])

    pieces = []
    for (start, width), parts in zip(spans, partial):
        mine = pl.pallas_call(
            functools.partial(swiglu_kernel, width),
            out_shape=pltpu.VMEM((own, 3 * width), BF16),
            in_specs=[VMEM] * n_row,
            out_specs=VMEM,
            compiler_params=params(8),
            name="swiglu",
        )(*parts)
        pieces.append([mine] + [exchange(mine, "row", n_row, s) for s in range(1, n_row)])

    grad_input, outs = None, None
    for i, ((start, width), parts) in enumerate(zip(spans, pieces)):
        grad_input = pl.pallas_call(
            functools.partial(input_kernel, start, width, i == 0, i == CHUNKS - 1, n_row),
            out_shape=pltpu.VMEM((total, depth), F32),
            in_specs=[SMEM] + [VMEM] * (n_row + 2 + (i > 0)),
            out_specs=VMEM,
            compiler_params=params(8),
            name="input_grad",
        )(me, *parts, w_gate, w_up, *([grad_input] if i else []))
    for i, ((start, width), parts) in enumerate(zip(spans, pieces)):
        tile = 256 if width % 256 == 0 else 128
        n = width // tile
        first = start // tile
        piece = lambda j: pl.BlockSpec((own, tile), lambda t, j=j: (0, j * n + t))
        outs = pl.pallas_call(
            functools.partial(weights_kernel, n_row),
            grid=(n,),
            out_shape=[shape((depth, hidden), BF16)] * 2 + [shape((hidden, depth), BF16)],
            in_specs=[pl.BlockSpec((total, depth), lambda t: (0, 0))] * 2
            + [piece(j) for j in range(3) for _ in range(n_row)]
            + [HBM] * (3 if i else 0),
            out_specs=[pl.BlockSpec((depth, tile), lambda t: (0, first + t))] * 2
            + [pl.BlockSpec((tile, depth), lambda t: (first + t, 0))],
            input_output_aliases={2 + 3 * n_row + k: k for k in range(3)} if i else {},
            compiler_params=params(14),
            name="weight_grads",
        )(tokens, grads, *(parts * 3), *(outs if i else ()))

    blocks = grad_input.reshape(n_col // 2, 2, share, depth)
    summed = blocks[:, 0] + exchange(blocks[:, 1], "col", n_col, 1)
    result = summed[0]
    for k in range(1, n_col // 2):
        result = result + exchange(summed[k], "col", n_col, 2 * k)
    return (result.astype(BF16), *outs)


def solution(mesh):
    in_specs = (P("col", "row"), P("col", "row"), P("row", "col"), P("row", "col"), P("col", "row"))
    out_specs = (P("col", "row"), P("row", "col"), P("row", "col"), P("col", "row"))
    return jax.shard_map(
        functools.partial(per_device, mesh.shape["row"], mesh.shape["col"]),
        mesh=mesh,
        in_specs=in_specs,
        out_specs=out_specs,
        check_vma=False,
    )
```

time: 221 us -> 111 us (0.50)
  matrix products: 63 us -> 0 us
  blocking collectives: 58.8 us -> 0 us
  Pallas kernels: 0 us -> 38.2 us
  starting transfers between devices: 0.08 us -> 25.8 us
  waiting for transfers between devices: 42 us -> 17.8 us
  between operations: 14.1 us -> 0.78 us
  local copies, waits for them, and re-layouts: 37.3 us -> 27.4 us
  other arithmetic: 4.46 us -> 0.66 us
    dot_general x8 -> x0, matrix products: 63 us -> none  [the longest x1 10.5 us: per_device(): lax.dot_general(grad_up, w_up, contract_last, preferred_element_type=jnp....]
    all_gather x5 -> x0, blocking collectives: 58.8 us -> none  [the longest x1 16.2 us: per_device(): lax.all_gather(activations, 'col', axis=0, tiled=True)]
    reduce_scatter x2 -> x0, waiting for transfers between devices: 41.9 us -> none  [the longest x1 41.9 us: per_device(): lax.psum_scatter(jnp.concatenate([gate, upward, back], axis=1), 'row', sc...]
    pallas_call x0 -> x9, Pallas kernels: none -> 38.2 us  [the longest x2 19.2 us: per_device(): pl.pallas_call(functools.partial(weights_kernel, n_row), grid=(n,), out_s...]
    ppermute x0 -> x20, starting transfers between devices: none -> 25.8 us  [exchange(): return lax.ppermute(x, axis, [(i, i ^ offset) for i in range(size)])]
    ppermute x0 -> x20, waiting for transfers between devices: none -> 17.8 us  [exchange(): return lax.ppermute(x, axis, [(i, i ^ offset) for i in range(size)])]
    unnamed x6 -> x13, local copies, waits for them, and re-layouts: 37.3 us -> 26.6 us
  transfers between devices with their start and end apart: 2 -> 20, of which waited for: 1 -> 6; matrix products, arithmetic and copies ran while one was open for 20% -> 0% of each run, Pallas kernels for 0% -> 26%
where the time goes in v1:
time: 111 us
  Pallas kernels  38.2 us (34%)
  local copies, waits for them, and re-layouts  27.4 us (25%)
  starting transfers between devices  25.8 us (23%)
  waiting for transfers between devices  17.8 us (16%)
    unnamed x13, local copies, waits for them, and re-layouts  26.6 us
    ppermute x20, starting transfers between devices, exchange(): return lax.ppermute(x, axis, [(i, i ^ offset) for i in range(size)])  25.8 us
    pallas_call x2, Pallas kernels, per_device(): pl.pallas_call(functools.partial(weights_kernel, n_row), grid=(n,), out_s...  19.2 us
    ppermute x20, waiting for transfers between devices, exchange(): return lax.ppermute(x, axis, [(i, i ^ offset) for i in range(size)])  17.8 us
    pallas_call x2, Pallas kernels, per_device(): pl.pallas_call(functools.partial(forward_kernel, start, width, own), out_...  9.54 us
    pallas_call x2, Pallas kernels, per_device(): pl.pallas_call(functools.partial(input_kernel, start, width, i == 0, i ==...  9 us
  transfers between devices with their start and end apart: 20, of which 6 were waited for; matrix products, arithmetic and copies ran while one was open for 0% of the time, Pallas kernels for 26%

profile of v1, /device:TPU:0, one launch (start us, length us, event | category | flops | bytes accessed | tf_op | source)
XLA Modules:
  0.0 110.6 jit_solution(17136775609022829281)
XLA Ops:
  2.2 3.0 %collective-permute-start = (bf16[16,2048]{1,0:T(8,128)(2,1)S(1)}, bf16[16,2048]{1,0:T(8,128)(2,1)S(1)}, u32[]{:S(2)}, u32[]{:S(2)}) collective-permute-start(bf16[16,2048]{1,0:T(8,128)(2,1)S(1)} %get-tuple-element.39), channel_id=1, source_target_pairs={{0,2},{1,3},{2,0},{3,1},{4,6},{5,7},{6,4},{7,5},{8,10},{9,11},{10,... | collective-permute-start | bytes 196616 | tf_op jit(solution)/shard_map/ppermute | solution.py:28
  5.2 2.5 %collective-permute-start.2 = (bf16[16,2048]{1,0:T(8,128)(2,1)S(1)}, bf16[16,2048]{1,0:T(8,128)(2,1)S(1)}, u32[]{:S(2)}, u32[]{:S(2)}) collective-permute-start(bf16[16,2048]{1,0:T(8,128)(2,1)S(1)} %get-tuple-element.39), channel_id=1, source_target_pairs={{0,6},{1,7},{2,4},{3,5},{4,2},{5,3},{6,0},{7,1},{8,14},{9,15},{10,... | collective-permute-start | bytes 196616 | tf_op jit(solution)/shard_map/ppermute | solution.py:28
  7.8 6.3 %collective-permute-done.1 = bf16[16,2048]{1,0:T(8,128)(2,1)S(1)} collective-permute-done((bf16[16,2048]{1,0:T(8,128)(2,1)S(1)}, bf16[16,2048]{1,0:T(8,128)(2,1)S(1)}, u32[]{:S(2)}, u32[]{:S(2)}) %collective-permute-start.1) | collective-permute-done | bytes 65568 | tf_op jit(solution)/shard_map/ppermute | solution.py:28
  15.9 5.2 %copy-done = bf16[2048,3584]{1,0:T(8,128)(2,1)S(1)} copy-done((bf16[2048,3584]{1,0:T(8,128)(2,1)S(1)}, bf16[2048,3584]{1,0:T(8,128)(2,1)}, u32[]{:S(2)}) %copy-start) | copy-done | bytes 14680088
  21.0 5.2 %copy-done.2 = bf16[2048,3584]{1,0:T(8,128)(2,1)S(1)} copy-done((bf16[2048,3584]{1,0:T(8,128)(2,1)S(1)}, bf16[2048,3584]{1,0:T(8,128)(2,1)}, u32[]{:S(2)}) %copy-start.2) | copy-done | bytes 14680088
  26.2 5.2 %copy-done.4 = bf16[3584,2048]{1,0:T(8,128)(2,1)S(1)} copy-done((bf16[3584,2048]{1,0:T(8,128)(2,1)S(1)}, bf16[3584,2048]{1,0:T(8,128)(2,1)}, u32[]{:S(2)}) %copy-start.4) | copy-done | bytes 14680088
  31.4 4.8 %forward.3 = (f32[16,5376]{1,0:T(8,128)S(1)}, bf16[16,5376]{1,0:T(8,128)(2,1)S(1)}, bf16[16,5376]{1,0:T(8,128)(2,1)S(1)}, bf16[16,5376]{1,0:T(8,128)(2,1)S(1)}) custom-call(bf16[64,2048]{1,0:T(8,128)(2,1)S(1)} %get-tuple-element.20.tokens_ref, bf16[64,2048]{1,0:T(8,128)(2,1)S(1)} %get-tuple-element.21.grads_ref, bf16[2048,3584]{1,0:T(8,128)(2,1)S(1)} %copy-done, ...), custom_call_target="tpu_custom_call" | custom-call | tf_op jit(solution)/shard_map/forward/pallas_call | solution.py:132
  36.2 1.6 %collective-permute-start.10 = (bf16[16,5376]{1,0:T(8,128)(2,1)S(1)}, bf16[16,5376]{1,0:T(8,128)(2,1)S(1)}, u32[]{:S(2)}, u32[]{:S(2)}) collective-permute-start(bf16[16,5376]{1,0:T(8,128)(2,1)S(1)} %get-tuple-element.27), channel_id=1, source_target_pairs={{0,8},{8,0},{16,24},{24,16},{1,9},{9,1},{17,25},{25,17},{2,10},{10... | collective-permute-start | bytes 516104 | tf_op jit(solution)/shard_map/ppermute | solution.py:28
  37.7 1.5 %collective-permute-start.11 = (bf16[16,5376]{1,0:T(8,128)(2,1)S(1)}, bf16[16,5376]{1,0:T(8,128)(2,1)S(1)}, u32[]{:S(2)}, u32[]{:S(2)}) collective-permute-start(bf16[16,5376]{1,0:T(8,128)(2,1)S(1)} %get-tuple-element.28), channel_id=1, source_target_pairs={{0,16},{8,24},{16,0},{24,8},{1,17},{9,25},{17,1},{25,9},{2,18},{10... | collective-permute-start | bytes 516104 | tf_op jit(solution)/shard_map/ppermute | solution.py:28
  39.7 4.8 %forward.2 = (f32[16,5376]{1,0:T(8,128)S(1)}, bf16[16,5376]{1,0:T(8,128)(2,1)S(1)}, bf16[16,5376]{1,0:T(8,128)(2,1)S(1)}, bf16[16,5376]{1,0:T(8,128)(2,1)S(1)}) custom-call(bf16[64,2048]{1,0:T(8,128)(2,1)S(1)} %get-tuple-element.20.tokens_ref, bf16[64,2048]{1,0:T(8,128)(2,1)S(1)} %get-tuple-element.21.grads_ref, bf16[2048,3584]{1,0:T(8,128)(2,1)S(1)} %copy-done, ...), custom_call_target="tpu_custom_call" | custom-call | tf_op jit(solution)/shard_map/forward/pallas_call | solution.py:132
  44.5 1.6 %collective-permute-start.4 = (bf16[16,5376]{1,0:T(8,128)(2,1)S(1)}, bf16[16,5376]{1,0:T(8,128)(2,1)S(1)}, u32[]{:S(2)}, u32[]{:S(2)}) collective-permute-start(bf16[16,5376]{1,0:T(8,128)(2,1)S(1)} %get-tuple-element.23), channel_id=1, source_target_pairs={{0,8},{8,0},{16,24},{24,16},{1,9},{9,1},{17,25},{25,17},{2,10},{10... | collective-permute-start | bytes 516104 | tf_op jit(solution)/shard_map/ppermute | solution.py:28
  48.2 2.5 %collective-permute-start.15 = (bf16[16,5376]{1,0:T(8,128)(2,1)S(1)}, bf16[16,5376]{1,0:T(8,128)(2,1)S(1)}, u32[]{:S(2)}, u32[]{:S(2)}) collective-permute-start(bf16[16,5376]{1,0:T(8,128)(2,1)S(1)} %swiglu.3.refs_0_.refs_4_.refs_8_), channel_id=1, source_target_pairs={{0,24},{8,16},{16,8},{24,0},{1,25},{9,17},{17,9},{25,1},{2,26},{10... | collective-permute-start | bytes 516104 | tf_op jit(solution)/shard_map/ppermute | solution.py:28
  51.5 1.9 %collective-permute-start.13 = (bf16[16,5376]{1,0:T(8,128)(2,1)S(1)}, bf16[16,5376]{1,0:T(8,128)(2,1)S(1)}, u32[]{:S(2)}, u32[]{:S(2)}) collective-permute-start(bf16[16,5376]{1,0:T(8,128)(2,1)S(1)} %swiglu.3.refs_0_.refs_4_.refs_8_), channel_id=1, source_target_pairs={{0,8},{8,0},{16,24},{24,16},{1,9},{9,1},{17,25},{25,17},{2,10},{10... | collective-permute-start | bytes 516104 | tf_op jit(solution)/shard_map/ppermute | solution.py:28
  53.4 6.0 %collective-permute-done.5.refs_1_ = bf16[16,5376]{1,0:T(8,128)(2,1)S(1)} collective-permute-done((bf16[16,5376]{1,0:T(8,128)(2,1)S(1)}, bf16[16,5376]{1,0:T(8,128)(2,1)S(1)}, u32[]{:S(2)}, u32[]{:S(2)}) %collective-permute-start.5) | collective-permute-done | bytes 172064 | tf_op jit(solution)/shard_map/ppermute | solution.py:28
  59.5 2.2 %collective-permute-start.9 = (bf16[16,5376]{1,0:T(8,128)(2,1)S(1)}, bf16[16,5376]{1,0:T(8,128)(2,1)S(1)}, u32[]{:S(2)}, u32[]{:S(2)}) collective-permute-start(bf16[16,5376]{1,0:T(8,128)(2,1)S(1)} %swiglu.2.refs_0_.refs_4_.refs_8_), channel_id=1, source_target_pairs={{0,24},{8,16},{16,8},{24,0},{1,25},{9,17},{17,9},{25,1},{2,26},{10... | collective-permute-start | bytes 516104 | tf_op jit(solution)/shard_map/ppermute | solution.py:28
  64.0 2.1 %collective-permute-done.14.refs_2_.refs_6_.refs_10_ = bf16[16,5376]{1,0:T(8,128)(2,1)S(1)} collective-permute-done((bf16[16,5376]{1,0:T(8,128)(2,1)S(1)}, bf16[16,5376]{1,0:T(8,128)(2,1)S(1)}, u32[]{:S(2)}, u32[]{:S(2)}) %collective-permute-start.14) | collective-permute-done | bytes 172064 | tf_op jit(solution)/shard_map/ppermute | solution.py:28
  66.1 5.2 %copy-done.1 = bf16[2048,3584]{1,0:T(8,128)(2,1)S(1)} copy-done((bf16[2048,3584]{1,0:T(8,128)(2,1)S(1)}, bf16[2048,3584]{1,0:T(8,128)(2,1)}, u32[]{:S(2)}) %copy-start.1) | copy-done | bytes 14680088
  71.3 5.2 %copy-done.3 = bf16[2048,3584]{1,0:T(8,128)(2,1)S(1)} copy-done((bf16[2048,3584]{1,0:T(8,128)(2,1)S(1)}, bf16[2048,3584]{1,0:T(8,128)(2,1)}, u32[]{:S(2)}) %copy-start.3) | copy-done | bytes 14680088
  76.5 4.5 %input_grad.2.refs_6_ = f32[64,2048]{1,0:T(8,128)S(1)} custom-call(s32[1]{0:T(128)} %bitcast.me_ref, bf16[16,5376]{1,0:T(8,128)(2,1)S(1)} %swiglu.3.refs_0_.refs_4_.refs_8_, bf16[16,5376]{1,0:T(8,128)(2,1)S(1)} %collective-permute-done.13.refs_1_.refs_5_.refs_9_, bf16[16,5376]{1,0:T(8,128)(2,1)S(1)} %collective-permute-done.14.refs_2_.refs_6_.refs_10_, ...), custom_call_target="tpu_custom_call" | custom-call | tf_op jit(solution)/shard_map/input_grad/pallas_call | solution.py:156
  81.0 4.5 %input_grad.3 = f32[64,2048]{1,0:T(8,128)S(1)} custom-call(s32[1]{0:T(128)} %bitcast.me_ref, bf16[16,5376]{1,0:T(8,128)(2,1)S(1)} %swiglu.2.refs_0_.refs_4_.refs_8_, bf16[16,5376]{1,0:T(8,128)(2,1)S(1)} %collective-permute-done.7.refs_1_.refs_5_.refs_9_, bf16[16,5376]{1,0:T(8,128)(2,1)S(1)} %collective-permute-done.8.refs_2_.refs_6_.refs_10_, ...), custom_call_target="tpu_custom_call" | custom-call | tf_op jit(solution)/shard_map/input_grad/pallas_call | solution.py:156
  85.6 1.5 %collective-permute-done.16 = f32[4,8,2048]{2,1,0:T(8,128)S(1)} collective-permute-done((f32[4,8,2048]{2,1,0:T(8,128)S(1)}, f32[4,8,2048]{2,1,0:T(8,128)S(1)}, u32[]{:S(2)}, u32[]{:S(2)}) %collective-permute-start.16) | collective-permute-done | bytes 262176 | tf_op jit(solution)/shard_map/ppermute | solution.py:28
  87.3 2.5 %collective-permute-start.19 = (f32[8,2048]{1,0:T(8,128)S(1)}, f32[8,2048]{1,0:T(8,128)S(1)}, u32[]{:S(2)}, u32[]{:S(2)}) collective-permute-start(f32[8,2048]{1,0:T(8,128)S(1)} %get-tuple-element.37), channel_id=1, source_target_pairs={{0,6},{1,7},{2,4},{3,5},{4,2},{5,3},{6,0},{7,1},{8,14},{9,15},{10,... | collective-permute-start | bytes 196616 | tf_op jit(solution)/shard_map/ppermute | solution.py:28
  90.7 9.6 %weight_grads.2 = (bf16[2048,3584]{1,0:T(8,128)(2,1)}, bf16[2048,3584]{1,0:T(8,128)(2,1)}, bf16[3584,2048]{1,0:T(8,128)(2,1)}) custom-call(bf16[64,2048]{1,0:T(8,128)(2,1)S(1)} %get-tuple-element.20.tokens_ref, bf16[64,2048]{1,0:T(8,128)(2,1)S(1)} %get-tuple-element.21.grads_ref, bf16[16,5376]{1,0:T(8,128)(2,1)S(1)} %swiglu.3.refs_0_.refs_4_.refs_8_, ...), custom_call_target="tpu_custom_call" | custom-call | tf_op jit(solution)/shard_map/weight_grads/pallas_call | solution.py:169
  100.3 9.6 %weight_grads.3 = (bf16[2048,3584]{1,0:T(8,128)(2,1)}, bf16[2048,3584]{1,0:T(8,128)(2,1)}, bf16[3584,2048]{1,0:T(8,128)(2,1)}) custom-call(bf16[64,2048]{1,0:T(8,128)(2,1)S(1)} %get-tuple-element.20.tokens_ref, bf16[64,2048]{1,0:T(8,128)(2,1)S(1)} %get-tuple-element.21.grads_ref, ...), custom_call_target="tpu_custom_call", output_to_operand_aliasing={{0}: (14, {}), {1}: (15, {}), {2}: (16, {})} | custom-call | tf_op jit(solution)/shard_map/weight_grads/pallas_call | solution.py:169
  (44 shorter events, 11.0 us)
Async XLA Ops:
  2.2 5.6 %collective-permute-start = (bf16[16,2048]{1,0:T(8,128)(2,1)S(1)}, bf16[16,2048]{1,0:T(8,128)(2,1)S(1)}, u32[]{:S(2)}, u32[]{:S(2)}) collective-permute-start(bf16[16,2048]{1,0:T(8,128)(2,1)S(1)} %get-tuple-element.39), channel_id=1, source_target_pairs={{0,2},{1,3},{2,0},{3,1},{4,6},{5,7},{6,4},{7,5},{8,10},{9,11},{10,... | collective-permute-start | bytes 196616 | tf_op jit(solution)/shard_map/ppermute | solution.py:28
  5.2 8.9 %collective-permute-start.2 = (bf16[16,2048]{1,0:T(8,128)(2,1)S(1)}, bf16[16,2048]{1,0:T(8,128)(2,1)S(1)}, u32[]{:S(2)}, u32[]{:S(2)}) collective-permute-start(bf16[16,2048]{1,0:T(8,128)(2,1)S(1)} %get-tuple-element.39), channel_id=1, source_target_pairs={{0,6},{1,7},{2,4},{3,5},{4,2},{5,3},{6,0},{7,1},{8,14},{9,15},{10,... | collective-permute-start | bytes 196616 | tf_op jit(solution)/shard_map/ppermute | solution.py:28
  7.7 6.4 %collective-permute-start.1 = (bf16[16,2048]{1,0:T(8,128)(2,1)S(1)}, bf16[16,2048]{1,0:T(8,128)(2,1)S(1)}, u32[]{:S(2)}, u32[]{:S(2)}) collective-permute-start(bf16[16,2048]{1,0:T(8,128)(2,1)S(1)} %get-tuple-element.39), channel_id=1, source_target_pairs={{0,4},{1,5},{2,6},{3,7},{4,0},{5,1},{6,2},{7,3},{8,12},{9,13},{10,... | collective-permute-start | bytes 196616 | tf_op jit(solution)/shard_map/ppermute | solution.py:28
  14.1 1.6 %collective-permute-start.3 = (bf16[64,2048]{1,0:T(8,128)(2,1)S(1)}, bf16[64,2048]{1,0:T(8,128)(2,1)S(1)}, u32[]{:S(2)}, u32[]{:S(2)}) collective-permute-start(bf16[64,2048]{1,0:T(8,128)(2,1)S(1)} %constant_dynamic-update-slice_fusion.2.mine_ref), channel_id=1, source_target_pairs={{0,1},{1,0},{2,3},{3,2},{4,5},{5,4},{6,7},{7,6},{8,9},{9,8},{10,11... | collective-permute-start | bytes 786440 | tf_op jit(solution)/shard_map/ppermute | solution.py:28
  15.9 5.2 %copy-start = (bf16[2048,3584]{1,0:T(8,128)(2,1)S(1)}, bf16[2048,3584]{1,0:T(8,128)(2,1)}, u32[]{:S(2)}) copy-start(bf16[2048,3584]{1,0:T(8,128)(2,1)} %refs_4_.3) | copy-start | bytes 44040196
  21.0 5.2 %copy-start.2 = (bf16[2048,3584]{1,0:T(8,128)(2,1)S(1)}, bf16[2048,3584]{1,0:T(8,128)(2,1)}, u32[]{:S(2)}) copy-start(bf16[2048,3584]{1,0:T(8,128)(2,1)} %refs_5_.3) | copy-start | bytes 44040196
  26.2 5.2 %copy-start.4 = (bf16[3584,2048]{1,0:T(8,128)(2,1)S(1)}, bf16[3584,2048]{1,0:T(8,128)(2,1)}, u32[]{:S(2)}) copy-start(bf16[3584,2048]{1,0:T(8,128)(2,1)} %down_ref.3) | copy-start | bytes 44040196
  36.2 11.4 %collective-permute-start.10 = (bf16[16,5376]{1,0:T(8,128)(2,1)S(1)}, bf16[16,5376]{1,0:T(8,128)(2,1)S(1)}, u32[]{:S(2)}, u32[]{:S(2)}) collective-permute-start(bf16[16,5376]{1,0:T(8,128)(2,1)S(1)} %get-tuple-element.27), channel_id=1, source_target_pairs={{0,8},{8,0},{16,24},{24,16},{1,9},{9,1},{17,25},{25,17},{2,10},{10... | collective-permute-start | bytes 516104 | tf_op jit(solution)/shard_map/ppermute | solution.py:28
  37.7 10.3 %collective-permute-start.11 = (bf16[16,5376]{1,0:T(8,128)(2,1)S(1)}, bf16[16,5376]{1,0:T(8,128)(2,1)S(1)}, u32[]{:S(2)}, u32[]{:S(2)}) collective-permute-start(bf16[16,5376]{1,0:T(8,128)(2,1)S(1)} %get-tuple-element.28), channel_id=1, source_target_pairs={{0,16},{8,24},{16,0},{24,8},{1,17},{9,25},{17,1},{25,9},{2,18},{10... | collective-permute-start | bytes 516104 | tf_op jit(solution)/shard_map/ppermute | solution.py:28
  39.2 8.8 %collective-permute-start.12 = (bf16[16,5376]{1,0:T(8,128)(2,1)S(1)}, bf16[16,5376]{1,0:T(8,128)(2,1)S(1)}, u32[]{:S(2)}, u32[]{:S(2)}) collective-permute-start(bf16[16,5376]{1,0:T(8,128)(2,1)S(1)} %get-tuple-element.29), channel_id=1, source_target_pairs={{0,24},{8,16},{16,8},{24,0},{1,25},{9,17},{17,9},{25,1},{2,26},{10... | collective-permute-start | bytes 516104 | tf_op jit(solution)/shard_map/ppermute | solution.py:28
  44.5 7.0 %collective-permute-start.4 = (bf16[16,5376]{1,0:T(8,128)(2,1)S(1)}, bf16[16,5376]{1,0:T(8,128)(2,1)S(1)}, u32[]{:S(2)}, u32[]{:S(2)}) collective-permute-start(bf16[16,5376]{1,0:T(8,128)(2,1)S(1)} %get-tuple-element.23), channel_id=1, source_target_pairs={{0,8},{8,0},{16,24},{24,16},{1,9},{9,1},{17,25},{25,17},{2,10},{10... | collective-permute-start | bytes 516104 | tf_op jit(solution)/shard_map/ppermute | solution.py:28
  46.1 13.3 %collective-permute-start.5 = (bf16[16,5376]{1,0:T(8,128)(2,1)S(1)}, bf16[16,5376]{1,0:T(8,128)(2,1)S(1)}, u32[]{:S(2)}, u32[]{:S(2)}) collective-permute-start(bf16[16,5376]{1,0:T(8,128)(2,1)S(1)} %get-tuple-element.24), channel_id=1, source_target_pairs={{0,16},{8,24},{16,0},{24,8},{1,17},{9,25},{17,1},{25,9},{2,18},{10... | collective-permute-start | bytes 516104 | tf_op jit(solution)/shard_map/ppermute | solution.py:28
  47.6 11.8 %collective-permute-start.6 = (bf16[16,5376]{1,0:T(8,128)(2,1)S(1)}, bf16[16,5376]{1,0:T(8,128)(2,1)S(1)}, u32[]{:S(2)}, u32[]{:S(2)}) collective-permute-start(bf16[16,5376]{1,0:T(8,128)(2,1)S(1)} %get-tuple-element.25), channel_id=1, source_target_pairs={{0,24},{8,16},{16,8},{24,0},{1,25},{9,17},{17,9},{25,1},{2,26},{10... | collective-permute-start | bytes 516104 | tf_op jit(solution)/shard_map/ppermute | solution.py:28
  48.2 14.4 %collective-permute-start.15 = (bf16[16,5376]{1,0:T(8,128)(2,1)S(1)}, bf16[16,5376]{1,0:T(8,128)(2,1)S(1)}, u32[]{:S(2)}, u32[]{:S(2)}) collective-permute-start(bf16[16,5376]{1,0:T(8,128)(2,1)S(1)} %swiglu.3.refs_0_.refs_4_.refs_8_), channel_id=1, source_target_pairs={{0,24},{8,16},{16,8},{24,0},{1,25},{9,17},{17,9},{25,1},{2,26},{10... | collective-permute-start | bytes 516104 | tf_op jit(solution)/shard_map/ppermute | solution.py:28
  50.7 15.4 %collective-permute-start.14 = (bf16[16,5376]{1,0:T(8,128)(2,1)S(1)}, bf16[16,5376]{1,0:T(8,128)(2,1)S(1)}, u32[]{:S(2)}, u32[]{:S(2)}) collective-permute-start(bf16[16,5376]{1,0:T(8,128)(2,1)S(1)} %swiglu.3.refs_0_.refs_4_.refs_8_), channel_id=1, source_target_pairs={{0,16},{8,24},{16,0},{24,8},{1,17},{9,25},{17,1},{25,9},{2,18},{10... | collective-permute-start | bytes 516104 | tf_op jit(solution)/shard_map/ppermute | solution.py:28
  51.5 14.6 %collective-permute-start.13 = (bf16[16,5376]{1,0:T(8,128)(2,1)S(1)}, bf16[16,5376]{1,0:T(8,128)(2,1)S(1)}, u32[]{:S(2)}, u32[]{:S(2)}) collective-permute-start(bf16[16,5376]{1,0:T(8,128)(2,1)S(1)} %swiglu.3.refs_0_.refs_4_.refs_8_), channel_id=1, source_target_pairs={{0,8},{8,0},{16,24},{24,16},{1,9},{9,1},{17,25},{25,17},{2,10},{10... | collective-permute-start | bytes 516104 | tf_op jit(solution)/shard_map/ppermute | solution.py:28
  59.5 21.4 %collective-permute-start.9 = (bf16[16,5376]{1,0:T(8,128)(2,1)S(1)}, bf16[16,5376]{1,0:T(8,128)(2,1)S(1)}, u32[]{:S(2)}, u32[]{:S(2)}) collective-permute-start(bf16[16,5376]{1,0:T(8,128)(2,1)S(1)} %swiglu.2.refs_0_.refs_4_.refs_8_), channel_id=1, source_target_pairs={{0,24},{8,16},{16,8},{24,0},{1,25},{9,17},{17,9},{25,1},{2,26},{10... | collective-permute-start | bytes 516104 | tf_op jit(solution)/shard_map/ppermute | solution.py:28
  61.8 19.2 %collective-permute-start.8 = (bf16[16,5376]{1,0:T(8,128)(2,1)S(1)}, bf16[16,5376]{1,0:T(8,128)(2,1)S(1)}, u32[]{:S(2)}, u32[]{:S(2)}) collective-permute-start(bf16[16,5376]{1,0:T(8,128)(2,1)S(1)} %swiglu.2.refs_0_.refs_4_.refs_8_), channel_id=1, source_target_pairs={{0,16},{8,24},{16,0},{24,8},{1,17},{9,25},{17,1},{25,9},{2,18},{10... | collective-permute-start | bytes 516104 | tf_op jit(solution)/shard_map/ppermute | solution.py:28
  62.6 18.4 %collective-permute-start.7 = (bf16[16,5376]{1,0:T(8,128)(2,1)S(1)}, bf16[16,5376]{1,0:T(8,128)(2,1)S(1)}, u32[]{:S(2)}, u32[]{:S(2)}) collective-permute-start(bf16[16,5376]{1,0:T(8,128)(2,1)S(1)} %swiglu.2.refs_0_.refs_4_.refs_8_), channel_id=1, source_target_pairs={{0,8},{8,0},{16,24},{24,16},{1,9},{9,1},{17,25},{25,17},{2,10},{10... | collective-permute-start | bytes 516104 | tf_op jit(solution)/shard_map/ppermute | solution.py:28
  66.1 5.2 %copy-start.1 = (bf16[2048,3584]{1,0:T(8,128)(2,1)S(1)}, bf16[2048,3584]{1,0:T(8,128)(2,1)}, u32[]{:S(2)}) copy-start(bf16[2048,3584]{1,0:T(8,128)(2,1)} %refs_4_.3) | copy-start | bytes 44040196
  85.5 1.6 %collective-permute-start.16 = (f32[4,8,2048]{2,1,0:T(8,128)S(1)}, f32[4,8,2048]{2,1,0:T(8,128)S(1)}, u32[]{:S(2)}, u32[]{:S(2)}) collective-permute-start(f32[4,8,2048]{2,1,0:T(8,128)S(1)} %slice_bitcast_fusion), channel_id=1, source_target_pairs={{0,1},{1,0},{2,3},{3,2},{4,5},{5,4},{6,7},{7,6},{8,9},{9,8},{10,11... | collective-permute-start | bytes 786440 | tf_op jit(solution)/shard_map/ppermute | solution.py:28
  87.2 22.8 %collective-permute-start.17 = (f32[8,2048]{1,0:T(8,128)S(1)}, f32[8,2048]{1,0:T(8,128)S(1)}, u32[]{:S(2)}, u32[]{:S(2)}) collective-permute-start(f32[8,2048]{1,0:T(8,128)S(1)} %get-tuple-element.36), channel_id=1, source_target_pairs={{0,2},{1,3},{2,0},{3,1},{4,6},{5,7},{6,4},{7,5},{8,10},{9,11},{10,... | collective-permute-start | bytes 196616 | tf_op jit(solution)/shard_map/ppermute | solution.py:28
  87.3 22.7 %collective-permute-start.19 = (f32[8,2048]{1,0:T(8,128)S(1)}, f32[8,2048]{1,0:T(8,128)S(1)}, u32[]{:S(2)}, u32[]{:S(2)}) collective-permute-start(f32[8,2048]{1,0:T(8,128)S(1)} %get-tuple-element.37), channel_id=1, source_target_pairs={{0,6},{1,7},{2,4},{3,5},{4,2},{5,3},{6,0},{7,1},{8,14},{9,15},{10,... | collective-permute-start | bytes 196616 | tf_op jit(solution)/shard_map/ppermute | solution.py:28
  89.8 20.2 %collective-permute-start.18 = (f32[8,2048]{1,0:T(8,128)S(1)}, f32[8,2048]{1,0:T(8,128)S(1)}, u32[]{:S(2)}, u32[]{:S(2)}) collective-permute-start(f32[8,2048]{1,0:T(8,128)S(1)} %get-tuple-element.38), channel_id=1, source_target_pairs={{0,4},{1,5},{2,6},{3,7},{4,0},{5,1},{6,2},{7,3},{8,12},{9,13},{10,... | collective-permute-start | bytes 196616 | tf_op jit(solution)/shard_map/ppermute | solution.py:28
  (1 other events, 5.2 us)

commit v2 on v0

v2 whole, which is shorter than its diff:
```python
import functools

import jax
import jax.numpy as jnp
from jax import lax
from jax.experimental import pallas as pl
from jax.experimental.pallas import tpu as pltpu
from jax.sharding import PartitionSpec as P

BF16, F32 = jnp.bfloat16, jnp.float32
HBM = pl.BlockSpec(memory_space=pl.ANY)
VMEM = pl.BlockSpec(memory_space=pltpu.VMEM)
SMEM = pl.BlockSpec(memory_space=pltpu.SMEM)
CONTRACT_LAST = (((1,), (1,)), ((), ()))
CONTRACT_FIRST = (((0,), (0,)), ((), ()))
PARAMS = pltpu.CompilerParams(vmem_limit_bytes=14 << 20)
vmem = pltpu.VMEM
shape = jax.ShapeDtypeStruct


def exchange(x, axis, size, offset):
    return lax.ppermute(x, axis, [(i, i ^ offset) for i in range(size)])


def tiles(width, tile):
    return [(at, min(tile, width - at)) for at in range(0, width, tile)]


def join_kernel(*refs):
    rows = refs[0].shape[0]
    for i, ref in enumerate(refs[:-2]):
        refs[-1][i * rows : (i + 1) * rows, :] = ref[...]


def order_kernel(rows, me_ref, mine_ref, other_ref, tokens_ref, grads_ref, turned_ref, scratch):
    me = me_ref[0]
    share = rows // 2
    n = mine_ref.shape[0] // rows
    total = tokens_ref.shape[0]
    per_row = total // scratch.shape[1]
    for half, out in ((0, tokens_ref), (1, grads_ref)):
        for k in range(n):
            for c, ref in ((0, mine_ref), (1, other_ref)):
                block = ref[k * rows : (k + 1) * rows, :].astype(F32)
                at = (2 * k + c) * share
                scratch[half, at // per_row, at % per_row : at % per_row + share, :] = block[
                    half * share : (half + 1) * share
                ]
        parts = [scratch[half, k ^ me] for k in range(scratch.shape[1])]
        rows_in_order = jnp.concatenate(parts, axis=0)
        out[...] = rows_in_order.astype(BF16)
        if half == 0:
            turned_ref[...] = rows_in_order.T.astype(BF16)


def weights_copies(sources, wanted, targets, sems):
    copies = []
    for i, ((which, start, width), target) in enumerate(zip(wanted, targets)):
        part = pl.ds(start, width)
        source = sources[which].at[part] if which == 2 else sources[which].at[:, part]
        copies.append(pltpu.make_async_copy(source, target, sems.at[i]))
    return copies


def fetch_kernel(wanted, me_ref, *refs):
    sources, targets, (done_ref, sems) = refs[:3], refs[3:-2], refs[-2:]
    copies = weights_copies(sources, wanted, targets, sems)
    for copy in copies:
        copy.start()
    done_ref[...] = jnp.zeros_like(done_ref)
    for copy in copies:
        copy.wait()


def forward_kernel(start, width, ready, wanted, own, sends, tile, tokens_ref, grads_ref, gate_ref, up_ref, *refs):
    if ready:
        down_ref, refs = refs[0], refs[1:]
    sources, refs = refs[:3], refs[4:]
    keep_ref, send_refs, refs = refs[0], refs[1 : 1 + sends], refs[1 + sends :]
    targets, refs = refs[: len(wanted)], refs[len(wanted) :]
    if not ready:
        down_ref, refs = refs[0], refs[1:]
        wanted, targets = ((2, start, width), *wanted), (down_ref, *targets)
    copies = weights_copies(sources, wanted, targets, refs[0])
    for copy in copies:
        copy.start()

    def put(i, at, part):
        to = pl.ds(pl.multiple_of(i * width + at, tile), tile)
        keep_ref[:, to] = part[:own]
        for s, ref in enumerate(send_refs):
            ref[:, to] = part[(s + 1) * own : (s + 2) * own].astype(BF16)

    @pl.loop(0, width // tile)
    def _(t):
        at = pl.multiple_of(t * tile, tile)
        put(0, at, jnp.dot(tokens_ref[...], gate_ref[:, pl.ds(at, tile)], preferred_element_type=F32))
        put(1, at, jnp.dot(tokens_ref[...], up_ref[:, pl.ds(at, tile)], preferred_element_type=F32))

    if not ready:
        copies[0].wait()

    @pl.loop(0, width // tile)
    def _(t):
        at = pl.multiple_of(t * tile, tile)
        down = down_ref[pl.ds(at, tile), :]
        put(2, at, lax.dot_general(grads_ref[...], down, CONTRACT_LAST, preferred_element_type=F32))

    for copy in copies[0 if ready else 1 :]:
        copy.wait()


def swiglu_kernel(width, n, after_ref, keep_ref, *refs):
    pieces, refs = refs[: n - 1], refs[n - 1 :]
    later, out_ref, send_refs = refs[: len(refs) // 2], refs[len(refs) // 2], refs[len(refs) // 2 + 1 :]
    sums = keep_ref[...]
    for ref in pieces:
        sums = sums + ref[:, : 3 * width].astype(F32)
    gate, upward, back = (sums[:, i * width : (i + 1) * width] for i in range(3))
    sigma = 1.0 / (1.0 + jnp.exp(-gate))
    parts = (back * upward * sigma * (1.0 + gate * (1.0 - sigma)), back * gate * sigma, gate * sigma * upward)
    for i, part in enumerate(parts):
        out_ref[:, i * width : (i + 1) * width] = part.astype(BF16)
    for before, after in zip(later, send_refs):
        split = before.shape[1]
        after[:, :split] = before[...]
        after[:, split:] = out_ref[...]


def input_kernel(width, n, me_ref, *refs):
    pieces, (gate_ref, up_ref, sum_ref, out_ref) = refs[:n], refs[n:]
    grads = jnp.concatenate([ref[:, : 2 * width] for ref in pieces], axis=0)
    own = pieces[0].shape[0]
    for at, size in tiles(gate_ref.shape[0], 512):
        rows = slice(at, at + size)
        part = lax.dot_general(grads[:, :width], gate_ref[rows, :], CONTRACT_LAST, preferred_element_type=F32)
        part += lax.dot_general(grads[:, width:], up_ref[rows, :], CONTRACT_LAST, preferred_element_type=F32)
        part += sum_ref[:, rows]
        for k in range(n):
            out_ref[pl.ds(pl.multiple_of((k ^ me_ref[0]) * own, 8), own), rows] = part[k * own : (k + 1) * own]


def backward_kernel(n, start, width, shift, begin, count, tile, n_in, adds, turned_ref, grads_ref, *refs):
    mine_ref, pieces, refs = refs[0], refs[1:n], refs[n:]
    bufs, sems = refs[-4:-1], refs[-1]
    outs, sum_refs = refs[n_in : n_in + 3], refs[n_in + 3 : -4]
    turned, grads = turned_ref[...], grads_ref[...]
    copies = []
    for t in range(count):
        slot, at = t % 2, begin + t * tile

        def rows(j):
            cols = j * width + at
            parts = [mine_ref[:, cols : cols + tile]] + [r[:, shift + cols : shift + cols + tile] for r in pieces]
            return jnp.concatenate(parts, axis=0)

        grad_gate, grad_up, hidden = rows(0), rows(1), rows(2)
        to = pl.ds(start + at, tile)
        if t >= 2:
            for copy in copies[t - 2]:
                copy.wait()
        targets = (outs[0].at[:, to], outs[1].at[:, to], outs[2].at[to])
        copies.append([pltpu.make_async_copy(b.at[slot], o, sems.at[slot, j]) for j, (b, o) in enumerate(zip(bufs, targets))])
        bufs[0][slot] = jnp.dot(turned, grad_gate, preferred_element_type=F32).astype(BF16)
        copies[t][0].start()
        bufs[1][slot] = jnp.dot(turned, grad_up, preferred_element_type=F32).astype(BF16)
        copies[t][1].start()
        bufs[2][slot] = lax.dot_general(hidden, grads, CONTRACT_FIRST, preferred_element_type=F32).astype(BF16)
        copies[t][2].start()
        for sum_ref in sum_refs:
            gate_ref, up_ref = refs[:2]
            part = lax.dot_general(grad_gate, gate_ref[:, at : at + tile], CONTRACT_LAST, preferred_element_type=F32)
            part += lax.dot_general(grad_up, up_ref[:, at : at + tile], CONTRACT_LAST, preferred_element_type=F32)
            if t > 0:
                part += sum_ref[...]
            elif adds:
                part += refs[2][...]
            sum_ref[...] = part
    for group in copies[-2:]:
        for copy in group:
            copy.wait()


def per_device(n_row, n_col, activations, out_grad, w_gate, w_up, w_down):
    share, depth = activations.shape
    hidden = w_gate.shape[1]
    total = share * n_col
    own = total // n_row
    me = lax.axis_index("row").astype(jnp.int32).reshape(1)
    w_gate, w_up, w_down = (pltpu.with_memory_space_constraint(w, pltpu.HBM) for w in (w_gate, w_up, w_down))
    unit = next(u for u in (512, 256, 128) if hidden % u == 0)
    small = max(unit // 2, 128)
    units = hidden // unit
    cuts = [0, 2 * units // 7 * unit, 4 * units // 7 * unit, hidden]
    one, two, three = ((a, b - a) for a, b in zip(cuts[:-1], cuts[1:]))

    def held(wanted):
        return [vmem((width, depth) if which == 2 else (depth, width), BF16) for which, _, width in wanted]

    mine = jnp.concatenate([activations, out_grad], axis=0)
    wanted = ((0, *one), (1, *one), (2, *one), (0, *two))
    gate_one, up_one, down_one, gate_two, fetched = pl.pallas_call(
        functools.partial(fetch_kernel, wanted),
        out_shape=held(wanted) + [shape((8, 128), F32)],
        in_specs=[SMEM] + [HBM] * 3,
        out_specs=[VMEM] * 5,
        scratch_shapes=[pltpu.SemaphoreType.DMA((4,))],
        compiler_params=PARAMS,
        name="fetch",
    )(me, w_gate, w_up, w_down)
    others = [exchange(mine, "col", n_col, 2 * k) for k in range(1, n_col // 2)]
    near = pl.pallas_call(
        join_kernel,
        out_shape=vmem((n_col * share, depth), BF16),
        in_specs=[VMEM] * (n_col // 2 + 1),
        out_specs=VMEM,
        compiler_params=PARAMS,
        name="join",
    )(mine, *others, fetched)
    far = exchange(near, "col", n_col, 1)
    tokens, grads, turned = pl.pallas_call(
        functools.partial(order_kernel, 2 * share),
        out_shape=[vmem((total, depth), BF16)] * 2 + [vmem((depth, total), BF16)],
        in_specs=[SMEM] + [VMEM] * 2,
        out_specs=[VMEM] * 3,
        scratch_shapes=[vmem((2, n_row, own, depth), F32)],
        compiler_params=PARAMS,
        name="order",
    )(me, near, far)

    def forward(start, width, gate, up, down, wanted, after):
        ready = down is not None
        keep, *rest = pl.pallas_call(
            functools.partial(forward_kernel, start, width, ready, wanted, own, n_row - 1, unit),
            out_shape=[vmem((own, 3 * width), F32)] + [vmem((own, 3 * width), BF16)] * (n_row - 1) + held(wanted),
            in_specs=[VMEM] * (5 if ready else 4) + [HBM] * 4,
            out_specs=[VMEM] * (n_row + len(wanted)),
            scratch_shapes=([] if ready else [vmem((width, depth), BF16)]) + [pltpu.SemaphoreType.DMA((3,))],
            compiler_params=PARAMS,
            name="forward",
        )(tokens, grads, gate, up, *([down] if ready else []), w_gate, w_up, w_down, after)
        return keep, rest[: n_row - 1], rest[n_row - 1 :]

    def to_others(blocks):
        return [exchange(x, "row", n_row, s + 1) for s, x in enumerate(blocks)]

    def swiglu(width, keep, got, later, after):
        mine, *sends = pl.pallas_call(
            functools.partial(swiglu_kernel, width, n_row),
            out_shape=[vmem((own, 3 * width), BF16)] + [vmem((own, x.shape[1] + 3 * width), BF16) for x in later],
            in_specs=[HBM] + [VMEM] * (n_row + len(later)),
            out_specs=[VMEM] * (1 + len(later)),
            compiler_params=PARAMS,
            name="swiglu",
        )(after, keep, *got, *later)
        return mine, sends

    def backward(start, width, shift, begin, count, tile, pieces, weights, outs, after, name):
        known = 2 + n_row + len(weights)
        return pl.pallas_call(
            functools.partial(
                backward_kernel, n_row, start, width, shift, begin, count // tile, tile,
                len(weights) + len(outs) + 1, len(weights) > 2,
            ),
            out_shape=[shape((depth, hidden), BF16)] * 2
            + [shape((hidden, depth), BF16)]
            + ([vmem((total, depth), F32)] if weights else []),
            in_specs=[VMEM] * known + [HBM] * (len(outs) + 1),
            out_specs=[HBM] * 3 + ([VMEM] if weights else []),
            input_output_aliases={known + k: k for k in range(len(outs))},
            scratch_shapes=[vmem((2, depth, tile), BF16)] * 2
            + [vmem((2, tile, depth), BF16), pltpu.SemaphoreType.DMA((2, 3))],
            compiler_params=PARAMS,
            name=name,
        )(turned, grads, *pieces, *weights, *outs, after)

    keep_one, sends, (up_two, gate_three) = forward(*one, gate_one, up_one, down_one, ((1, *two), (0, *three)), me)
    got_one = to_others(sends)
    keep_two, sends, (up_three,) = forward(*two, gate_two, up_two, None, ((1, *three),), me)
    mine_one, sends = swiglu(one[1], keep_one, got_one, sends, me)
    got_two = to_others(sends)
    keep_three, sends, _ = forward(*three, gate_three, up_three, None, (), mine_one)
    mine_two, sends = swiglu(two[1], keep_two, got_two, sends, me)
    got_three = to_others(sends)
    *outs, grad_input = backward(
        *one, 3 * two[1], 0, one[1], small, [mine_one, *got_two], (gate_one, up_one), (), mine_two, "backward_one"
    )
    mine_three, _ = swiglu(three[1], keep_three, got_three, (), grad_input)
    got_last = to_others([mine_three] * (n_row - 1))
    *outs, grad_input = backward(
        *two, 3 * three[1], 0, two[1], small, [mine_two, *got_three], (gate_two, up_two, grad_input), outs, mine_three, "backward_two"
    )
    pieces = [mine_three, *got_last]
    grad_input = pl.pallas_call(
        functools.partial(input_kernel, three[1], n_row),
        out_shape=vmem((total, depth), F32),
        in_specs=[SMEM] + [VMEM] * (n_row + 3),
        out_specs=VMEM,
        compiler_params=PARAMS,
        name="input_grad",
    )(me, *pieces, gate_three, up_three, grad_input)
    outs = backward(*three, 0, 0, unit, small, pieces, (), outs, me, "weight_grads_early")
    blocks = grad_input.reshape(n_col // 2, 2, share, depth)
    summed = blocks[:, 0] + exchange(blocks[:, 1], "col", n_col, 1)
    summed, *outs = lax.optimization_barrier((summed, *outs))
    outs = backward(*three, 0, unit, three[1] - unit, small, pieces, (), outs, me, "weight_grads")
    result = summed[0]
    for k in range(1, n_col // 2):
        result = result + exchange(summed[k], "col", n_col, 2 * k)
    return (result.astype(BF16), *outs)


def solution(mesh):
    in_specs = (P("col", "row"), P("col", "row"), P("row", "col"), P("row", "col"), P("col", "row"))
    out_specs = (P("col", "row"), P("row", "col"), P("row", "col"), P("col", "row"))
    return jax.shard_map(
        functools.partial(per_device, mesh.shape["row"], mesh.shape["col"]),
        mesh=mesh,
        in_specs=in_specs,
        out_specs=out_specs,
        check_vma=False,
    )
```

time: 221 us -> 84.4 us (0.38)
  matrix products: 63 us -> 0 us
  blocking collectives: 58.8 us -> 0 us
  Pallas kernels: 0 us -> 46.9 us
  local copies, waits for them, and re-layouts: 37.3 us -> 1.55 us
  waiting for transfers between devices: 42 us -> 9.91 us
  starting transfers between devices: 0.08 us -> 24.2 us
  between operations: 14.1 us -> 0.88 us
  other arithmetic: 4.46 us -> 0.67 us
    dot_general x8 -> x0, matrix products: 63 us -> none  [the longest x1 10.5 us: per_device(): lax.dot_general(grad_up, w_up, contract_last, preferred_element_type=jnp....]
    all_gather x5 -> x0, blocking collectives: 58.8 us -> none  [the longest x1 16.2 us: per_device(): lax.all_gather(activations, 'col', axis=0, tiled=True)]
    pallas_call x0 -> x14, Pallas kernels: none -> 46.9 us  [the longest x4 22.8 us: backward(): pl.pallas_call(functools.partial(backward_kernel, n_row, start, width, sh...]
    reduce_scatter x2 -> x0, waiting for transfers between devices: 41.9 us -> none  [the longest x1 41.9 us: per_device(): lax.psum_scatter(jnp.concatenate([gate, upward, back], axis=1), 'row', sc...]
    unnamed x6 -> x1, local copies, waits for them, and re-layouts: 37.3 us -> 0.76 us
    ppermute x0 -> x20, starting transfers between devices: none -> 24.2 us  [exchange(): return lax.ppermute(x, axis, [(i, i ^ offset) for i in range(size)])]
    ppermute x0 -> x20, waiting for transfers between devices: none -> 9.91 us  [exchange(): return lax.ppermute(x, axis, [(i, i ^ offset) for i in range(size)])]
  transfers between devices with their start and end apart: 2 -> 20, of which waited for: 1 -> 5; matrix products, arithmetic and copies ran while one was open for 20% -> 0% of each run, Pallas kernels for 0% -> 45%
where the time goes in v2:
time: 84.4 us; the launch traced here: 84.1 us
  Pallas kernels  46.9 us (56%)
  starting transfers between devices  24.2 us (29%)
  waiting for transfers between devices  9.91 us (12%)
  local copies, waits for them, and re-layouts  1.55 us (2%)
  between operations  0.88 us (1%)
    ppermute x20, starting transfers between devices, exchange(): return lax.ppermute(x, axis, [(i, i ^ offset) for i in range(size)])  24.2 us
    pallas_call x4, Pallas kernels, backward(): pl.pallas_call(functools.partial(backward_kernel, n_row, start, width, sh...  22.8 us
    pallas_call x3, Pallas kernels, forward(): pl.pallas_call(functools.partial(forward_kernel, start, width, ready, wan...  13.5 us
    ppermute x20, waiting for transfers between devices, exchange(): return lax.ppermute(x, axis, [(i, i ^ offset) for i in range(size)])  9.91 us
    pallas_call x1, Pallas kernels, per_device(): pl.pallas_call(functools.partial(fetch_kernel, wanted), out_shape=held(wa...  6.11 us
    pallas_call x1, Pallas kernels, per_device(): pl.pallas_call(functools.partial(input_kernel, three[1], n_row), out_shap...  3.88 us
  transfers between devices with their start and end apart: 20, of which 5 were waited for; matrix products, arithmetic and copies ran while one was open for 0% of the time, Pallas kernels for 45%

profile of v2, /device:TPU:0, one launch (start us, length us, event | category | flops | bytes accessed | tf_op | source)
XLA Modules:
  0.0 84.1 jit_solution(4610850313798545643)
XLA Ops:
  2.2 5.0 %collective-permute-start.2 = (bf16[16,2048]{1,0:T(8,128)(2,1)S(1)}, bf16[16,2048]{1,0:T(8,128)(2,1)S(1)}, u32[]{:S(2)}, u32[]{:S(2)}) collective-permute-start(bf16[16,2048]{1,0:T(8,128)(2,1)S(1)} %constant_dynamic-update-slice_fusion.refs_0_), channel_id=1, source_target_pairs={{0,6},{1,7},{2,4},{3,5},{4,2},{5,3},{6,0},{7,1},{8,14},{9,15},{10,... | collective-permute-start | bytes 196616 | tf_op jit(solution)/shard_map/ppermute | solution.py:22
  7.8 6.1 %fetch.1 = (bf16[2048,1024]{1,0:T(8,128)(2,1)S(1)}, bf16[2048,1024]{1,0:T(8,128)(2,1)S(1)}, bf16[1024,2048]{1,0:T(8,128)(2,1)S(1)}, bf16[2048,1024]{1,0:T(8,128)(2,1)S(1)}, f32[8,128]{1,0:T(8,128)S(1)}) custom-call(s32[1]{0:T(128)} %bitcast.me_ref.refs_4_.refs_3_.after_ref.refs_7_, bf16[2048,3584]{1,0:T(8,128)(2,1)} %refs_0_.5, bf16[2048,3584]{1,0:T(8,128)(2,1)} %refs_1_.7, ...), custom_call_target="tpu_custom_call" | custom-call | tf_op jit(solution)/shard_map/fetch/pallas_call | solution.py:202
  14.0 1.5 %collective-permute-done.3.other_ref = bf16[64,2048]{1,0:T(8,128)(2,1)S(1)} collective-permute-done((bf16[64,2048]{1,0:T(8,128)(2,1)S(1)}, bf16[64,2048]{1,0:T(8,128)(2,1)S(1)}, u32[]{:S(2)}, u32[]{:S(2)}) %collective-permute-start.3) | collective-permute-done | bytes 262176 | tf_op jit(solution)/shard_map/ppermute | solution.py:22
  15.9 4.1 %forward.3 = (f32[16,3072]{1,0:T(8,128)S(1)}, bf16[16,3072]{1,0:T(8,128)(2,1)S(1)}, bf16[16,3072]{1,0:T(8,128)(2,1)S(1)}, bf16[16,3072]{1,0:T(8,128)(2,1)S(1)}, ...) custom-call(bf16[64,2048]{1,0:T(8,128)(2,1)S(1)} %get-tuple-element.56.tokens_ref, ...), custom_call_target="tpu_custom_call" | custom-call | tf_op jit(solution)/shard_map/forward/pallas_call | solution.py:233
  20.0 1.8 %collective-permute-start.4 = (bf16[16,3072]{1,0:T(8,128)(2,1)S(1)}, bf16[16,3072]{1,0:T(8,128)(2,1)S(1)}, u32[]{:S(2)}, u32[]{:S(2)}) collective-permute-start(bf16[16,3072]{1,0:T(8,128)(2,1)S(1)} %get-tuple-element.61), channel_id=1, source_target_pairs={{0,8},{8,0},{16,24},{24,16},{1,9},{9,1},{17,25},{25,17},{2,10},{10... | collective-permute-start | bytes 294920 | tf_op jit(solution)/shard_map/ppermute | solution.py:22
  21.8 1.5 %collective-permute-start.5 = (bf16[16,3072]{1,0:T(8,128)(2,1)S(1)}, bf16[16,3072]{1,0:T(8,128)(2,1)S(1)}, u32[]{:S(2)}, u32[]{:S(2)}) collective-permute-start(bf16[16,3072]{1,0:T(8,128)(2,1)S(1)} %get-tuple-element.62), channel_id=1, source_target_pairs={{0,16},{8,24},{16,0},{24,8},{1,17},{9,25},{17,1},{25,9},{2,18},{10... | collective-permute-start | bytes 294920 | tf_op jit(solution)/shard_map/ppermute | solution.py:22
  23.5 4.1 %forward.4 = (f32[16,3072]{1,0:T(8,128)S(1)}, bf16[16,3072]{1,0:T(8,128)(2,1)S(1)}, bf16[16,3072]{1,0:T(8,128)(2,1)S(1)}, bf16[16,3072]{1,0:T(8,128)(2,1)S(1)}, bf16[2048,1536]{1,0:T(8,128)(2,1)S(1)}) custom-call(bf16[64,2048]{1,0:T(8,128)(2,1)S(1)} %get-tuple-element.56.tokens_ref, bf16[64,2048]{1,0:T(8,128)(2,1)S(1)} %get-tuple-element.55.grads_ref, ...), custom_call_target="tpu_custom_call" | custom-call | tf_op jit(solution)/shard_map/forward/pallas_call | solution.py:233
  27.7 1.1 %collective-permute-done.6.refs_2_ = bf16[16,3072]{1,0:T(8,128)(2,1)S(1)} collective-permute-done((bf16[16,3072]{1,0:T(8,128)(2,1)S(1)}, bf16[16,3072]{1,0:T(8,128)(2,1)S(1)}, u32[]{:S(2)}, u32[]{:S(2)}) %collective-permute-start.6) | collective-permute-done | bytes 98336 | tf_op jit(solution)/shard_map/ppermute | solution.py:22
  29.9 1.2 %collective-permute-start.8 = (bf16[16,6144]{1,0:T(8,128)(2,1)S(1)}, bf16[16,6144]{1,0:T(8,128)(2,1)S(1)}, u32[]{:S(2)}, u32[]{:S(2)}) collective-permute-start(bf16[16,6144]{1,0:T(8,128)(2,1)S(1)} %get-tuple-element.71), channel_id=1, source_target_pairs={{0,16},{8,24},{16,0},{24,8},{1,17},{9,25},{17,1},{25,9},{2,18},{10... | collective-permute-start | bytes 589832 | tf_op jit(solution)/shard_map/ppermute | solution.py:22
  31.1 1.4 %collective-permute-start.9 = (bf16[16,6144]{1,0:T(8,128)(2,1)S(1)}, bf16[16,6144]{1,0:T(8,128)(2,1)S(1)}, u32[]{:S(2)}, u32[]{:S(2)}) collective-permute-start(bf16[16,6144]{1,0:T(8,128)(2,1)S(1)} %get-tuple-element.72), channel_id=1, source_target_pairs={{0,24},{8,16},{16,8},{24,0},{1,25},{9,17},{17,9},{25,1},{2,26},{10... | collective-permute-start | bytes 589832 | tf_op jit(solution)/shard_map/ppermute | solution.py:22
  32.5 5.3 %forward.5 = (f32[16,4608]{1,0:T(8,128)S(1)}, bf16[16,4608]{1,0:T(8,128)(2,1)S(1)}, bf16[16,4608]{1,0:T(8,128)(2,1)S(1)}, bf16[16,4608]{1,0:T(8,128)(2,1)S(1)}) custom-call(bf16[64,2048]{1,0:T(8,128)(2,1)S(1)} %get-tuple-element.56.tokens_ref, bf16[64,2048]{1,0:T(8,128)(2,1)S(1)} %get-tuple-element.55.grads_ref, ...), custom_call_target="tpu_custom_call" | custom-call | tf_op jit(solution)/shard_map/forward/pallas_call | solution.py:233
  37.8 2.2 %collective-permute-done.8.refs_1_.refs_2_ = bf16[16,6144]{1,0:T(8,128)(2,1)S(1)} collective-permute-done((bf16[16,6144]{1,0:T(8,128)(2,1)S(1)}, bf16[16,6144]{1,0:T(8,128)(2,1)S(1)}, u32[]{:S(2)}, u32[]{:S(2)}) %collective-permute-start.8) | collective-permute-done | bytes 196640 | tf_op jit(solution)/shard_map/ppermute | solution.py:22
  40.1 1.0 %collective-permute-start.10 = (bf16[16,7680]{1,0:T(8,128)(2,1)S(1)}, bf16[16,7680]{1,0:T(8,128)(2,1)S(1)}, u32[]{:S(2)}, u32[]{:S(2)}) collective-permute-start(bf16[16,7680]{1,0:T(8,128)(2,1)S(1)} %get-tuple-element.82), channel_id=1, source_target_pairs={{0,8},{8,0},{16,24},{24,16},{1,9},{9,1},{17,25},{25,17},{2,10},{10... | collective-permute-start | bytes 737288 | tf_op jit(solution)/shard_map/ppermute | solution.py:22
  41.1 1.2 %collective-permute-start.11 = (bf16[16,7680]{1,0:T(8,128)(2,1)S(1)}, bf16[16,7680]{1,0:T(8,128)(2,1)S(1)}, u32[]{:S(2)}, u32[]{:S(2)}) collective-permute-start(bf16[16,7680]{1,0:T(8,128)(2,1)S(1)} %get-tuple-element.83), channel_id=1, source_target_pairs={{0,16},{8,24},{16,0},{24,8},{1,17},{9,25},{17,1},{25,9},{2,18},{10... | collective-permute-start | bytes 737288 | tf_op jit(solution)/shard_map/ppermute | solution.py:22
  42.3 1.3 %collective-permute-start.12 = (bf16[16,7680]{1,0:T(8,128)(2,1)S(1)}, bf16[16,7680]{1,0:T(8,128)(2,1)S(1)}, u32[]{:S(2)}, u32[]{:S(2)}) collective-permute-start(bf16[16,7680]{1,0:T(8,128)(2,1)S(1)} %get-tuple-element.84), channel_id=1, source_target_pairs={{0,24},{8,16},{16,8},{24,0},{1,25},{9,17},{17,9},{25,1},{2,26},{10... | collective-permute-start | bytes 737288 | tf_op jit(solution)/shard_map/ppermute | solution.py:22
  43.6 6.7 %backward_one.1 = (bf16[2048,3584]{1,0:T(8,128)(2,1)}, bf16[2048,3584]{1,0:T(8,128)(2,1)}, bf16[3584,2048]{1,0:T(8,128)(2,1)}, f32[64,2048]{1,0:T(8,128)S(1)}) custom-call(bf16[2048,64]{1,0:T(8,128)(2,1)S(1)} %get-tuple-element.54.turned_ref, bf16[64,2048]{1,0:T(8,128)(2,1)S(1)} %get-tuple-element.55.grads_ref, ...), custom_call_target="tpu_custom_call" | custom-call | tf_op jit(solution)/shard_map/backward_one/pallas_call | solution.py:260
  50.3 4.1 %collective-permute-done.11.refs_1_.refs_2_ = bf16[16,7680]{1,0:T(8,128)(2,1)S(1)} collective-permute-done((bf16[16,7680]{1,0:T(8,128)(2,1)S(1)}, bf16[16,7680]{1,0:T(8,128)(2,1)S(1)}, u32[]{:S(2)}, u32[]{:S(2)}) %collective-permute-start.11) | collective-permute-done | bytes 245792 | tf_op jit(solution)/shard_map/ppermute | solution.py:22
  55.4 2.7 %collective-permute-start.13 = (bf16[16,4608]{1,0:T(8,128)(2,1)S(1)}, bf16[16,4608]{1,0:T(8,128)(2,1)S(1)}, u32[]{:S(2)}, u32[]{:S(2)}) collective-permute-start(bf16[16,4608]{1,0:T(8,128)(2,1)S(1)} %swiglu.5.refs_10_.refs_0_), channel_id=1, source_target_pairs={{0,8},{8,0},{16,24},{24,16},{1,9},{9,1},{17,25},{25,17},{2,10},{10... | collective-permute-start | bytes 442376 | tf_op jit(solution)/shard_map/ppermute | solution.py:22
  58.1 6.7 %backward_two.1 = (bf16[2048,3584]{1,0:T(8,128)(2,1)}, bf16[2048,3584]{1,0:T(8,128)(2,1)}, bf16[3584,2048]{1,0:T(8,128)(2,1)}, f32[64,2048]{1,0:T(8,128)S(1)}) custom-call(bf16[2048,64]{1,0:T(8,128)(2,1)S(1)} %get-tuple-element.54.turned_ref, ...), custom_call_target="tpu_custom_call", output_to_operand_aliasing={{0}: (9, {}), {1}: (10, {}), {2}: (11, {})} | custom-call | tf_op jit(solution)/shard_map/backward_two/pallas_call | solution.py:260
  64.9 3.9 %input_grad.1 = f32[64,2048]{1,0:T(8,128)S(1)} custom-call(s32[1]{0:T(128)} %bitcast.me_ref.refs_4_.refs_3_.after_ref.refs_7_, bf16[16,4608]{1,0:T(8,128)(2,1)S(1)} %swiglu.5.refs_10_.refs_0_, bf16[16,4608]{1,0:T(8,128)(2,1)S(1)} %collective-permute-done.13.refs_1_, bf16[16,4608]{1,0:T(8,128)(2,1)S(1)} %collective-permute-done.14.refs_2_, ...), custom_call_target="tpu_custom_call" | custom-call | tf_op jit(solution)/shard_map/input_grad/pallas_call | solution.py:294
  68.8 3.7 %weight_grads_early.1 = (bf16[2048,3584]{1,0:T(8,128)(2,1)}, bf16[2048,3584]{1,0:T(8,128)(2,1)}, bf16[3584,2048]{1,0:T(8,128)(2,1)}) custom-call(bf16[2048,64]{1,0:T(8,128)(2,1)S(1)} %get-tuple-element.54.turned_ref, bf16[64,2048]{1,0:T(8,128)(2,1)S(1)} %get-tuple-element.55.grads_ref, ...), custom_call_target="tpu_custom_call", output_to_operand_aliasing={{0}: (6, {}), {1}: (7, {}), {2}: (8, {})} | custom-call | tf_op jit(solution)/shard_map/weight_grads_early/pallas_call | solution.py:260
  72.6 1.3 %collective-permute-start.17 = (f32[8,2048]{1,0:T(8,128)S(1)}, f32[8,2048]{1,0:T(8,128)S(1)}, u32[]{:S(2)}, u32[]{:S(2)}) collective-permute-start(f32[8,2048]{1,0:T(8,128)S(1)} %get-tuple-element.102), channel_id=1, source_target_pairs={{0,2},{1,3},{2,0},{3,1},{4,6},{5,7},{6,4},{7,5},{8,10},{9,11},{10,... | collective-permute-start | bytes 196616 | tf_op jit(solution)/shard_map/ppermute | solution.py:22
  73.9 2.4 %collective-permute-start.19 = (f32[8,2048]{1,0:T(8,128)S(1)}, f32[8,2048]{1,0:T(8,128)S(1)}, u32[]{:S(2)}, u32[]{:S(2)}) collective-permute-start(f32[8,2048]{1,0:T(8,128)S(1)} %get-tuple-element.103), channel_id=1, source_target_pairs={{0,6},{1,7},{2,4},{3,5},{4,2},{5,3},{6,0},{7,1},{8,14},{9,15},{10,... | collective-permute-start | bytes 196616 | tf_op jit(solution)/shard_map/ppermute | solution.py:22
  76.8 5.7 %weight_grads.1 = (bf16[2048,3584]{1,0:T(8,128)(2,1)}, bf16[2048,3584]{1,0:T(8,128)(2,1)}, bf16[3584,2048]{1,0:T(8,128)(2,1)}) custom-call(bf16[2048,64]{1,0:T(8,128)(2,1)S(1)} %get-tuple-element.54.turned_ref, bf16[64,2048]{1,0:T(8,128)(2,1)S(1)} %get-tuple-element.55.grads_ref, ...), custom_call_target="tpu_custom_call", output_to_operand_aliasing={{0}: (6, {}), {1}: (7, {}), {2}: (8, {})} | custom-call | tf_op jit(solution)/shard_map/weight_grads/pallas_call | solution.py:260
  (36 shorter events, 7.1 us)
Async XLA Ops:
  2.2 11.7 %collective-permute-start.2 = (bf16[16,2048]{1,0:T(8,128)(2,1)S(1)}, bf16[16,2048]{1,0:T(8,128)(2,1)S(1)}, u32[]{:S(2)}, u32[]{:S(2)}) collective-permute-start(bf16[16,2048]{1,0:T(8,128)(2,1)S(1)} %constant_dynamic-update-slice_fusion.refs_0_), channel_id=1, source_target_pairs={{0,6},{1,7},{2,4},{3,5},{4,2},{5,3},{6,0},{7,1},{8,14},{9,15},{10,... | collective-permute-start | bytes 196616 | tf_op jit(solution)/shard_map/ppermute | solution.py:22
  7.2 6.7 %collective-permute-start.1 = (bf16[16,2048]{1,0:T(8,128)(2,1)S(1)}, bf16[16,2048]{1,0:T(8,128)(2,1)S(1)}, u32[]{:S(2)}, u32[]{:S(2)}) collective-permute-start(bf16[16,2048]{1,0:T(8,128)(2,1)S(1)} %constant_dynamic-update-slice_fusion.refs_0_), channel_id=1, source_target_pairs={{0,4},{1,5},{2,6},{3,7},{4,0},{5,1},{6,2},{7,3},{8,12},{9,13},{10,... | collective-permute-start | bytes 196616 | tf_op jit(solution)/shard_map/ppermute | solution.py:22
  7.2 6.7 %collective-permute-start = (bf16[16,2048]{1,0:T(8,128)(2,1)S(1)}, bf16[16,2048]{1,0:T(8,128)(2,1)S(1)}, u32[]{:S(2)}, u32[]{:S(2)}) collective-permute-start(bf16[16,2048]{1,0:T(8,128)(2,1)S(1)} %constant_dynamic-update-slice_fusion.refs_0_), channel_id=1, source_target_pairs={{0,2},{1,3},{2,0},{3,1},{4,6},{5,7},{6,4},{7,5},{8,10},{9,11},{10,... | collective-permute-start | bytes 196616 | tf_op jit(solution)/shard_map/ppermute | solution.py:22
  13.9 1.6 %collective-permute-start.3 = (bf16[64,2048]{1,0:T(8,128)(2,1)S(1)}, bf16[64,2048]{1,0:T(8,128)(2,1)S(1)}, u32[]{:S(2)}, u32[]{:S(2)}) collective-permute-start(bf16[64,2048]{1,0:T(8,128)(2,1)S(1)} %join.1.mine_ref), channel_id=1, source_target_pairs={{0,1},{1,0},{2,3},{3,2},{4,5},{5,4},{6,7},{7,6},{8,9},{9,8},{10,11... | collective-permute-start | bytes 786440 | tf_op jit(solution)/shard_map/ppermute | solution.py:22
  20.0 7.6 %collective-permute-start.4 = (bf16[16,3072]{1,0:T(8,128)(2,1)S(1)}, bf16[16,3072]{1,0:T(8,128)(2,1)S(1)}, u32[]{:S(2)}, u32[]{:S(2)}) collective-permute-start(bf16[16,3072]{1,0:T(8,128)(2,1)S(1)} %get-tuple-element.61), channel_id=1, source_target_pairs={{0,8},{8,0},{16,24},{24,16},{1,9},{9,1},{17,25},{25,17},{2,10},{10... | collective-permute-start | bytes 294920 | tf_op jit(solution)/shard_map/ppermute | solution.py:22
  21.8 5.9 %collective-permute-start.5 = (bf16[16,3072]{1,0:T(8,128)(2,1)S(1)}, bf16[16,3072]{1,0:T(8,128)(2,1)S(1)}, u32[]{:S(2)}, u32[]{:S(2)}) collective-permute-start(bf16[16,3072]{1,0:T(8,128)(2,1)S(1)} %get-tuple-element.62), channel_id=1, source_target_pairs={{0,16},{8,24},{16,0},{24,8},{1,17},{9,25},{17,1},{25,9},{2,18},{10... | collective-permute-start | bytes 294920 | tf_op jit(solution)/shard_map/ppermute | solution.py:22
  23.3 5.5 %collective-permute-start.6 = (bf16[16,3072]{1,0:T(8,128)(2,1)S(1)}, bf16[16,3072]{1,0:T(8,128)(2,1)S(1)}, u32[]{:S(2)}, u32[]{:S(2)}) collective-permute-start(bf16[16,3072]{1,0:T(8,128)(2,1)S(1)} %get-tuple-element.63), channel_id=1, source_target_pairs={{0,24},{8,16},{16,8},{24,0},{1,25},{9,17},{17,9},{25,1},{2,26},{10... | collective-permute-start | bytes 294920 | tf_op jit(solution)/shard_map/ppermute | solution.py:22
  28.9 8.8 %collective-permute-start.7 = (bf16[16,6144]{1,0:T(8,128)(2,1)S(1)}, bf16[16,6144]{1,0:T(8,128)(2,1)S(1)}, u32[]{:S(2)}, u32[]{:S(2)}) collective-permute-start(bf16[16,6144]{1,0:T(8,128)(2,1)S(1)} %get-tuple-element.70), channel_id=1, source_target_pairs={{0,8},{8,0},{16,24},{24,16},{1,9},{9,1},{17,25},{25,17},{2,10},{10... | collective-permute-start | bytes 589832 | tf_op jit(solution)/shard_map/ppermute | solution.py:22
  29.9 10.1 %collective-permute-start.8 = (bf16[16,6144]{1,0:T(8,128)(2,1)S(1)}, bf16[16,6144]{1,0:T(8,128)(2,1)S(1)}, u32[]{:S(2)}, u32[]{:S(2)}) collective-permute-start(bf16[16,6144]{1,0:T(8,128)(2,1)S(1)} %get-tuple-element.71), channel_id=1, source_target_pairs={{0,16},{8,24},{16,0},{24,8},{1,17},{9,25},{17,1},{25,9},{2,18},{10... | collective-permute-start | bytes 589832 | tf_op jit(solution)/shard_map/ppermute | solution.py:22
  31.1 8.8 %collective-permute-start.9 = (bf16[16,6144]{1,0:T(8,128)(2,1)S(1)}, bf16[16,6144]{1,0:T(8,128)(2,1)S(1)}, u32[]{:S(2)}, u32[]{:S(2)}) collective-permute-start(bf16[16,6144]{1,0:T(8,128)(2,1)S(1)} %get-tuple-element.72), channel_id=1, source_target_pairs={{0,24},{8,16},{16,8},{24,0},{1,25},{9,17},{17,9},{25,1},{2,26},{10... | collective-permute-start | bytes 589832 | tf_op jit(solution)/shard_map/ppermute | solution.py:22
  40.1 10.2 %collective-permute-start.10 = (bf16[16,7680]{1,0:T(8,128)(2,1)S(1)}, bf16[16,7680]{1,0:T(8,128)(2,1)S(1)}, u32[]{:S(2)}, u32[]{:S(2)}) collective-permute-start(bf16[16,7680]{1,0:T(8,128)(2,1)S(1)} %get-tuple-element.82), channel_id=1, source_target_pairs={{0,8},{8,0},{16,24},{24,16},{1,9},{9,1},{17,25},{25,17},{2,10},{10... | collective-permute-start | bytes 737288 | tf_op jit(solution)/shard_map/ppermute | solution.py:22
  41.1 13.3 %collective-permute-start.11 = (bf16[16,7680]{1,0:T(8,128)(2,1)S(1)}, bf16[16,7680]{1,0:T(8,128)(2,1)S(1)}, u32[]{:S(2)}, u32[]{:S(2)}) collective-permute-start(bf16[16,7680]{1,0:T(8,128)(2,1)S(1)} %get-tuple-element.83), channel_id=1, source_target_pairs={{0,16},{8,24},{16,0},{24,8},{1,17},{9,25},{17,1},{25,9},{2,18},{10... | collective-permute-start | bytes 737288 | tf_op jit(solution)/shard_map/ppermute | solution.py:22
  42.3 12.1 %collective-permute-start.12 = (bf16[16,7680]{1,0:T(8,128)(2,1)S(1)}, bf16[16,7680]{1,0:T(8,128)(2,1)S(1)}, u32[]{:S(2)}, u32[]{:S(2)}) collective-permute-start(bf16[16,7680]{1,0:T(8,128)(2,1)S(1)} %get-tuple-element.84), channel_id=1, source_target_pairs={{0,24},{8,16},{16,8},{24,0},{1,25},{9,17},{17,9},{25,1},{2,26},{10... | collective-permute-start | bytes 737288 | tf_op jit(solution)/shard_map/ppermute | solution.py:22
  54.5 10.3 %collective-permute-start.15 = (bf16[16,4608]{1,0:T(8,128)(2,1)S(1)}, bf16[16,4608]{1,0:T(8,128)(2,1)S(1)}, u32[]{:S(2)}, u32[]{:S(2)}) collective-permute-start(bf16[16,4608]{1,0:T(8,128)(2,1)S(1)} %swiglu.5.refs_10_.refs_0_), channel_id=1, source_target_pairs={{0,24},{8,16},{16,8},{24,0},{1,25},{9,17},{17,9},{25,1},{2,26},{10... | collective-permute-start | bytes 442376 | tf_op jit(solution)/shard_map/ppermute | solution.py:22
  54.6 10.2 %collective-permute-start.14 = (bf16[16,4608]{1,0:T(8,128)(2,1)S(1)}, bf16[16,4608]{1,0:T(8,128)(2,1)S(1)}, u32[]{:S(2)}, u32[]{:S(2)}) collective-permute-start(bf16[16,4608]{1,0:T(8,128)(2,1)S(1)} %swiglu.5.refs_10_.refs_0_), channel_id=1, source_target_pairs={{0,16},{8,24},{16,0},{24,8},{1,17},{9,25},{17,1},{25,9},{2,18},{10... | collective-permute-start | bytes 442376 | tf_op jit(solution)/shard_map/ppermute | solution.py:22
  55.4 9.5 %collective-permute-start.13 = (bf16[16,4608]{1,0:T(8,128)(2,1)S(1)}, bf16[16,4608]{1,0:T(8,128)(2,1)S(1)}, u32[]{:S(2)}, u32[]{:S(2)}) collective-permute-start(bf16[16,4608]{1,0:T(8,128)(2,1)S(1)} %swiglu.5.refs_10_.refs_0_), channel_id=1, source_target_pairs={{0,8},{8,0},{16,24},{24,16},{1,9},{9,1},{17,25},{25,17},{2,10},{10... | collective-permute-start | bytes 442376 | tf_op jit(solution)/shard_map/ppermute | solution.py:22
  68.8 3.7 %collective-permute-start.16 = (f32[4,8,2048]{2,1,0:T(8,128)S(1)}, f32[4,8,2048]{2,1,0:T(8,128)S(1)}, u32[]{:S(2)}, u32[]{:S(2)}) collective-permute-start(f32[4,8,2048]{2,1,0:T(8,128)S(1)} %slice_bitcast_fusion), channel_id=1, source_target_pairs={{0,1},{1,0},{2,3},{3,2},{4,5},{5,4},{6,7},{7,6},{8,9},{9,8},{10,11... | collective-permute-start | bytes 786440 | tf_op jit(solution)/shard_map/ppermute | solution.py:22
  72.6 9.9 %collective-permute-start.17 = (f32[8,2048]{1,0:T(8,128)S(1)}, f32[8,2048]{1,0:T(8,128)S(1)}, u32[]{:S(2)}, u32[]{:S(2)}) collective-permute-start(f32[8,2048]{1,0:T(8,128)S(1)} %get-tuple-element.102), channel_id=1, source_target_pairs={{0,2},{1,3},{2,0},{3,1},{4,6},{5,7},{6,4},{7,5},{8,10},{9,11},{10,... | collective-permute-start | bytes 196616 | tf_op jit(solution)/shard_map/ppermute | solution.py:22
  73.9 8.6 %collective-permute-start.19 = (f32[8,2048]{1,0:T(8,128)S(1)}, f32[8,2048]{1,0:T(8,128)S(1)}, u32[]{:S(2)}, u32[]{:S(2)}) collective-permute-start(f32[8,2048]{1,0:T(8,128)S(1)} %get-tuple-element.103), channel_id=1, source_target_pairs={{0,6},{1,7},{2,4},{3,5},{4,2},{5,3},{6,0},{7,1},{8,14},{9,15},{10,... | collective-permute-start | bytes 196616 | tf_op jit(solution)/shard_map/ppermute | solution.py:22
  76.3 7.2 %collective-permute-start.18 = (f32[8,2048]{1,0:T(8,128)S(1)}, f32[8,2048]{1,0:T(8,128)S(1)}, u32[]{:S(2)}, u32[]{:S(2)}) collective-permute-start(f32[8,2048]{1,0:T(8,128)S(1)} %get-tuple-element.104), channel_id=1, source_target_pairs={{0,4},{1,5},{2,6},{3,7},{4,0},{5,1},{6,2},{7,3},{8,12},{9,13},{10,... | collective-permute-start | bytes 196616 | tf_op jit(solution)/shard_map/ppermute | solution.py:22

commit v3 on v2

v3 whole, which is shorter than its diff:
```python
import functools

import jax
import jax.numpy as jnp
from jax import lax
from jax.experimental import pallas as pl
from jax.experimental.pallas import tpu as pltpu
from jax.sharding import PartitionSpec as P

BF16, F32 = jnp.bfloat16, jnp.float32
HBM = pl.BlockSpec(memory_space=pl.ANY)
VMEM = pl.BlockSpec(memory_space=pltpu.VMEM)
SMEM = pl.BlockSpec(memory_space=pltpu.SMEM)
CONTRACT_LAST = (((1,), (1,)), ((), ()))
CONTRACT_FIRST = (((0,), (0,)), ((), ()))
CUTS = (0, 4, 12, 20, 28)
SPLIT = (0, 1, 2)
PARAMS = pltpu.CompilerParams(vmem_limit_bytes=14 << 20)
vmem = pltpu.VMEM
shape = jax.ShapeDtypeStruct


def exchange(x, axis, size, offset):
    return lax.ppermute(x, axis, [(i, i ^ offset) for i in range(size)])


def tile_of(width, most=512):
    return next(t for t in (512, 256, 128) if t <= most and width % t == 0)


def tiles(width, tile):
    return [(at, min(tile, width - at)) for at in range(0, width, tile)]


def pair_kernel(first_hbm, second_hbm, out_ref, both, sems):
    copies = [pltpu.make_async_copy(x, both.at[i], sems.at[i]) for i, x in enumerate((first_hbm, second_hbm))]
    for copy in copies:
        copy.start()
    for copy in copies:
        copy.wait()
    out_ref[...] = jnp.concatenate([both[0], both[1]], axis=0)


def join_kernel(*refs):
    rows = refs[0].shape[0]
    for i, ref in enumerate(refs[:-2]):
        refs[-1][i * rows : (i + 1) * rows, :] = ref[...]


def order_kernel(rows, me_ref, mine_ref, other_ref, tokens_ref, grads_ref, turned_ref, scratch):
    me = me_ref[0]
    share = rows // 2
    n = mine_ref.shape[0] // rows
    total = tokens_ref.shape[0]
    per_row = total // scratch.shape[1]
    for half, out in ((0, tokens_ref), (1, grads_ref)):
        for k in range(n):
            for c, ref in ((0, mine_ref), (1, other_ref)):
                block = ref[k * rows : (k + 1) * rows, :].astype(F32)
                at = (2 * k + c) * share
                scratch[half, at // per_row, at % per_row : at % per_row + share, :] = block[
                    half * share : (half + 1) * share
                ]
        parts = [scratch[half, k ^ me] for k in range(scratch.shape[1])]
        rows_in_order = jnp.concatenate(parts, axis=0)
        out[...] = rows_in_order.astype(BF16)
        if half == 0:
            turned_ref[...] = rows_in_order.T.astype(BF16)


def weights_copies(sources, wanted, targets, sems):
    copies = []
    for i, ((which, start, width), target) in enumerate(zip(wanted, targets)):
        part = pl.ds(start, width)
        source = sources[which].at[part] if which == 2 else sources[which].at[:, part]
        copies.append(pltpu.make_async_copy(source, target, sems.at[i]))
    return copies


def fetch_kernel(wanted, me_ref, *refs):
    sources, targets, (done_ref, sems) = refs[:3], refs[3:-2], refs[-2:]
    copies = weights_copies(sources, wanted, targets, sems)
    for copy in copies:
        copy.start()
    done_ref[...] = jnp.zeros_like(done_ref)
    for copy in copies:
        copy.wait()


def forward_kernel(start, width, ready, wanted, own, sends, tile, me_ref, tokens_ref, grads_ref, gate_ref, up_ref, *refs):
    if ready:
        down_ref, refs = refs[0], refs[1:]
    sources, refs = refs[:3], refs[4:]
    keep_ref, send_refs, refs = refs[0], refs[1 : 1 + sends], refs[1 + sends :]
    targets, refs = refs[: len(wanted)], refs[len(wanted) :]
    if not ready:
        down_ref, refs = refs[0], refs[1:]
        wanted, targets = ((2, start, width), *wanted), (down_ref, *targets)
    copies = weights_copies(sources, wanted, targets, refs[0])
    for copy in copies:
        copy.start()

    def put(i, at, part):
        to = slice(i * width + at, i * width + at + tile)
        keep_ref[:, to] = part[:own]
        for s, ref in enumerate(send_refs):
            ref[:, to] = part[(s + 1) * own : (s + 2) * own].astype(BF16)

    def gate_and_up():
        for at in range(0, width, tile):
            put(0, at, jnp.dot(tokens_ref[...], gate_ref[:, at : at + tile], preferred_element_type=F32))
            put(1, at, jnp.dot(tokens_ref[...], up_ref[:, at : at + tile], preferred_element_type=F32))

    def back():
        for at in range(0, width, tile):
            down = down_ref[at : at + tile, :]
            put(2, at, lax.dot_general(grads_ref[...], down, CONTRACT_LAST, preferred_element_type=F32))

    if ready:

        @pl.when(me_ref[0] >= 0)
        def _():
            gate_and_up()
            back()

        for copy in copies:
            copy.wait()
    else:
        pl.when(me_ref[0] >= 0)(gate_and_up)
        copies[0].wait()
        pl.when(me_ref[0] >= 0)(back)
        for copy in copies[1:]:
            copy.wait()


def swiglu_kernel(width, n, after_ref, keep_ref, *refs):
    pieces, refs = refs[: n - 1], refs[n - 1 :]
    later, out_ref, send_refs = refs[: len(refs) // 2], refs[len(refs) // 2], refs[len(refs) // 2 + 1 :]
    sums = keep_ref[...]
    for ref in pieces:
        sums = sums + ref[:, : 3 * width].astype(F32)
    gate, upward, back = (sums[:, i * width : (i + 1) * width] for i in range(3))
    sigma = 1.0 / (1.0 + jnp.exp(-gate))
    parts = (back * upward * sigma * (1.0 + gate * (1.0 - sigma)), back * gate * sigma, gate * sigma * upward)
    for i, part in enumerate(parts):
        out_ref[:, i * width : (i + 1) * width] = part.astype(BF16)
    for before, after in zip(later, send_refs):
        split = before.shape[1]
        after[:, :split] = before[...]
        after[:, split:] = out_ref[...]


def input_kernel(width, n, me_ref, *refs):
    pieces, (gate_ref, up_ref, sum_ref, out_ref) = refs[:n], refs[n:]
    grads = jnp.concatenate([ref[:, : 2 * width] for ref in pieces], axis=0)
    turned = (grads[:, :width].T, grads[:, width:].T)
    own = pieces[0].shape[0]
    for at, size in tiles(gate_ref.shape[0], 512):
        rows = slice(at, at + size)
        part = jnp.dot(gate_ref[rows, :], turned[0], preferred_element_type=F32)
        part += jnp.dot(up_ref[rows, :], turned[1], preferred_element_type=F32)
        part = (part + sum_ref[rows, :]).T
        for k in range(n):
            out_ref[pl.ds(pl.multiple_of((k ^ me_ref[0]) * own, 8), own), rows] = part[k * own : (k + 1) * own]


def backward_kernel(n, start, width, shift, begin, count, tile, n_in, adds, me_ref, turned_ref, grads_ref, *refs):
    mine_ref, pieces, refs = refs[0], refs[1:n], refs[n:]
    bufs, sems = refs[-4:-1], refs[-1]
    outs, sum_refs = refs[n_in : n_in + 3], refs[n_in + 3 : -4]

    def rows(j, at, size):
        cols = j * width + at
        parts = [mine_ref[:, cols : cols + size]] + [r[:, shift + cols : shift + cols + size] for r in pieces]
        return jnp.concatenate(parts, axis=0)

    def copies(t):
        to = pl.ds(start + begin + t * tile, tile)
        targets = (outs[0].at[:, to], outs[1].at[:, to], outs[2].at[to])
        return [pltpu.make_async_copy(b.at[t % 2], o, sems.at[t % 2, j]) for j, (b, o) in enumerate(zip(bufs, targets))]

    def products(t, which):
        at = begin + t * tile
        for j in which:
            if j == 2:
                part = lax.dot_general(rows(2, at, tile), grads_ref[...], CONTRACT_FIRST, preferred_element_type=F32)
            else:
                part = jnp.dot(turned_ref[...], rows(j, at, tile), preferred_element_type=F32)
            bufs[j][t % 2] = part.astype(BF16)
        into = copies(t)
        for j in which:
            into[j].start()

    for t in range(count):

        @pl.when(me_ref[0] >= 0)
        def _():
            if t >= 2:
                for copy in copies(t - 2):
                    copy.wait()
            products(t, SPLIT if t == 0 else (0, 1, 2))

        if t == 0:
            for j in range(len(SPLIT), 3):
                pl.when(me_ref[0] >= 0)(functools.partial(products, t, (j,)))

    for sum_ref in sum_refs:
        gate_ref, up_ref = refs[:2]
        cols = slice(begin, begin + count * tile)

        @pl.when(me_ref[0] >= 0)
        def _():
            part = jnp.dot(gate_ref[:, cols], rows(0, begin, count * tile).T, preferred_element_type=F32)
            part += jnp.dot(up_ref[:, cols], rows(1, begin, count * tile).T, preferred_element_type=F32)
            sum_ref[...] = part + refs[2][...] if adds else part

    for t in range(max(count - 2, 0), count):
        for copy in copies(t):
            copy.wait()


def per_device(n_row, n_col, activations, out_grad, w_gate, w_up, w_down):
    share, depth = activations.shape
    hidden = w_gate.shape[1]
    total = share * n_col
    own = total // n_row
    me = lax.axis_index("row").astype(jnp.int32).reshape(1)
    w_gate, w_up, w_down = (pltpu.with_memory_space_constraint(w, pltpu.HBM) for w in (w_gate, w_up, w_down))
    units = hidden // 128
    cuts = [-(-units * part // 28) * 128 for part in CUTS]
    chunks = [(a, b - a) for a, b in zip(cuts[:-1], cuts[1:])]
    one, two, three, four = chunks

    def held(wanted):
        return [vmem((width, depth) if which == 2 else (depth, width), BF16) for which, _, width in wanted]

    mine = pl.pallas_call(
        pair_kernel,
        out_shape=vmem((2 * share, depth), BF16),
        in_specs=[HBM] * 2,
        out_specs=VMEM,
        scratch_shapes=[vmem((2, share, depth), BF16), pltpu.SemaphoreType.DMA((2,))],
        compiler_params=PARAMS,
        name="pair",
    )(*(pltpu.with_memory_space_constraint(x, pltpu.HBM) for x in (activations, out_grad)))
    wanted = ((0, *one), (1, *one), (2, *one), (0, *two), (1, *two))
    gate_one, up_one, down_one, gate_two, up_two, fetched = pl.pallas_call(
        functools.partial(fetch_kernel, wanted),
        out_shape=held(wanted) + [shape((8, 128), F32)],
        in_specs=[SMEM] + [HBM] * 3,
        out_specs=[VMEM] * 6,
        scratch_shapes=[pltpu.SemaphoreType.DMA((5,))],
        compiler_params=PARAMS,
        name="fetch",
    )(me, w_gate, w_up, w_down)
    others = [exchange(mine, "col", n_col, 2 * k) for k in range(1, n_col // 2)]
    near = pl.pallas_call(
        join_kernel,
        out_shape=vmem((n_col * share, depth), BF16),
        in_specs=[VMEM] * (n_col // 2 + 1),
        out_specs=VMEM,
        compiler_params=PARAMS,
        name="join",
    )(mine, *others, fetched)
    far = exchange(near, "col", n_col, 1)
    tokens, grads, turned = pl.pallas_call(
        functools.partial(order_kernel, 2 * share),
        out_shape=[vmem((total, depth), BF16)] * 2 + [vmem((depth, total), BF16)],
        in_specs=[SMEM] + [VMEM] * 2,
        out_specs=[VMEM] * 3,
        scratch_shapes=[vmem((2, n_row, own, depth), F32)],
        compiler_params=PARAMS,
        name="order",
    )(me, near, far)

    def forward(start, width, gate, up, down, wanted, after):
        ready = down is not None
        keep, *rest = pl.pallas_call(
            functools.partial(forward_kernel, start, width, ready, wanted, own, n_row - 1, tile_of(width)),
            out_shape=[vmem((own, 3 * width), F32)] + [vmem((own, 3 * width), BF16)] * (n_row - 1) + held(wanted),
            in_specs=[SMEM] + [VMEM] * (5 if ready else 4) + [HBM] * 4,
            out_specs=[VMEM] * (n_row + len(wanted)),
            scratch_shapes=([] if ready else [vmem((width, depth), BF16)]) + [pltpu.SemaphoreType.DMA((3,))],
            compiler_params=PARAMS,
            name="forward",
        )(me, tokens, grads, gate, up, *([down] if ready else []), w_gate, w_up, w_down, after)
        return keep, rest[: n_row - 1], rest[n_row - 1 :]

    def to_others(blocks):
        return [exchange(x, "row", n_row, s + 1) for s, x in enumerate(blocks)]

    def swiglu(width, keep, got, later, after):
        mine, *sends = pl.pallas_call(
            functools.partial(swiglu_kernel, width, n_row),
            out_shape=[vmem((own, 3 * width), BF16)] + [vmem((own, x.shape[1] + 3 * width), BF16) for x in later],
            in_specs=[HBM] + [VMEM] * (n_row + len(later)),
            out_specs=[VMEM] * (1 + len(later)),
            compiler_params=PARAMS,
            name="swiglu",
        )(after, keep, *got, *later)
        return mine, sends

    def backward(start, width, shift, begin, count, tile, pieces, weights, outs, after, name):
        known = 3 + n_row + len(weights)
        return pl.pallas_call(
            functools.partial(
                backward_kernel, n_row, start, width, shift, begin, count // tile, tile,
                len(weights) + len(outs) + 1, len(weights) > 2,
            ),
            out_shape=[shape((depth, hidden), BF16)] * 2
            + [shape((hidden, depth), BF16)]
            + ([vmem((depth, total), F32)] if weights else []),
            in_specs=[SMEM] + [VMEM] * (known - 1) + [HBM] * (len(outs) + 1),
            out_specs=[HBM] * 3 + ([VMEM] if weights else []),
            input_output_aliases={known + k: k for k in range(len(outs))},
            scratch_shapes=[vmem((2, depth, tile), BF16)] * 2
            + [vmem((2, tile, depth), BF16), pltpu.SemaphoreType.DMA((2, 3))],
            compiler_params=PARAMS,
            name=name,
        )(me, turned, grads, *pieces, *weights, *outs, after)

    keep_one, sends, (down_two,) = forward(*one, gate_one, up_one, down_one, ((2, *two),), me)
    got_one = to_others(sends)
    keep_two, sends, (gate_three, up_three) = forward(*two, gate_two, up_two, down_two, ((0, *three), (1, *three)), me)
    mine_one, sends = swiglu(one[1], keep_one, got_one, sends, me)
    got_two = to_others(sends)
    keep_three, sends, (gate_four, up_four) = forward(*three, gate_three, up_three, None, ((0, *four), (1, *four)), mine_one)
    mine_two, sends = swiglu(two[1], keep_two, got_two, sends, me)
    got_three = to_others(sends)
    keep_four, sends, _ = forward(*four, gate_four, up_four, None, (), mine_two)
    *outs, grad_input = backward(
        *one, 3 * two[1], 0, one[1], tile_of(one[1], 256), [mine_one, *got_two], (gate_one, up_one), (), mine_two, "backward_one"
    )
    mine_three, sends = swiglu(three[1], keep_three, got_three, sends, grad_input)
    got_four = to_others(sends)
    *outs, grad_input = backward(
        *two, 3 * three[1], 0, two[1], tile_of(two[1]), [mine_two, *got_three], (gate_two, up_two, grad_input), outs, mine_three, "backward_two"
    )
    mine_four, _ = swiglu(four[1], keep_four, got_four, (), grad_input)
    got_last = to_others([mine_four] * (n_row - 1))
    *outs, grad_input = backward(
        *three, 3 * four[1], 0, three[1], tile_of(three[1]), [mine_three, *got_four], (gate_three, up_three, grad_input), outs, mine_four, "backward_three"
    )
    pieces = [mine_four, *got_last]
    grad_input = pl.pallas_call(
        functools.partial(input_kernel, four[1], n_row),
        out_shape=vmem((total, depth), F32),
        in_specs=[SMEM] + [VMEM] * (n_row + 3),
        out_specs=VMEM,
        compiler_params=PARAMS,
        name="input_grad",
    )(me, *pieces, gate_four, up_four, grad_input)
    blocks = grad_input.reshape(n_col // 2, 2, share, depth)
    summed = blocks[:, 0] + exchange(blocks[:, 1], "col", n_col, 1)
    outs = backward(*four, 0, 0, four[1], tile_of(four[1], 256), pieces, (), outs, summed, "weight_grads")
    result = summed[0]
    for k in range(1, n_col // 2):
        result = result + exchange(summed[k], "col", n_col, 2 * k)
    return (result.astype(BF16), *outs)


def solution(mesh):
    in_specs = (P("col", "row"), P("col", "row"), P("row", "col"), P("row", "col"), P("col", "row"))
    out_specs = (P("col", "row"), P("row", "col"), P("row", "col"), P("col", "row"))
    return jax.shard_map(
        functools.partial(per_device, mesh.shape["row"], mesh.shape["col"]),
        mesh=mesh,
        in_specs=in_specs,
        out_specs=out_specs,
        check_vma=False,
    )
```

time: 84.4 us -> 79.9 us (0.947)
  waiting for transfers between devices: 9.91 us -> 5.46 us
  starting transfers between devices: 24.2 us -> 27.9 us
  Pallas kernels: 46.9 us -> 44.6 us
  local copies, waits for them, and re-layouts: 1.55 us -> 0.03 us
    ppermute x20 -> x23, waiting for transfers between devices: 9.91 us -> 5.46 us  [exchange(): return lax.ppermute(x, axis, [(i, i ^ offset) for i in range(size)])]
    ppermute x20 -> x23, starting transfers between devices: 24.2 us -> 27.9 us  [exchange(): return lax.ppermute(x, axis, [(i, i ^ offset) for i in range(size)])]
    pallas_call x4, Pallas kernels: 22.8 us -> 21.3 us  [backward(): pl.pallas_call(functools.partial(backward_kernel, n_row, start, width, sh...]
    pallas_call x1 -> x2, Pallas kernels: 3.88 us -> 3.2 us  [the longest x1 2.4 us: per_device(): pl.pallas_call(functools.partial(input_kernel, four[1], n_row), out_shape...]
    pallas_call x3 -> x4, Pallas kernels: 13.5 us -> 14 us  [forward(): pl.pallas_call(functools.partial(forward_kernel, start, width, ready, wan...]
  transfers between devices with their start and end apart: 20 -> 23, of which waited for: 5 -> 5; matrix products, arithmetic and copies ran while one was open for 0% -> 0% of each run, Pallas kernels for 45% -> 48%
where the time goes in v3:
time: 79.9 us; the launch traced here: 79.6 us
  Pallas kernels  44.6 us (56%)
  starting transfers between devices  27.9 us (35%)
  waiting for transfers between devices  5.46 us (7%)
  between operations  0.93 us (1%)
    ppermute x23, starting transfers between devices, exchange(): return lax.ppermute(x, axis, [(i, i ^ offset) for i in range(size)])  27.9 us
    pallas_call x4, Pallas kernels, backward(): pl.pallas_call(functools.partial(backward_kernel, n_row, start, width, sh...  21.3 us
    pallas_call x4, Pallas kernels, forward(): pl.pallas_call(functools.partial(forward_kernel, start, width, ready, wan...  14 us
    ppermute x23, waiting for transfers between devices, exchange(): return lax.ppermute(x, axis, [(i, i ^ offset) for i in range(size)])  5.46 us
    pallas_call x1, Pallas kernels, per_device(): pl.pallas_call(functools.partial(fetch_kernel, wanted), out_shape=held(wa...  5.35 us
    pallas_call x1, Pallas kernels, per_device(): pl.pallas_call(functools.partial(input_kernel, four[1], n_row), out_shape...  2.4 us
  transfers between devices with their start and end apart: 23, of which 5 were waited for; matrix products, arithmetic and copies ran while one was open for 0% of the time, Pallas kernels for 48%

profile of v3, /device:TPU:0, one launch (start us, length us, event | category | flops | bytes accessed | tf_op | source)
XLA Modules:
  0.0 79.6 jit_solution(4646516626511641771)
XLA Ops:
  1.4 5.1 %collective-permute-start.2 = (bf16[16,2048]{1,0:T(8,128)(2,1)S(1)}, bf16[16,2048]{1,0:T(8,128)(2,1)S(1)}, u32[]{:S(2)}, u32[]{:S(2)}) collective-permute-start(bf16[16,2048]{1,0:T(8,128)(2,1)S(1)} %pair.1.refs_0_), channel_id=1, source_target_pairs={{0,6},{1,7},{2,4},{3,5},{4,2},{5,3},{6,0},{7,1},{8,14},{9,15},{10,... | collective-permute-start | bytes 196616 | tf_op jit(solution)/shard_map/ppermute | solution.py:24
  7.2 5.3 %fetch.1 = (bf16[2048,512]{1,0:T(8,128)(2,1)S(1)}, bf16[2048,512]{1,0:T(8,128)(2,1)S(1)}, bf16[512,2048]{1,0:T(8,128)(2,1)S(1)}, bf16[2048,1024]{1,0:T(8,128)(2,...) custom-call(s32[1]{0:T(128)} %bitcast.me_ref.refs_4_.after_ref, bf16[2048,3584]{1,0:T(8,128)(2,1)} %refs_0_.5, ...), custom_call_target="tpu_custom_call" | custom-call | tf_op jit(solution)/shard_map/fetch/pallas_call | solution.py:247
  12.7 1.5 %collective-permute-done.3.other_ref = bf16[64,2048]{1,0:T(8,128)(2,1)S(1)} collective-permute-done((bf16[64,2048]{1,0:T(8,128)(2,1)S(1)}, bf16[64,2048]{1,0:T(8,128)(2,1)S(1)}, u32[]{:S(2)}, u32[]{:S(2)}) %collective-permute-start.3) | collective-permute-done | bytes 262176 | tf_op jit(solution)/shard_map/ppermute | solution.py:24
  14.5 2.2 %forward.4 = (f32[16,1536]{1,0:T(8,128)S(1)}, bf16[16,1536]{1,0:T(8,128)(2,1)S(1)}, bf16[16,1536]{1,0:T(8,128)(2,1)S(1)}, bf16[16,1536]{1,0:T(8,128)(2,1)S(1)}, bf16[1024,2048]{1,0:T(8,128)(2,1)S(1)}) custom-call(s32[1]{0:T(128)} %bitcast.me_ref.refs_4_.after_ref, bf16[64,2048]{1,0:T(8,128)(2,1)S(1)} %get-tuple-element.64.tokens_ref, ...), custom_call_target="tpu_custom_call" | custom-call | tf_op jit(solution)/shard_map/forward/pallas_call | solution.py:278
  16.8 1.7 %collective-permute-start.4 = (bf16[16,1536]{1,0:T(8,128)(2,1)S(1)}, bf16[16,1536]{1,0:T(8,128)(2,1)S(1)}, u32[]{:S(2)}, u32[]{:S(2)}) collective-permute-start(bf16[16,1536]{1,0:T(8,128)(2,1)S(1)} %get-tuple-element.73), channel_id=1, source_target_pairs={{0,8},{8,0},{16,24},{24,16},{1,9},{9,1},{17,25},{25,17},{2,10},{10... | collective-permute-start | bytes 147464 | tf_op jit(solution)/shard_map/ppermute | solution.py:24
  18.5 1.5 %collective-permute-start.5 = (bf16[16,1536]{1,0:T(8,128)(2,1)S(1)}, bf16[16,1536]{1,0:T(8,128)(2,1)S(1)}, u32[]{:S(2)}, u32[]{:S(2)}) collective-permute-start(bf16[16,1536]{1,0:T(8,128)(2,1)S(1)} %get-tuple-element.74), channel_id=1, source_target_pairs={{0,16},{8,24},{16,0},{24,8},{1,17},{9,25},{17,1},{25,9},{2,18},{10... | collective-permute-start | bytes 147464 | tf_op jit(solution)/shard_map/ppermute | solution.py:24
  20.3 3.5 %forward.5 = (f32[16,3072]{1,0:T(8,128)S(1)}, bf16[16,3072]{1,0:T(8,128)(2,1)S(1)}, bf16[16,3072]{1,0:T(8,128)(2,1)S(1)}, bf16[16,3072]{1,0:T(8,128)(2,1)S(1)}, ...) custom-call(s32[1]{0:T(128)} %bitcast.me_ref.refs_4_.after_ref, ...), custom_call_target="tpu_custom_call" | custom-call | tf_op jit(solution)/shard_map/forward/pallas_call | solution.py:278
  25.6 1.5 %collective-permute-start.8 = (bf16[16,4608]{1,0:T(8,128)(2,1)S(1)}, bf16[16,4608]{1,0:T(8,128)(2,1)S(1)}, u32[]{:S(2)}, u32[]{:S(2)}) collective-permute-start(bf16[16,4608]{1,0:T(8,128)(2,1)S(1)} %get-tuple-element.80), channel_id=1, source_target_pairs={{0,16},{8,24},{16,0},{24,8},{1,17},{9,25},{17,1},{25,9},{2,18},{10... | collective-permute-start | bytes 442376 | tf_op jit(solution)/shard_map/ppermute | solution.py:24
  27.2 1.4 %collective-permute-start.9 = (bf16[16,4608]{1,0:T(8,128)(2,1)S(1)}, bf16[16,4608]{1,0:T(8,128)(2,1)S(1)}, u32[]{:S(2)}, u32[]{:S(2)}) collective-permute-start(bf16[16,4608]{1,0:T(8,128)(2,1)S(1)} %get-tuple-element.81), channel_id=1, source_target_pairs={{0,24},{8,16},{16,8},{24,0},{1,25},{9,17},{17,9},{25,1},{2,26},{10... | collective-permute-start | bytes 442376 | tf_op jit(solution)/shard_map/ppermute | solution.py:24
  28.6 4.7 %forward.6 = (f32[16,3072]{1,0:T(8,128)S(1)}, bf16[16,3072]{1,0:T(8,128)(2,1)S(1)}, bf16[16,3072]{1,0:T(8,128)(2,1)S(1)}, bf16[16,3072]{1,0:T(8,128)(2,1)S(1)}, ...) custom-call(s32[1]{0:T(128)} %bitcast.me_ref.refs_4_.after_ref, ...), custom_call_target="tpu_custom_call" | custom-call | tf_op jit(solution)/shard_map/forward/pallas_call | solution.py:278
  34.1 1.2 %collective-permute-start.10 = (bf16[16,6144]{1,0:T(8,128)(2,1)S(1)}, bf16[16,6144]{1,0:T(8,128)(2,1)S(1)}, u32[]{:S(2)}, u32[]{:S(2)}) collective-permute-start(bf16[16,6144]{1,0:T(8,128)(2,1)S(1)} %get-tuple-element.89), channel_id=1, source_target_pairs={{0,8},{8,0},{16,24},{24,16},{1,9},{9,1},{17,25},{25,17},{2,10},{10... | collective-permute-start | bytes 589832 | tf_op jit(solution)/shard_map/ppermute | solution.py:24
  35.8 1.8 %collective-permute-start.12 = (bf16[16,6144]{1,0:T(8,128)(2,1)S(1)}, bf16[16,6144]{1,0:T(8,128)(2,1)S(1)}, u32[]{:S(2)}, u32[]{:S(2)}) collective-permute-start(bf16[16,6144]{1,0:T(8,128)(2,1)S(1)} %get-tuple-element.91), channel_id=1, source_target_pairs={{0,24},{8,16},{16,8},{24,0},{1,25},{9,17},{17,9},{25,1},{2,26},{10... | collective-permute-start | bytes 589832 | tf_op jit(solution)/shard_map/ppermute | solution.py:24
  37.6 3.6 %forward.7 = (f32[16,3072]{1,0:T(8,128)S(1)}, bf16[16,3072]{1,0:T(8,128)(2,1)S(1)}, bf16[16,3072]{1,0:T(8,128)(2,1)S(1)}, bf16[16,3072]{1,0:T(8,128)(2,1)S(1)}) custom-call(s32[1]{0:T(128)} %bitcast.me_ref.refs_4_.after_ref, bf16[64,2048]{1,0:T(8,128)(2,1)S(1)} %get-tuple-element.64.tokens_ref, bf16[64,2048]{1,0:T(8,128)(2,1)S(1)} %get-tuple-element.63.grads_ref, ...), custom_call_target="tpu_custom_call" | custom-call | tf_op jit(solution)/shard_map/forward/pallas_call | solution.py:278
  41.2 3.4 %backward_one.1 = (bf16[2048,3584]{1,0:T(8,128)(2,1)}, bf16[2048,3584]{1,0:T(8,128)(2,1)}, bf16[3584,2048]{1,0:T(8,128)(2,1)}, f32[2048,64]{1,0:T(8,128)S(1)}) custom-call(s32[1]{0:T(128)} %bitcast.me_ref.refs_4_.after_ref, bf16[2048,64]{1,0:T(8,128)(2,1)S(1)} %get-tuple-element.62.turned_ref, bf16[64,2048]{1,0:T(8,128)(2,1)S(1)} %get-tuple-element.63.grads_ref, ...), custom_call_target="tpu_custom_call" | custom-call | tf_op jit(solution)/shard_map/backward_one/pallas_call | solution.py:305
  46.6 1.8 %collective-permute-start.15 = (bf16[16,6144]{1,0:T(8,128)(2,1)S(1)}, bf16[16,6144]{1,0:T(8,128)(2,1)S(1)}, u32[]{:S(2)}, u32[]{:S(2)}) collective-permute-start(bf16[16,6144]{1,0:T(8,128)(2,1)S(1)} %get-tuple-element.107), channel_id=1, source_target_pairs={{0,24},{8,16},{16,8},{24,0},{1,25},{9,17},{17,9},{25,1},{2,26},{10... | collective-permute-start | bytes 589832 | tf_op jit(solution)/shard_map/ppermute | solution.py:24
  48.4 6.0 %backward_two.1 = (bf16[2048,3584]{1,0:T(8,128)(2,1)}, bf16[2048,3584]{1,0:T(8,128)(2,1)}, bf16[3584,2048]{1,0:T(8,128)(2,1)}, f32[2048,64]{1,0:T(8,128)S(1)}) custom-call(s32[1]{0:T(128)} %bitcast.me_ref.refs_4_.after_ref, bf16[2048,64]{1,0:T(8,128)(2,1)S(1)} %get-tuple-element.62.turned_ref, ...), custom_call_target="tpu_custom_call", output_to_operand_aliasing={{0}: (10, {}), {1}: (11, {}), {2}: (12, {})} | custom-call | tf_op jit(solution)/shard_map/backward_two/pallas_call | solution.py:305
  54.5 1.2 %collective-permute-start.18 = (bf16[16,3072]{1,0:T(8,128)(2,1)S(1)}, bf16[16,3072]{1,0:T(8,128)(2,1)S(1)}, u32[]{:S(2)}, u32[]{:S(2)}) collective-permute-start(bf16[16,3072]{1,0:T(8,128)(2,1)S(1)} %swiglu.7.refs_10_.refs_0_), channel_id=1, source_target_pairs={{0,24},{8,16},{16,8},{24,0},{1,25},{9,17},{17,9},{25,1},{2,26},{10... | collective-permute-start | bytes 294920 | tf_op jit(solution)/shard_map/ppermute | solution.py:24
  55.7 1.4 %collective-permute-start.17 = (bf16[16,3072]{1,0:T(8,128)(2,1)S(1)}, bf16[16,3072]{1,0:T(8,128)(2,1)S(1)}, u32[]{:S(2)}, u32[]{:S(2)}) collective-permute-start(bf16[16,3072]{1,0:T(8,128)(2,1)S(1)} %swiglu.7.refs_10_.refs_0_), channel_id=1, source_target_pairs={{0,16},{8,24},{16,0},{24,8},{1,17},{9,25},{17,1},{25,9},{2,18},{10... | collective-permute-start | bytes 294920 | tf_op jit(solution)/shard_map/ppermute | solution.py:24
  58.1 6.2 %backward_three.1 = (bf16[2048,3584]{1,0:T(8,128)(2,1)}, bf16[2048,3584]{1,0:T(8,128)(2,1)}, bf16[3584,2048]{1,0:T(8,128)(2,1)}, f32[2048,64]{1,0:T(8,128)S(1)}) custom-call(s32[1]{0:T(128)} %bitcast.me_ref.refs_4_.after_ref, bf16[2048,64]{1,0:T(8,128)(2,1)S(1)} %get-tuple-element.62.turned_ref, ...), custom_call_target="tpu_custom_call", output_to_operand_aliasing={{0}: (10, {}), {1}: (11, {}), {2}: (12, {})} | custom-call | tf_op jit(solution)/shard_map/backward_three/pallas_call | solution.py:305
  64.3 2.4 %input_grad.1 = f32[64,2048]{1,0:T(8,128)S(1)} custom-call(s32[1]{0:T(128)} %bitcast.me_ref.refs_4_.after_ref, bf16[16,3072]{1,0:T(8,128)(2,1)S(1)} %swiglu.7.refs_10_.refs_0_, bf16[16,3072]{1,0:T(8,128)(2,1)S(1)} %collective-permute-done.16.refs_1_, bf16[16,3072]{1,0:T(8,128)(2,1)S(1)} %collective-permute-done.17.refs_2_, ...), custom_call_target="tpu_custom_call" | custom-call | tf_op jit(solution)/shard_map/input_grad/pallas_call | solution.py:345
  66.8 1.5 %collective-permute-done.19 = f32[4,8,2048]{2,1,0:T(8,128)S(1)} collective-permute-done((f32[4,8,2048]{2,1,0:T(8,128)S(1)}, f32[4,8,2048]{2,1,0:T(8,128)S(1)}, u32[]{:S(2)}, u32[]{:S(2)}) %collective-permute-start.19) | collective-permute-done | bytes 262176 | tf_op jit(solution)/shard_map/ppermute | solution.py:24
  68.4 1.3 %collective-permute-start.20 = (f32[8,2048]{1,0:T(8,128)S(1)}, f32[8,2048]{1,0:T(8,128)S(1)}, u32[]{:S(2)}, u32[]{:S(2)}) collective-permute-start(f32[8,2048]{1,0:T(8,128)S(1)} %get-tuple-element.118), channel_id=1, source_target_pairs={{0,2},{1,3},{2,0},{3,1},{4,6},{5,7},{6,4},{7,5},{8,10},{9,11},{10,... | collective-permute-start | bytes 196616 | tf_op jit(solution)/shard_map/ppermute | solution.py:24
  69.7 2.4 %collective-permute-start.22 = (f32[8,2048]{1,0:T(8,128)S(1)}, f32[8,2048]{1,0:T(8,128)S(1)}, u32[]{:S(2)}, u32[]{:S(2)}) collective-permute-start(f32[8,2048]{1,0:T(8,128)S(1)} %get-tuple-element.119), channel_id=1, source_target_pairs={{0,6},{1,7},{2,4},{3,5},{4,2},{5,3},{6,0},{7,1},{8,14},{9,15},{10,... | collective-permute-start | bytes 196616 | tf_op jit(solution)/shard_map/ppermute | solution.py:24
  72.6 5.7 %weight_grads.1 = (bf16[2048,3584]{1,0:T(8,128)(2,1)}, bf16[2048,3584]{1,0:T(8,128)(2,1)}, bf16[3584,2048]{1,0:T(8,128)(2,1)}) custom-call(s32[1]{0:T(128)} %bitcast.me_ref.refs_4_.after_ref, bf16[2048,64]{1,0:T(8,128)(2,1)S(1)} %get-tuple-element.62.turned_ref, ...), custom_call_target="tpu_custom_call", output_to_operand_aliasing={{0}: (7, {}), {1}: (8, {}), {2}: (9, {})} | custom-call | tf_op jit(solution)/shard_map/weight_grads/pallas_call | solution.py:305
  (43 shorter events, 10.1 us)
Async XLA Ops:
  1.4 11.1 %collective-permute-start.2 = (bf16[16,2048]{1,0:T(8,128)(2,1)S(1)}, bf16[16,2048]{1,0:T(8,128)(2,1)S(1)}, u32[]{:S(2)}, u32[]{:S(2)}) collective-permute-start(bf16[16,2048]{1,0:T(8,128)(2,1)S(1)} %pair.1.refs_0_), channel_id=1, source_target_pairs={{0,6},{1,7},{2,4},{3,5},{4,2},{5,3},{6,0},{7,1},{8,14},{9,15},{10,... | collective-permute-start | bytes 196616 | tf_op jit(solution)/shard_map/ppermute | solution.py:24
  6.6 6.0 %collective-permute-start.1 = (bf16[16,2048]{1,0:T(8,128)(2,1)S(1)}, bf16[16,2048]{1,0:T(8,128)(2,1)S(1)}, u32[]{:S(2)}, u32[]{:S(2)}) collective-permute-start(bf16[16,2048]{1,0:T(8,128)(2,1)S(1)} %pair.1.refs_0_), channel_id=1, source_target_pairs={{0,4},{1,5},{2,6},{3,7},{4,0},{5,1},{6,2},{7,3},{8,12},{9,13},{10,... | collective-permute-start | bytes 196616 | tf_op jit(solution)/shard_map/ppermute | solution.py:24
  6.6 6.0 %collective-permute-start = (bf16[16,2048]{1,0:T(8,128)(2,1)S(1)}, bf16[16,2048]{1,0:T(8,128)(2,1)S(1)}, u32[]{:S(2)}, u32[]{:S(2)}) collective-permute-start(bf16[16,2048]{1,0:T(8,128)(2,1)S(1)} %pair.1.refs_0_), channel_id=1, source_target_pairs={{0,2},{1,3},{2,0},{3,1},{4,6},{5,7},{6,4},{7,5},{8,10},{9,11},{10,... | collective-permute-start | bytes 196616 | tf_op jit(solution)/shard_map/ppermute | solution.py:24
  12.6 1.6 %collective-permute-start.3 = (bf16[64,2048]{1,0:T(8,128)(2,1)S(1)}, bf16[64,2048]{1,0:T(8,128)(2,1)S(1)}, u32[]{:S(2)}, u32[]{:S(2)}) collective-permute-start(bf16[64,2048]{1,0:T(8,128)(2,1)S(1)} %join.1.mine_ref), channel_id=1, source_target_pairs={{0,1},{1,0},{2,3},{3,2},{4,5},{5,4},{6,7},{7,6},{8,9},{9,8},{10,11... | collective-permute-start | bytes 786440 | tf_op jit(solution)/shard_map/ppermute | solution.py:24
  16.8 7.1 %collective-permute-start.4 = (bf16[16,1536]{1,0:T(8,128)(2,1)S(1)}, bf16[16,1536]{1,0:T(8,128)(2,1)S(1)}, u32[]{:S(2)}, u32[]{:S(2)}) collective-permute-start(bf16[16,1536]{1,0:T(8,128)(2,1)S(1)} %get-tuple-element.73), channel_id=1, source_target_pairs={{0,8},{8,0},{16,24},{24,16},{1,9},{9,1},{17,25},{25,17},{2,10},{10... | collective-permute-start | bytes 147464 | tf_op jit(solution)/shard_map/ppermute | solution.py:24
  18.5 5.4 %collective-permute-start.5 = (bf16[16,1536]{1,0:T(8,128)(2,1)S(1)}, bf16[16,1536]{1,0:T(8,128)(2,1)S(1)}, u32[]{:S(2)}, u32[]{:S(2)}) collective-permute-start(bf16[16,1536]{1,0:T(8,128)(2,1)S(1)} %get-tuple-element.74), channel_id=1, source_target_pairs={{0,16},{8,24},{16,0},{24,8},{1,17},{9,25},{17,1},{25,9},{2,18},{10... | collective-permute-start | bytes 147464 | tf_op jit(solution)/shard_map/ppermute | solution.py:24
  20.0 5.0 %collective-permute-start.6 = (bf16[16,1536]{1,0:T(8,128)(2,1)S(1)}, bf16[16,1536]{1,0:T(8,128)(2,1)S(1)}, u32[]{:S(2)}, u32[]{:S(2)}) collective-permute-start(bf16[16,1536]{1,0:T(8,128)(2,1)S(1)} %get-tuple-element.75), channel_id=1, source_target_pairs={{0,24},{8,16},{16,8},{24,0},{1,25},{9,17},{17,9},{25,1},{2,26},{10... | collective-permute-start | bytes 147464 | tf_op jit(solution)/shard_map/ppermute | solution.py:24
  25.0 8.3 %collective-permute-start.7 = (bf16[16,4608]{1,0:T(8,128)(2,1)S(1)}, bf16[16,4608]{1,0:T(8,128)(2,1)S(1)}, u32[]{:S(2)}, u32[]{:S(2)}) collective-permute-start(bf16[16,4608]{1,0:T(8,128)(2,1)S(1)} %get-tuple-element.79), channel_id=1, source_target_pairs={{0,8},{8,0},{16,24},{24,16},{1,9},{9,1},{17,25},{25,17},{2,10},{10... | collective-permute-start | bytes 442376 | tf_op jit(solution)/shard_map/ppermute | solution.py:24
  25.6 8.3 %collective-permute-start.8 = (bf16[16,4608]{1,0:T(8,128)(2,1)S(1)}, bf16[16,4608]{1,0:T(8,128)(2,1)S(1)}, u32[]{:S(2)}, u32[]{:S(2)}) collective-permute-start(bf16[16,4608]{1,0:T(8,128)(2,1)S(1)} %get-tuple-element.80), channel_id=1, source_target_pairs={{0,16},{8,24},{16,0},{24,8},{1,17},{9,25},{17,1},{25,9},{2,18},{10... | collective-permute-start | bytes 442376 | tf_op jit(solution)/shard_map/ppermute | solution.py:24
  27.2 6.8 %collective-permute-start.9 = (bf16[16,4608]{1,0:T(8,128)(2,1)S(1)}, bf16[16,4608]{1,0:T(8,128)(2,1)S(1)}, u32[]{:S(2)}, u32[]{:S(2)}) collective-permute-start(bf16[16,4608]{1,0:T(8,128)(2,1)S(1)} %get-tuple-element.81), channel_id=1, source_target_pairs={{0,24},{8,16},{16,8},{24,0},{1,25},{9,17},{17,9},{25,1},{2,26},{10... | collective-permute-start | bytes 442376 | tf_op jit(solution)/shard_map/ppermute | solution.py:24
  34.1 10.6 %collective-permute-start.10 = (bf16[16,6144]{1,0:T(8,128)(2,1)S(1)}, bf16[16,6144]{1,0:T(8,128)(2,1)S(1)}, u32[]{:S(2)}, u32[]{:S(2)}) collective-permute-start(bf16[16,6144]{1,0:T(8,128)(2,1)S(1)} %get-tuple-element.89), channel_id=1, source_target_pairs={{0,8},{8,0},{16,24},{24,16},{1,9},{9,1},{17,25},{25,17},{2,10},{10... | collective-permute-start | bytes 589832 | tf_op jit(solution)/shard_map/ppermute | solution.py:24
  35.2 9.4 %collective-permute-start.11 = (bf16[16,6144]{1,0:T(8,128)(2,1)S(1)}, bf16[16,6144]{1,0:T(8,128)(2,1)S(1)}, u32[]{:S(2)}, u32[]{:S(2)}) collective-permute-start(bf16[16,6144]{1,0:T(8,128)(2,1)S(1)} %get-tuple-element.90), channel_id=1, source_target_pairs={{0,16},{8,24},{16,0},{24,8},{1,17},{9,25},{17,1},{25,9},{2,18},{10... | collective-permute-start | bytes 589832 | tf_op jit(solution)/shard_map/ppermute | solution.py:24
  35.8 8.9 %collective-permute-start.12 = (bf16[16,6144]{1,0:T(8,128)(2,1)S(1)}, bf16[16,6144]{1,0:T(8,128)(2,1)S(1)}, u32[]{:S(2)}, u32[]{:S(2)}) collective-permute-start(bf16[16,6144]{1,0:T(8,128)(2,1)S(1)} %get-tuple-element.91), channel_id=1, source_target_pairs={{0,24},{8,16},{16,8},{24,0},{1,25},{9,17},{17,9},{25,1},{2,26},{10... | collective-permute-start | bytes 589832 | tf_op jit(solution)/shard_map/ppermute | solution.py:24
  44.8 9.6 %collective-permute-start.13 = (bf16[16,6144]{1,0:T(8,128)(2,1)S(1)}, bf16[16,6144]{1,0:T(8,128)(2,1)S(1)}, u32[]{:S(2)}, u32[]{:S(2)}) collective-permute-start(bf16[16,6144]{1,0:T(8,128)(2,1)S(1)} %get-tuple-element.105), channel_id=1, source_target_pairs={{0,8},{8,0},{16,24},{24,16},{1,9},{9,1},{17,25},{25,17},{2,10},{10... | collective-permute-start | bytes 589832 | tf_op jit(solution)/shard_map/ppermute | solution.py:24
  46.0 8.4 %collective-permute-start.14 = (bf16[16,6144]{1,0:T(8,128)(2,1)S(1)}, bf16[16,6144]{1,0:T(8,128)(2,1)S(1)}, u32[]{:S(2)}, u32[]{:S(2)}) collective-permute-start(bf16[16,6144]{1,0:T(8,128)(2,1)S(1)} %get-tuple-element.106), channel_id=1, source_target_pairs={{0,16},{8,24},{16,0},{24,8},{1,17},{9,25},{17,1},{25,9},{2,18},{10... | collective-permute-start | bytes 589832 | tf_op jit(solution)/shard_map/ppermute | solution.py:24
  46.6 7.9 %collective-permute-start.15 = (bf16[16,6144]{1,0:T(8,128)(2,1)S(1)}, bf16[16,6144]{1,0:T(8,128)(2,1)S(1)}, u32[]{:S(2)}, u32[]{:S(2)}) collective-permute-start(bf16[16,6144]{1,0:T(8,128)(2,1)S(1)} %get-tuple-element.107), channel_id=1, source_target_pairs={{0,24},{8,16},{16,8},{24,0},{1,25},{9,17},{17,9},{25,1},{2,26},{10... | collective-permute-start | bytes 589832 | tf_op jit(solution)/shard_map/ppermute | solution.py:24
  54.5 9.8 %collective-permute-start.18 = (bf16[16,3072]{1,0:T(8,128)(2,1)S(1)}, bf16[16,3072]{1,0:T(8,128)(2,1)S(1)}, u32[]{:S(2)}, u32[]{:S(2)}) collective-permute-start(bf16[16,3072]{1,0:T(8,128)(2,1)S(1)} %swiglu.7.refs_10_.refs_0_), channel_id=1, source_target_pairs={{0,24},{8,16},{16,8},{24,0},{1,25},{9,17},{17,9},{25,1},{2,26},{10... | collective-permute-start | bytes 294920 | tf_op jit(solution)/shard_map/ppermute | solution.py:24
  55.7 8.6 %collective-permute-start.17 = (bf16[16,3072]{1,0:T(8,128)(2,1)S(1)}, bf16[16,3072]{1,0:T(8,128)(2,1)S(1)}, u32[]{:S(2)}, u32[]{:S(2)}) collective-permute-start(bf16[16,3072]{1,0:T(8,128)(2,1)S(1)} %swiglu.7.refs_10_.refs_0_), channel_id=1, source_target_pairs={{0,16},{8,24},{16,0},{24,8},{1,17},{9,25},{17,1},{25,9},{2,18},{10... | collective-permute-start | bytes 294920 | tf_op jit(solution)/shard_map/ppermute | solution.py:24
  57.1 7.2 %collective-permute-start.16 = (bf16[16,3072]{1,0:T(8,128)(2,1)S(1)}, bf16[16,3072]{1,0:T(8,128)(2,1)S(1)}, u32[]{:S(2)}, u32[]{:S(2)}) collective-permute-start(bf16[16,3072]{1,0:T(8,128)(2,1)S(1)} %swiglu.7.refs_10_.refs_0_), channel_id=1, source_target_pairs={{0,8},{8,0},{16,24},{24,16},{1,9},{9,1},{17,25},{25,17},{2,10},{10... | collective-permute-start | bytes 294920 | tf_op jit(solution)/shard_map/ppermute | solution.py:24
  66.8 1.6 %collective-permute-start.19 = (f32[4,8,2048]{2,1,0:T(8,128)S(1)}, f32[4,8,2048]{2,1,0:T(8,128)S(1)}, u32[]{:S(2)}, u32[]{:S(2)}) collective-permute-start(f32[4,8,2048]{2,1,0:T(8,128)S(1)} %slice_bitcast_fusion), channel_id=1, source_target_pairs={{0,1},{1,0},{2,3},{3,2},{4,5},{5,4},{6,7},{7,6},{8,9},{9,8},{10,11... | collective-permute-start | bytes 786440 | tf_op jit(solution)/shard_map/ppermute | solution.py:24
  68.4 9.9 %collective-permute-start.20 = (f32[8,2048]{1,0:T(8,128)S(1)}, f32[8,2048]{1,0:T(8,128)S(1)}, u32[]{:S(2)}, u32[]{:S(2)}) collective-permute-start(f32[8,2048]{1,0:T(8,128)S(1)} %get-tuple-element.118), channel_id=1, source_target_pairs={{0,2},{1,3},{2,0},{3,1},{4,6},{5,7},{6,4},{7,5},{8,10},{9,11},{10,... | collective-permute-start | bytes 196616 | tf_op jit(solution)/shard_map/ppermute | solution.py:24
  69.7 8.7 %collective-permute-start.22 = (f32[8,2048]{1,0:T(8,128)S(1)}, f32[8,2048]{1,0:T(8,128)S(1)}, u32[]{:S(2)}, u32[]{:S(2)}) collective-permute-start(f32[8,2048]{1,0:T(8,128)S(1)} %get-tuple-element.119), channel_id=1, source_target_pairs={{0,6},{1,7},{2,4},{3,5},{4,2},{5,3},{6,0},{7,1},{8,14},{9,15},{10,... | collective-permute-start | bytes 196616 | tf_op jit(solution)/shard_map/ppermute | solution.py:24
  72.1 6.8 %collective-permute-start.21 = (f32[8,2048]{1,0:T(8,128)S(1)}, f32[8,2048]{1,0:T(8,128)S(1)}, u32[]{:S(2)}, u32[]{:S(2)}) collective-permute-start(f32[8,2048]{1,0:T(8,128)S(1)} %get-tuple-element.120), channel_id=1, source_target_pairs={{0,4},{1,5},{2,6},{3,7},{4,0},{5,1},{6,2},{7,3},{8,12},{9,13},{10,... | collective-permute-start | bytes 196616 | tf_op jit(solution)/shard_map/ppermute | solution.py:24

commit v4 on v3

--- a/solution.py
+++ b/solution.py
@@ -13,9 +13,9 @@
 SMEM = pl.BlockSpec(memory_space=pltpu.SMEM)
 CONTRACT_LAST = (((1,), (1,)), ((), ()))
 CONTRACT_FIRST = (((0,), (0,)), ((), ()))
-CUTS = (0, 4, 12, 20, 28)
+CUTS = (0, 8, 16, 26, 28)
 SPLIT = (0, 1, 2)
-PARAMS = pltpu.CompilerParams(vmem_limit_bytes=14 << 20)
+PARAMS = pltpu.CompilerParams(vmem_limit_bytes=15 << 20)
 vmem = pltpu.VMEM
 shape = jax.ShapeDtypeStruct
 
@@ -87,50 +87,60 @@
         copy.wait()
 
 
-def forward_kernel(start, width, ready, wanted, own, sends, tile, me_ref, tokens_ref, grads_ref, gate_ref, up_ref, *refs):
-    if ready:
-        down_ref, refs = refs[0], refs[1:]
+def forward_kernel(start, width, given, wanted, own, sends, tile, me_ref, tokens_ref, grads_ref, *refs):
+    weights, refs = dict(zip(given, refs)), refs[len(given) :]
     sources, refs = refs[:3], refs[4:]
-    keep_ref, send_refs, refs = refs[0], refs[1 : 1 + sends], refs[1 + sends :]
+    keep_ref, send_refs, refs = refs[0], refs[1 : 1 + max(sends, 1)], refs[1 + max(sends, 1) :]
+    send_ref = send_refs[0]
     targets, refs = refs[: len(wanted)], refs[len(wanted) :]
-    if not ready:
-        down_ref, refs = refs[0], refs[1:]
-        wanted, targets = ((2, start, width), *wanted), (down_ref, *targets)
-    copies = weights_copies(sources, wanted, targets, refs[0])
+    streamed = [which for which in (0, 2, 1) if which not in given]
+    if 2 in streamed:
+        wanted, targets = ((2, start, width), *wanted), (refs[0], *targets)
+    pairs = sorted(zip(wanted, targets), key=lambda p: streamed.index(p[0][0]) if p[0] == (p[0][0], start, width) else 3)
+    copies = weights_copies(sources, [p[0] for p in pairs], [p[1] for p in pairs], refs[-1])
     for copy in copies:
         copy.start()
+    for which, (_, target) in zip(streamed, pairs):
+        weights[which] = target
 
     def put(i, at, part):
-        to = slice(i * width + at, i * width + at + tile)
-        keep_ref[:, to] = part[:own]
-        for s, ref in enumerate(send_refs):
-            ref[:, to] = part[(s + 1) * own : (s + 2) * own].astype(BF16)
-
-    def gate_and_up():
+        to = i * width + at
+        if sends == 0:
+            keep_ref[:, to : to + tile] = part
+            for k in range(part.shape[0] // own):
+                send_ref[:, 3 * k * width + to : 3 * k * width + to + tile] = part[k * own : (k + 1) * own].astype(BF16)
+        else:
+            keep_ref[:, to : to + tile] = part[:own]
+            for s, ref in enumerate(send_refs):
+                ref[:, to : to + tile] = part[(s + 1) * own : (s + 2) * own].astype(BF16)
+
+    def product(which):
         for at in range(0, width, tile):
-            put(0, at, jnp.dot(tokens_ref[...], gate_ref[:, at : at + tile], preferred_element_type=F32))
-            put(1, at, jnp.dot(tokens_ref[...], up_ref[:, at : at + tile], preferred_element_type=F32))
-
-    def back():
-        for at in range(0, width, tile):
-            down = down_ref[at : at + tile, :]
-            put(2, at, lax.dot_general(grads_ref[...], down, CONTRACT_LAST, preferred_element_type=F32))
-
-    if ready:
+            if which == 2:
+                down = weights[2][at : at + tile, :]
+                put(2, at, lax.dot_general(grads_ref[...], down, CONTRACT_LAST, preferred_element_type=F32))
+            else:
+                columns = weights[which][:, at : at + tile]
+                put(which, at, jnp.dot(tokens_ref[...], columns, preferred_element_type=F32))
+
+    if given:
 
         @pl.when(me_ref[0] >= 0)
         def _():
-            gate_and_up()
-            back()
-
-        for copy in copies:
-            copy.wait()
-    else:
-        pl.when(me_ref[0] >= 0)(gate_and_up)
-        copies[0].wait()
-        pl.when(me_ref[0] >= 0)(back)
-        for copy in copies[1:]:
-            copy.wait()
+            for which in given:
+                product(which)
+
+    for which, copy in zip(streamed, copies):
+        copy.wait()
+        pl.when(me_ref[0] >= 0)(functools.partial(product, which))
+    for copy in copies[len(streamed) :]:
+        copy.wait()
+
+
+def gradients(sums, width):
+    gate, upward, back = (sums[:, i * width : (i + 1) * width] for i in range(3))
+    sigma = 1.0 / (1.0 + jnp.exp(-gate))
+    return back * upward * sigma * (1.0 + gate * (1.0 - sigma)), back * gate * sigma, gate * sigma * upward
 
 
 def swiglu_kernel(width, n, after_ref, keep_ref, *refs):
@@ -139,10 +149,7 @@
     sums = keep_ref[...]
     for ref in pieces:
         sums = sums + ref[:, : 3 * width].astype(F32)
-    gate, upward, back = (sums[:, i * width : (i + 1) * width] for i in range(3))
-    sigma = 1.0 / (1.0 + jnp.exp(-gate))
-    parts = (back * upward * sigma * (1.0 + gate * (1.0 - sigma)), back * gate * sigma, gate * sigma * upward)
-    for i, part in enumerate(parts):
+    for i, part in enumerate(gradients(sums, width)):
         out_ref[:, i * width : (i + 1) * width] = part.astype(BF16)
     for before, after in zip(later, send_refs):
         split = before.shape[1]
@@ -150,16 +157,35 @@
         after[:, split:] = out_ref[...]
 
 
-def input_kernel(width, n, me_ref, *refs):
-    pieces, (gate_ref, up_ref, sum_ref, out_ref) = refs[:n], refs[n:]
-    grads = jnp.concatenate([ref[:, : 2 * width] for ref in pieces], axis=0)
-    turned = (grads[:, :width].T, grads[:, width:].T)
-    own = pieces[0].shape[0]
-    for at, size in tiles(gate_ref.shape[0], 512):
+def swiglu_all_kernel(width, n, after_ref, keep_ref, *refs):
+    pieces, out_refs = refs[: n - 1], refs[n - 1 :]
+    own = out_refs[0].shape[0]
+    for k, out_ref in enumerate(out_refs):
+        sums = keep_ref[k * own : (k + 1) * own, :]
+        for s, ref in enumerate(pieces):
+            at = 3 * (k ^ (s + 1)) * width
+            sums = sums + ref[:, at : at + 3 * width].astype(F32)
+        for i, part in enumerate(gradients(sums, width)):
+            out_ref[:, i * width : (i + 1) * width] = part.astype(BF16)
+
+
+def input_kernel(n, chunks, me_ref, *refs):
+    sum_ref, out_ref = refs[-2:]
+    products = []
+    for i, (width, shift) in enumerate(chunks):
+        mine_ref, *pieces = refs[i * n : (i + 1) * n]
+        weights = refs[n * len(chunks) + 2 * i : n * len(chunks) + 2 * i + 2]
+        for j, ref in enumerate(weights):
+            cols = slice(j * width, (j + 1) * width)
+            others = [r[:, shift + j * width : shift + (j + 1) * width] for r in pieces]
+            products.append((ref, jnp.concatenate([mine_ref[:, cols]] + others, axis=0).T))
+    own = refs[0].shape[0]
+    for at, size in tiles(sum_ref.shape[0], 512):
         rows = slice(at, at + size)
-        part = jnp.dot(gate_ref[rows, :], turned[0], preferred_element_type=F32)
-        part += jnp.dot(up_ref[rows, :], turned[1], preferred_element_type=F32)
-        part = (part + sum_ref[rows, :]).T
+        part = sum_ref[rows, :]
+        for ref, grads in products:
+            part += jnp.dot(ref[rows, :], grads, preferred_element_type=F32)
+        part = part.T
         for k in range(n):
             out_ref[pl.ds(pl.multiple_of((k ^ me_ref[0]) * own, 8), own), rows] = part[k * own : (k + 1) * own]
 
@@ -227,9 +253,8 @@
     me = lax.axis_index("row").astype(jnp.int32).reshape(1)
     w_gate, w_up, w_down = (pltpu.with_memory_space_constraint(w, pltpu.HBM) for w in (w_gate, w_up, w_down))
     units = hidden // 128
-    cuts = [-(-units * part // 28) * 128 for part in CUTS]
-    chunks = [(a, b - a) for a, b in zip(cuts[:-1], cuts[1:])]
-    one, two, three, four = chunks
+    cuts = [128 * min(-(-units * part // 28), units - (len(CUTS) - 1 - i)) for i, part in enumerate(CUTS)]
+    one, two, three, four = ((a, b - a) for a, b in zip(cuts[:-1], cuts[1:]))
 
     def held(wanted):
         return [vmem((width, depth) if which == 2 else (depth, width), BF16) for which, _, width in wanted]
@@ -243,13 +268,13 @@
         compiler_params=PARAMS,
         name="pair",
     )(*(pltpu.with_memory_space_constraint(x, pltpu.HBM) for x in (activations, out_grad)))
-    wanted = ((0, *one), (1, *one), (2, *one), (0, *two), (1, *two))
-    gate_one, up_one, down_one, gate_two, up_two, fetched = pl.pallas_call(
+    wanted = ((0, *one), (1, *one), (2, *one))
+    gate_one, up_one, down_one, fetched = pl.pallas_call(
         functools.partial(fetch_kernel, wanted),
         out_shape=held(wanted) + [shape((8, 128), F32)],
         in_specs=[SMEM] + [HBM] * 3,
-        out_specs=[VMEM] * 6,
-        scratch_shapes=[pltpu.SemaphoreType.DMA((5,))],
+        out_specs=[VMEM] * 4,
+        scratch_shapes=[pltpu.SemaphoreType.DMA((3,))],
         compiler_params=PARAMS,
         name="fetch",
     )(me, w_gate, w_up, w_down)
@@ -273,18 +298,24 @@
         name="order",
     )(me, near, far)
 
-    def forward(start, width, gate, up, down, wanted, after):
-        ready = down is not None
+    def forward(start, width, gate, up, down, wanted, after, whole=False):
+        weights = (gate, up, down)
+        given = tuple(i for i, x in enumerate(weights) if x is not None)
+        sends = 0 if whole else n_row - 1
+        if whole:
+            sums = [vmem((total, 3 * width), F32), vmem((own, 3 * n_row * width), BF16)]
+        else:
+            sums = [vmem((own, 3 * width), F32)] + [vmem((own, 3 * width), BF16)] * sends
         keep, *rest = pl.pallas_call(
-            functools.partial(forward_kernel, start, width, ready, wanted, own, n_row - 1, tile_of(width)),
-            out_shape=[vmem((own, 3 * width), F32)] + [vmem((own, 3 * width), BF16)] * (n_row - 1) + held(wanted),
-            in_specs=[SMEM] + [VMEM] * (5 if ready else 4) + [HBM] * 4,
-            out_specs=[VMEM] * (n_row + len(wanted)),
-            scratch_shapes=([] if ready else [vmem((width, depth), BF16)]) + [pltpu.SemaphoreType.DMA((3,))],
+            functools.partial(forward_kernel, start, width, given, wanted, own, sends, tile_of(width)),
+            out_shape=sums + held(wanted),
+            in_specs=[SMEM] + [VMEM] * (2 + len(given)) + [HBM] * 4,
+            out_specs=[VMEM] * (len(sums) + len(wanted)),
+            scratch_shapes=([vmem((width, depth), BF16)] if down is None else []) + [pltpu.SemaphoreType.DMA((len(wanted) + 1,))],
             compiler_params=PARAMS,
             name="forward",
-        )(me, tokens, grads, gate, up, *([down] if ready else []), w_gate, w_up, w_down, after)
-        return keep, rest[: n_row - 1], rest[n_row - 1 :]
+        )(me, tokens, grads, *(x for x in weights if x is not None), w_gate, w_up, w_down, after)
+        return keep, rest[: len(sums) - 1], rest[len(sums) - 1 :]
 
     def to_others(blocks):
         return [exchange(x, "row", n_row, s + 1) for s, x in enumerate(blocks)]
@@ -319,40 +350,49 @@
             name=name,
         )(me, turned, grads, *pieces, *weights, *outs, after)
 
-    keep_one, sends, (down_two,) = forward(*one, gate_one, up_one, down_one, ((2, *two),), me)
+    keep_one, sends, (gate_two,) = forward(*one, gate_one, up_one, down_one, ((0, *two),), me)
     got_one = to_others(sends)
-    keep_two, sends, (gate_three, up_three) = forward(*two, gate_two, up_two, down_two, ((0, *three), (1, *three)), me)
+    keep_two, sends, (up_two,) = forward(*two, gate_two, None, None, ((1, *two),), me)
     mine_one, sends = swiglu(one[1], keep_one, got_one, sends, me)
     got_two = to_others(sends)
-    keep_three, sends, (gate_four, up_four) = forward(*three, gate_three, up_three, None, ((0, *four), (1, *four)), mine_one)
+    keep_three, sends, (gate_three, up_three, gate_four, up_four, down_four) = forward(
+        *three, None, None, None, ((0, *three), (1, *three), (0, *four), (1, *four), (2, *four)), mine_one
+    )
     mine_two, sends = swiglu(two[1], keep_two, got_two, sends, me)
     got_three = to_others(sends)
-    keep_four, sends, _ = forward(*four, gate_four, up_four, None, (), mine_two)
+    keep_four, sends, _ = forward(*four, gate_four, up_four, down_four, (), mine_two, whole=True)
     *outs, grad_input = backward(
-        *one, 3 * two[1], 0, one[1], tile_of(one[1], 256), [mine_one, *got_two], (gate_one, up_one), (), mine_two, "backward_one"
+        *one, 3 * two[1], 0, one[1], tile_of(one[1]), [mine_one, *got_two], (gate_one, up_one), (), mine_two, "backward_one"
     )
     mine_three, sends = swiglu(three[1], keep_three, got_three, sends, grad_input)
-    got_four = to_others(sends)
+    got_four = to_others(sends * (n_row - 1))
     *outs, grad_input = backward(
         *two, 3 * three[1], 0, two[1], tile_of(two[1]), [mine_two, *got_three], (gate_two, up_two, grad_input), outs, mine_three, "backward_two"
     )
-    mine_four, _ = swiglu(four[1], keep_four, got_four, (), grad_input)
-    got_last = to_others([mine_four] * (n_row - 1))
-    *outs, grad_input = backward(
-        *three, 3 * four[1], 0, three[1], tile_of(three[1]), [mine_three, *got_four], (gate_three, up_three, grad_input), outs, mine_four, "backward_three"
-    )
-    pieces = [mine_four, *got_last]
+    pieces = [mine_three, *got_four]
+    pieces_four = pl.pallas_call(
+        functools.partial(swiglu_all_kernel, four[1], n_row),
+        out_shape=[vmem((own, 3 * four[1]), BF16)] * n_row,
+        in_specs=[HBM] + [VMEM] * n_row,
+        out_specs=[VMEM] * n_row,
+        compiler_params=PARAMS,
+        name="swiglu_all",
+    )(grad_input, keep_four, *got_four)
+    shift = 3 * n_row * four[1]
     grad_input = pl.pallas_call(
-        functools.partial(input_kernel, four[1], n_row),
+        functools.partial(input_kernel, n_row, ((three[1], shift), (four[1], 0))),
         out_shape=vmem((total, depth), F32),
-        in_specs=[SMEM] + [VMEM] * (n_row + 3),
+        in_specs=[SMEM] + [VMEM] * (2 * n_row + 5),
         out_specs=VMEM,
         compiler_params=PARAMS,
         name="input_grad",
-    )(me, *pieces, gate_four, up_four, grad_input)
+    )(me, *pieces, *pieces_four, gate_three, up_three, gate_four, up_four, grad_input)
     blocks = grad_input.reshape(n_col // 2, 2, share, depth)
-    summed = blocks[:, 0] + exchange(blocks[:, 1], "col", n_col, 1)
-    outs = backward(*four, 0, 0, four[1], tile_of(four[1], 256), pieces, (), outs, summed, "weight_grads")
+    outs = backward(*four, 0, 0, four[1], tile_of(four[1], 256), pieces_four, (), outs, grad_input, "weight_grads_early")
+    other = exchange(blocks[:, 1], "col", n_col, 1)
+    other, *outs = lax.optimization_barrier((other, *outs))
+    summed = blocks[:, 0] + other
+    outs = backward(*three, shift, 0, three[1], tile_of(three[1], 256), pieces, (), outs, summed, "weight_grads")
     result = summed[0]
     for k in range(1, n_col // 2):
         result = result + exchange(summed[k], "col", n_col, 2 * k)

time: 79.9 us -> 76.3 us (0.955)
  starting transfers between devices: 27.9 us -> 24.3 us
  Pallas kernels: 44.6 us -> 46.4 us
  waiting for transfers between devices: 5.46 us -> 3.85 us
    ppermute x23 -> x20, starting transfers between devices: 27.9 us -> 24.3 us  [exchange(): return lax.ppermute(x, axis, [(i, i ^ offset) for i in range(size)])]
    pallas_call x5 -> x6, Pallas kernels: 16.4 us -> 18.6 us  [the longest x4 15 us: forward(): pl.pallas_call(functools.partial(forward_kernel, start, width, given, wan...]
    ppermute x23 -> x20, waiting for transfers between devices: 5.46 us -> 3.85 us  [exchange(): return lax.ppermute(x, axis, [(i, i ^ offset) for i in range(size)])]
  transfers between devices with their start and end apart: 23 -> 20, of which waited for: 5 -> 5; matrix products, arithmetic and copies ran while one was open for 0% -> 0% of each run, Pallas kernels for 48% -> 51%
where the time goes in v4:
time: 76.3 us; the launch traced here: 76.1 us
  Pallas kernels  46.4 us (61%)
  starting transfers between devices  24.3 us (32%)
  waiting for transfers between devices  3.85 us (5%)
  between operations  0.89 us (1%)
    ppermute x20, starting transfers between devices, exchange(): return lax.ppermute(x, axis, [(i, i ^ offset) for i in range(size)])  24.3 us
    pallas_call x4, Pallas kernels, backward(): pl.pallas_call(functools.partial(backward_kernel, n_row, start, width, sh...  21.6 us
    pallas_call x4, Pallas kernels, forward(): pl.pallas_call(functools.partial(forward_kernel, start, width, given, wan...  15 us
    pallas_call x1, Pallas kernels, per_device(): pl.pallas_call(functools.partial(fetch_kernel, wanted), out_shape=held(wa...  4.75 us
    ppermute x20, waiting for transfers between devices, exchange(): return lax.ppermute(x, axis, [(i, i ^ offset) for i in range(size)])  3.85 us
    pallas_call x1, Pallas kernels, per_device(): pl.pallas_call(functools.partial(input_kernel, n_row, ((three[1], shift),...  3.47 us
  transfers between devices with their start and end apart: 20, of which 5 were waited for; matrix products, arithmetic and copies ran while one was open for 0% of the time, Pallas kernels for 51%

profile of v4, /device:TPU:0, one launch (start us, length us, event | category | flops | bytes accessed | tf_op | source)
XLA Modules:
  0.0 76.1 jit_solution(9205647854537445318)
XLA Ops:
  1.4 5.1 %collective-permute-start.2 = (bf16[16,2048]{1,0:T(8,128)(2,1)S(1)}, bf16[16,2048]{1,0:T(8,128)(2,1)S(1)}, u32[]{:S(2)}, u32[]{:S(2)}) collective-permute-start(bf16[16,2048]{1,0:T(8,128)(2,1)S(1)} %pair.1.refs_0_), channel_id=1, source_target_pairs={{0,6},{1,7},{2,4},{3,5},{4,2},{5,3},{6,0},{7,1},{8,14},{9,15},{10,... | collective-permute-start | bytes 196616 | tf_op jit(solution)/shard_map/ppermute | solution.py:24
  7.2 4.8 %fetch.1 = (bf16[2048,1024]{1,0:T(8,128)(2,1)S(1)}, bf16[2048,1024]{1,0:T(8,128)(2,1)S(1)}, bf16[1024,2048]{1,0:T(8,128)(2,1)S(1)}, f32[8,128]{1,0:T(8,128)S(1)}) custom-call(s32[1]{0:T(128)} %bitcast.me_ref.refs_6_.refs_4_.after_ref, bf16[2048,3584]{1,0:T(8,128)(2,1)} %refs_3_.5, bf16[2048,3584]{1,0:T(8,128)(2,1)} %refs_4_.3, bf16[3584,2048]{1,0:T(8,128)(2,1)} %refs_5_.3), custom_call_target="tpu_custom_call" | custom-call | tf_op jit(solution)/shard_map/fetch/pallas_call | solution.py:272
  12.3 1.5 %collective-permute-done.3.other_ref = bf16[64,2048]{1,0:T(8,128)(2,1)S(1)} collective-permute-done((bf16[64,2048]{1,0:T(8,128)(2,1)S(1)}, bf16[64,2048]{1,0:T(8,128)(2,1)S(1)}, u32[]{:S(2)}, u32[]{:S(2)}) %collective-permute-start.3) | collective-permute-done | bytes 262176 | tf_op jit(solution)/shard_map/ppermute | solution.py:24
  14.1 2.9 %forward.4 = (f32[16,3072]{1,0:T(8,128)S(1)}, bf16[16,3072]{1,0:T(8,128)(2,1)S(1)}, bf16[16,3072]{1,0:T(8,128)(2,1)S(1)}, bf16[16,3072]{1,0:T(8,128)(2,1)S(1)}, bf16[2048,1024]{1,0:T(8,128)(2,1)S(1)}) custom-call(s32[1]{0:T(128)} %bitcast.me_ref.refs_6_.refs_4_.after_ref, bf16[64,2048]{1,0:T(8,128)(2,1)S(1)} %get-tuple-element.67.tokens_ref, ...), custom_call_target="tpu_custom_call" | custom-call | tf_op jit(solution)/shard_map/forward/pallas_call | solution.py:309
  17.0 1.6 %collective-permute-start.4 = (bf16[16,3072]{1,0:T(8,128)(2,1)S(1)}, bf16[16,3072]{1,0:T(8,128)(2,1)S(1)}, u32[]{:S(2)}, u32[]{:S(2)}) collective-permute-start(bf16[16,3072]{1,0:T(8,128)(2,1)S(1)} %get-tuple-element.72), channel_id=1, source_target_pairs={{0,8},{8,0},{16,24},{24,16},{1,9},{9,1},{17,25},{25,17},{2,10},{10... | collective-permute-start | bytes 294920 | tf_op jit(solution)/shard_map/ppermute | solution.py:24
  18.5 1.5 %collective-permute-start.5 = (bf16[16,3072]{1,0:T(8,128)(2,1)S(1)}, bf16[16,3072]{1,0:T(8,128)(2,1)S(1)}, u32[]{:S(2)}, u32[]{:S(2)}) collective-permute-start(bf16[16,3072]{1,0:T(8,128)(2,1)S(1)} %get-tuple-element.73), channel_id=1, source_target_pairs={{0,16},{8,24},{16,0},{24,8},{1,17},{9,25},{17,1},{25,9},{2,18},{10... | collective-permute-start | bytes 294920 | tf_op jit(solution)/shard_map/ppermute | solution.py:24
  20.5 4.5 %forward.5 = (f32[16,3072]{1,0:T(8,128)S(1)}, bf16[16,3072]{1,0:T(8,128)(2,1)S(1)}, bf16[16,3072]{1,0:T(8,128)(2,1)S(1)}, bf16[16,3072]{1,0:T(8,128)(2,1)S(1)}, bf16[2048,1024]{1,0:T(8,128)(2,1)S(1)}) custom-call(s32[1]{0:T(128)} %bitcast.me_ref.refs_6_.refs_4_.after_ref, bf16[64,2048]{1,0:T(8,128)(2,1)S(1)} %get-tuple-element.67.tokens_ref, ...), custom_call_target="tpu_custom_call" | custom-call | tf_op jit(solution)/shard_map/forward/pallas_call | solution.py:309
  25.7 1.0 %collective-permute-start.7 = (bf16[16,6144]{1,0:T(8,128)(2,1)S(1)}, bf16[16,6144]{1,0:T(8,128)(2,1)S(1)}, u32[]{:S(2)}, u32[]{:S(2)}) collective-permute-start(bf16[16,6144]{1,0:T(8,128)(2,1)S(1)} %get-tuple-element.80), channel_id=1, source_target_pairs={{0,8},{8,0},{16,24},{24,16},{1,9},{9,1},{17,25},{25,17},{2,10},{10... | collective-permute-start | bytes 589832 | tf_op jit(solution)/shard_map/ppermute | solution.py:24
  26.7 1.5 %collective-permute-start.8 = (bf16[16,6144]{1,0:T(8,128)(2,1)S(1)}, bf16[16,6144]{1,0:T(8,128)(2,1)S(1)}, u32[]{:S(2)}, u32[]{:S(2)}) collective-permute-start(bf16[16,6144]{1,0:T(8,128)(2,1)S(1)} %get-tuple-element.81), channel_id=1, source_target_pairs={{0,16},{8,24},{16,0},{24,8},{1,17},{9,25},{17,1},{25,9},{2,18},{10... | collective-permute-start | bytes 589832 | tf_op jit(solution)/shard_map/ppermute | solution.py:24
  28.2 1.0 %collective-permute-start.9 = (bf16[16,6144]{1,0:T(8,128)(2,1)S(1)}, bf16[16,6144]{1,0:T(8,128)(2,1)S(1)}, u32[]{:S(2)}, u32[]{:S(2)}) collective-permute-start(bf16[16,6144]{1,0:T(8,128)(2,1)S(1)} %get-tuple-element.82), channel_id=1, source_target_pairs={{0,24},{8,16},{16,8},{24,0},{1,25},{9,17},{17,9},{25,1},{2,26},{10... | collective-permute-start | bytes 589832 | tf_op jit(solution)/shard_map/ppermute | solution.py:24
  29.3 6.9 %forward.6 = (f32[16,3840]{1,0:T(8,128)S(1)}, bf16[16,3840]{1,0:T(8,128)(2,1)S(1)}, bf16[16,3840]{1,0:T(8,128)(2,1)S(1)}, bf16[16,3840]{1,0:T(8,128)(2,1)S(1)}, ...) custom-call(s32[1]{0:T(128)} %bitcast.me_ref.refs_6_.refs_4_.after_r, ...), custom_call_target="tpu_custom_call" | custom-call | tf_op jit(solution)/shard_map/forward/pallas_call | solution.py:309
  36.9 1.3 %collective-permute-start.10 = (bf16[16,6912]{1,0:T(8,128)(2,1)S(1)}, bf16[16,6912]{1,0:T(8,128)(2,1)S(1)}, u32[]{:S(2)}, u32[]{:S(2)}) collective-permute-start(bf16[16,6912]{1,0:T(8,128)(2,1)S(1)} %get-tuple-element.90), channel_id=1, source_target_pairs={{0,8},{8,0},{16,24},{24,16},{1,9},{9,1},{17,25},{25,17},{2,10},{10... | collective-permute-start | bytes 663560 | tf_op jit(solution)/shard_map/ppermute | solution.py:24
  38.2 0.9 %collective-permute-start.11 = (bf16[16,6912]{1,0:T(8,128)(2,1)S(1)}, bf16[16,6912]{1,0:T(8,128)(2,1)S(1)}, u32[]{:S(2)}, u32[]{:S(2)}) collective-permute-start(bf16[16,6912]{1,0:T(8,128)(2,1)S(1)} %get-tuple-element.91), channel_id=1, source_target_pairs={{0,16},{8,24},{16,0},{24,8},{1,17},{9,25},{17,1},{25,9},{2,18},{10... | collective-permute-start | bytes 663560 | tf_op jit(solution)/shard_map/ppermute | solution.py:24
  39.1 1.4 %collective-permute-start.12 = (bf16[16,6912]{1,0:T(8,128)(2,1)S(1)}, bf16[16,6912]{1,0:T(8,128)(2,1)S(1)}, u32[]{:S(2)}, u32[]{:S(2)}) collective-permute-start(bf16[16,6912]{1,0:T(8,128)(2,1)S(1)} %get-tuple-element.92), channel_id=1, source_target_pairs={{0,24},{8,16},{16,8},{24,0},{1,25},{9,17},{17,9},{25,1},{2,26},{10... | collective-permute-start | bytes 663560 | tf_op jit(solution)/shard_map/ppermute | solution.py:24
  41.3 6.1 %backward_one.1 = (bf16[2048,3584]{1,0:T(8,128)(2,1)}, bf16[2048,3584]{1,0:T(8,128)(2,1)}, bf16[3584,2048]{1,0:T(8,128)(2,1)}, f32[2048,64]{1,0:T(8,128)S(1)}) custom-call(s32[1]{0:T(128)} %bitcast.me_ref.refs_6_.refs_4_.after_ref, bf16[2048,64]{1,0:T(8,128)(2,1)S(1)} %get-tuple-element.65.turned_ref, bf16[64,2048]{1,0:T(8,128)(2,1)S(1)} %get-tuple-element.66.grads_ref, ...), custom_call_target="tpu_custom_call" | custom-call | tf_op jit(solution)/shard_map/backward_one/pallas_call | solution.py:336
  47.4 0.9 %collective-permute-done.11.refs_1_.refs_2_ = bf16[16,6912]{1,0:T(8,128)(2,1)S(1)} collective-permute-done((bf16[16,6912]{1,0:T(8,128)(2,1)S(1)}, bf16[16,6912]{1,0:T(8,128)(2,1)S(1)}, u32[]{:S(2)}, u32[]{:S(2)}) %collective-permute-start.11) | collective-permute-done | bytes 221216 | tf_op jit(solution)/shard_map/ppermute | solution.py:24
  48.5 1.6 %collective-permute-start.15 = (bf16[16,6912]{1,0:T(8,128)(2,1)S(1)}, bf16[16,6912]{1,0:T(8,128)(2,1)S(1)}, u32[]{:S(2)}, u32[]{:S(2)}) collective-permute-start(bf16[16,6912]{1,0:T(8,128)(2,1)S(1)} %get-tuple-element.98), channel_id=1, source_target_pairs={{0,24},{8,16},{16,8},{24,0},{1,25},{9,17},{17,9},{25,1},{2,26},{10... | collective-permute-start | bytes 663560 | tf_op jit(solution)/shard_map/ppermute | solution.py:24
  50.7 1.4 %collective-permute-start.13 = (bf16[16,6912]{1,0:T(8,128)(2,1)S(1)}, bf16[16,6912]{1,0:T(8,128)(2,1)S(1)}, u32[]{:S(2)}, u32[]{:S(2)}) collective-permute-start(bf16[16,6912]{1,0:T(8,128)(2,1)S(1)} %get-tuple-element.98), channel_id=1, source_target_pairs={{0,8},{8,0},{16,24},{24,16},{1,9},{9,1},{17,25},{25,17},{2,10},{10... | collective-permute-start | bytes 663560 | tf_op jit(solution)/shard_map/ppermute | solution.py:24
  52.0 6.0 %backward_two.1 = (bf16[2048,3584]{1,0:T(8,128)(2,1)}, bf16[2048,3584]{1,0:T(8,128)(2,1)}, bf16[3584,2048]{1,0:T(8,128)(2,1)}, f32[2048,64]{1,0:T(8,128)S(1)}) custom-call(s32[1]{0:T(128)} %bitcast.me_ref.refs_6_.refs_4_.after_ref, bf16[2048,64]{1,0:T(8,128)(2,1)S(1)} %get-tuple-element.65.turned_ref, ...), custom_call_target="tpu_custom_call", output_to_operand_aliasing={{0}: (10, {}), {1}: (11, {}), {2}: (12, {})} | custom-call | tf_op jit(solution)/shard_map/backward_two/pallas_call | solution.py:336
  58.2 3.5 %input_grad.1.refs_7_ = f32[64,2048]{1,0:T(8,128)S(1)} custom-call(s32[1]{0:T(128)} %bitcast.me_ref.refs_6_.refs_4_.after_ref, bf16[16,3840]{1,0:T(8,128)(2,1)S(1)} %get-tuple-element.97.refs_10_.refs_0_, bf16[16,6912]{1,0:T(8,128)(2,1)S(1)} %collective-permute-done.13.refs_0_.refs_1_, bf16[16,6912]{1,0:T(8,128)(2,1)S(1)} %collective-permute-done.14.refs_1_.refs_2_, ...), custom_call_target="tpu_custom_call" | custom-call | tf_op jit(solution)/shard_map/input_grad/pallas_call | solution.py:382
  61.8 2.4 %weight_grads_early.1 = (bf16[2048,3584]{1,0:T(8,128)(2,1)}, bf16[2048,3584]{1,0:T(8,128)(2,1)}, bf16[3584,2048]{1,0:T(8,128)(2,1)}) custom-call(s32[1]{0:T(128)} %bitcast.me_ref.refs_6_.refs_4_.after_ref, bf16[2048,64]{1,0:T(8,128)(2,1)S(1)} %get-tuple-element.65.turned_ref, ...), custom_call_target="tpu_custom_call", output_to_operand_aliasing={{0}: (7, {}), {1}: (8, {}), {2}: (9, {})} | custom-call | tf_op jit(solution)/shard_map/weight_grads_early/pallas_call | solution.py:336
  64.3 1.3 %collective-permute-start.17 = (f32[8,2048]{1,0:T(8,128)S(1)}, f32[8,2048]{1,0:T(8,128)S(1)}, u32[]{:S(2)}, u32[]{:S(2)}) collective-permute-start(f32[8,2048]{1,0:T(8,128)S(1)} %get-tuple-element.124), channel_id=1, source_target_pairs={{0,2},{1,3},{2,0},{3,1},{4,6},{5,7},{6,4},{7,5},{8,10},{9,11},{10,... | collective-permute-start | bytes 196616 | tf_op jit(solution)/shard_map/ppermute | solution.py:24
  65.6 2.4 %collective-permute-start.19 = (f32[8,2048]{1,0:T(8,128)S(1)}, f32[8,2048]{1,0:T(8,128)S(1)}, u32[]{:S(2)}, u32[]{:S(2)}) collective-permute-start(f32[8,2048]{1,0:T(8,128)S(1)} %get-tuple-element.125), channel_id=1, source_target_pairs={{0,6},{1,7},{2,4},{3,5},{4,2},{5,3},{6,0},{7,1},{8,14},{9,15},{10,... | collective-permute-start | bytes 196616 | tf_op jit(solution)/shard_map/ppermute | solution.py:24
  68.4 7.0 %weight_grads.1 = (bf16[2048,3584]{1,0:T(8,128)(2,1)}, bf16[2048,3584]{1,0:T(8,128)(2,1)}, bf16[3584,2048]{1,0:T(8,128)(2,1)}) custom-call(s32[1]{0:T(128)} %bitcast.me_ref.refs_6_.refs_4_.after_ref, bf16[2048,64]{1,0:T(8,128)(2,1)S(1)} %get-tuple-element.65.turned_ref, ...), custom_call_target="tpu_custom_call", output_to_operand_aliasing={{0}: (7, {}), {1}: (8, {}), {2}: (9, {})} | custom-call | tf_op jit(solution)/shard_map/weight_grads/pallas_call | solution.py:336
  (37 shorter events, 6.8 us)
Async XLA Ops:
  1.4 10.5 %collective-permute-start.2 = (bf16[16,2048]{1,0:T(8,128)(2,1)S(1)}, bf16[16,2048]{1,0:T(8,128)(2,1)S(1)}, u32[]{:S(2)}, u32[]{:S(2)}) collective-permute-start(bf16[16,2048]{1,0:T(8,128)(2,1)S(1)} %pair.1.refs_0_), channel_id=1, source_target_pairs={{0,6},{1,7},{2,4},{3,5},{4,2},{5,3},{6,0},{7,1},{8,14},{9,15},{10,... | collective-permute-start | bytes 196616 | tf_op jit(solution)/shard_map/ppermute | solution.py:24
  6.6 5.6 %collective-permute-start.1 = (bf16[16,2048]{1,0:T(8,128)(2,1)S(1)}, bf16[16,2048]{1,0:T(8,128)(2,1)S(1)}, u32[]{:S(2)}, u32[]{:S(2)}) collective-permute-start(bf16[16,2048]{1,0:T(8,128)(2,1)S(1)} %pair.1.refs_0_), channel_id=1, source_target_pairs={{0,4},{1,5},{2,6},{3,7},{4,0},{5,1},{6,2},{7,3},{8,12},{9,13},{10,... | collective-permute-start | bytes 196616 | tf_op jit(solution)/shard_map/ppermute | solution.py:24
  6.6 5.6 %collective-permute-start = (bf16[16,2048]{1,0:T(8,128)(2,1)S(1)}, bf16[16,2048]{1,0:T(8,128)(2,1)S(1)}, u32[]{:S(2)}, u32[]{:S(2)}) collective-permute-start(bf16[16,2048]{1,0:T(8,128)(2,1)S(1)} %pair.1.refs_0_), channel_id=1, source_target_pairs={{0,2},{1,3},{2,0},{3,1},{4,6},{5,7},{6,4},{7,5},{8,10},{9,11},{10,... | collective-permute-start | bytes 196616 | tf_op jit(solution)/shard_map/ppermute | solution.py:24
  12.2 1.6 %collective-permute-start.3 = (bf16[64,2048]{1,0:T(8,128)(2,1)S(1)}, bf16[64,2048]{1,0:T(8,128)(2,1)S(1)}, u32[]{:S(2)}, u32[]{:S(2)}) collective-permute-start(bf16[64,2048]{1,0:T(8,128)(2,1)S(1)} %join.1.mine_ref), channel_id=1, source_target_pairs={{0,1},{1,0},{2,3},{3,2},{4,5},{5,4},{6,7},{7,6},{8,9},{9,8},{10,11... | collective-permute-start | bytes 786440 | tf_op jit(solution)/shard_map/ppermute | solution.py:24
  17.0 8.0 %collective-permute-start.4 = (bf16[16,3072]{1,0:T(8,128)(2,1)S(1)}, bf16[16,3072]{1,0:T(8,128)(2,1)S(1)}, u32[]{:S(2)}, u32[]{:S(2)}) collective-permute-start(bf16[16,3072]{1,0:T(8,128)(2,1)S(1)} %get-tuple-element.72), channel_id=1, source_target_pairs={{0,8},{8,0},{16,24},{24,16},{1,9},{9,1},{17,25},{25,17},{2,10},{10... | collective-permute-start | bytes 294920 | tf_op jit(solution)/shard_map/ppermute | solution.py:24
  18.5 6.5 %collective-permute-start.5 = (bf16[16,3072]{1,0:T(8,128)(2,1)S(1)}, bf16[16,3072]{1,0:T(8,128)(2,1)S(1)}, u32[]{:S(2)}, u32[]{:S(2)}) collective-permute-start(bf16[16,3072]{1,0:T(8,128)(2,1)S(1)} %get-tuple-element.73), channel_id=1, source_target_pairs={{0,16},{8,24},{16,0},{24,8},{1,17},{9,25},{17,1},{25,9},{2,18},{10... | collective-permute-start | bytes 294920 | tf_op jit(solution)/shard_map/ppermute | solution.py:24
  20.1 5.5 %collective-permute-start.6 = (bf16[16,3072]{1,0:T(8,128)(2,1)S(1)}, bf16[16,3072]{1,0:T(8,128)(2,1)S(1)}, u32[]{:S(2)}, u32[]{:S(2)}) collective-permute-start(bf16[16,3072]{1,0:T(8,128)(2,1)S(1)} %get-tuple-element.74), channel_id=1, source_target_pairs={{0,24},{8,16},{16,8},{24,0},{1,25},{9,17},{17,9},{25,1},{2,26},{10... | collective-permute-start | bytes 294920 | tf_op jit(solution)/shard_map/ppermute | solution.py:24
  25.7 10.4 %collective-permute-start.7 = (bf16[16,6144]{1,0:T(8,128)(2,1)S(1)}, bf16[16,6144]{1,0:T(8,128)(2,1)S(1)}, u32[]{:S(2)}, u32[]{:S(2)}) collective-permute-start(bf16[16,6144]{1,0:T(8,128)(2,1)S(1)} %get-tuple-element.80), channel_id=1, source_target_pairs={{0,8},{8,0},{16,24},{24,16},{1,9},{9,1},{17,25},{25,17},{2,10},{10... | collective-permute-start | bytes 589832 | tf_op jit(solution)/shard_map/ppermute | solution.py:24
  26.7 10.0 %collective-permute-start.8 = (bf16[16,6144]{1,0:T(8,128)(2,1)S(1)}, bf16[16,6144]{1,0:T(8,128)(2,1)S(1)}, u32[]{:S(2)}, u32[]{:S(2)}) collective-permute-start(bf16[16,6144]{1,0:T(8,128)(2,1)S(1)} %get-tuple-element.81), channel_id=1, source_target_pairs={{0,16},{8,24},{16,0},{24,8},{1,17},{9,25},{17,1},{25,9},{2,18},{10... | collective-permute-start | bytes 589832 | tf_op jit(solution)/shard_map/ppermute | solution.py:24
  28.2 8.5 %collective-permute-start.9 = (bf16[16,6144]{1,0:T(8,128)(2,1)S(1)}, bf16[16,6144]{1,0:T(8,128)(2,1)S(1)}, u32[]{:S(2)}, u32[]{:S(2)}) collective-permute-start(bf16[16,6144]{1,0:T(8,128)(2,1)S(1)} %get-tuple-element.82), channel_id=1, source_target_pairs={{0,24},{8,16},{16,8},{24,0},{1,25},{9,17},{17,9},{25,1},{2,26},{10... | collective-permute-start | bytes 589832 | tf_op jit(solution)/shard_map/ppermute | solution.py:24
  36.9 10.5 %collective-permute-start.10 = (bf16[16,6912]{1,0:T(8,128)(2,1)S(1)}, bf16[16,6912]{1,0:T(8,128)(2,1)S(1)}, u32[]{:S(2)}, u32[]{:S(2)}) collective-permute-start(bf16[16,6912]{1,0:T(8,128)(2,1)S(1)} %get-tuple-element.90), channel_id=1, source_target_pairs={{0,8},{8,0},{16,24},{24,16},{1,9},{9,1},{17,25},{25,17},{2,10},{10... | collective-permute-start | bytes 663560 | tf_op jit(solution)/shard_map/ppermute | solution.py:24
  38.2 10.2 %collective-permute-start.11 = (bf16[16,6912]{1,0:T(8,128)(2,1)S(1)}, bf16[16,6912]{1,0:T(8,128)(2,1)S(1)}, u32[]{:S(2)}, u32[]{:S(2)}) collective-permute-start(bf16[16,6912]{1,0:T(8,128)(2,1)S(1)} %get-tuple-element.91), channel_id=1, source_target_pairs={{0,16},{8,24},{16,0},{24,8},{1,17},{9,25},{17,1},{25,9},{2,18},{10... | collective-permute-start | bytes 663560 | tf_op jit(solution)/shard_map/ppermute | solution.py:24
  39.1 9.3 %collective-permute-start.12 = (bf16[16,6912]{1,0:T(8,128)(2,1)S(1)}, bf16[16,6912]{1,0:T(8,128)(2,1)S(1)}, u32[]{:S(2)}, u32[]{:S(2)}) collective-permute-start(bf16[16,6912]{1,0:T(8,128)(2,1)S(1)} %get-tuple-element.92), channel_id=1, source_target_pairs={{0,24},{8,16},{16,8},{24,0},{1,25},{9,17},{17,9},{25,1},{2,26},{10... | collective-permute-start | bytes 663560 | tf_op jit(solution)/shard_map/ppermute | solution.py:24
  48.5 9.6 %collective-permute-start.15 = (bf16[16,6912]{1,0:T(8,128)(2,1)S(1)}, bf16[16,6912]{1,0:T(8,128)(2,1)S(1)}, u32[]{:S(2)}, u32[]{:S(2)}) collective-permute-start(bf16[16,6912]{1,0:T(8,128)(2,1)S(1)} %get-tuple-element.98), channel_id=1, source_target_pairs={{0,24},{8,16},{16,8},{24,0},{1,25},{9,17},{17,9},{25,1},{2,26},{10... | collective-permute-start | bytes 663560 | tf_op jit(solution)/shard_map/ppermute | solution.py:24
  50.1 7.9 %collective-permute-start.14 = (bf16[16,6912]{1,0:T(8,128)(2,1)S(1)}, bf16[16,6912]{1,0:T(8,128)(2,1)S(1)}, u32[]{:S(2)}, u32[]{:S(2)}) collective-permute-start(bf16[16,6912]{1,0:T(8,128)(2,1)S(1)} %get-tuple-element.98), channel_id=1, source_target_pairs={{0,16},{8,24},{16,0},{24,8},{1,17},{9,25},{17,1},{25,9},{2,18},{10... | collective-permute-start | bytes 663560 | tf_op jit(solution)/shard_map/ppermute | solution.py:24
  50.7 7.4 %collective-permute-start.13 = (bf16[16,6912]{1,0:T(8,128)(2,1)S(1)}, bf16[16,6912]{1,0:T(8,128)(2,1)S(1)}, u32[]{:S(2)}, u32[]{:S(2)}) collective-permute-start(bf16[16,6912]{1,0:T(8,128)(2,1)S(1)} %get-tuple-element.98), channel_id=1, source_target_pairs={{0,8},{8,0},{16,24},{24,16},{1,9},{9,1},{17,25},{25,17},{2,10},{10... | collective-permute-start | bytes 663560 | tf_op jit(solution)/shard_map/ppermute | solution.py:24
  61.7 2.5 %collective-permute-start.16 = (f32[4,8,2048]{2,1,0:T(8,128)S(1)}, f32[4,8,2048]{2,1,0:T(8,128)S(1)}, u32[]{:S(2)}, u32[]{:S(2)}) collective-permute-start(f32[4,8,2048]{2,1,0:T(8,128)S(1)} %slice_bitcast_fusion), channel_id=1, source_target_pairs={{0,1},{1,0},{2,3},{3,2},{4,5},{5,4},{6,7},{7,6},{8,9},{9,8},{10,11... | collective-permute-start | bytes 786440 | tf_op jit(solution)/shard_map/ppermute | solution.py:24
  64.3 11.2 %collective-permute-start.17 = (f32[8,2048]{1,0:T(8,128)S(1)}, f32[8,2048]{1,0:T(8,128)S(1)}, u32[]{:S(2)}, u32[]{:S(2)}) collective-permute-start(f32[8,2048]{1,0:T(8,128)S(1)} %get-tuple-element.124), channel_id=1, source_target_pairs={{0,2},{1,3},{2,0},{3,1},{4,6},{5,7},{6,4},{7,5},{8,10},{9,11},{10,... | collective-permute-start | bytes 196616 | tf_op jit(solution)/shard_map/ppermute | solution.py:24
  65.6 9.9 %collective-permute-start.19 = (f32[8,2048]{1,0:T(8,128)S(1)}, f32[8,2048]{1,0:T(8,128)S(1)}, u32[]{:S(2)}, u32[]{:S(2)}) collective-permute-start(f32[8,2048]{1,0:T(8,128)S(1)} %get-tuple-element.125), channel_id=1, source_target_pairs={{0,6},{1,7},{2,4},{3,5},{4,2},{5,3},{6,0},{7,1},{8,14},{9,15},{10,... | collective-permute-start | bytes 196616 | tf_op jit(solution)/shard_map/ppermute | solution.py:24
  68.0 7.5 %collective-permute-start.18 = (f32[8,2048]{1,0:T(8,128)S(1)}, f32[8,2048]{1,0:T(8,128)S(1)}, u32[]{:S(2)}, u32[]{:S(2)}) collective-permute-start(f32[8,2048]{1,0:T(8,128)S(1)} %get-tuple-element.126), channel_id=1, source_target_pairs={{0,4},{1,5},{2,6},{3,7},{4,0},{5,1},{6,2},{7,3},{8,12},{9,13},{10,... | collective-permute-start | bytes 196616 | tf_op jit(solution)/shard_map/ppermute | solution.py:24

commit v5 on v4

--- a/solution.py
+++ b/solution.py
@@ -47,7 +47,7 @@
         refs[-1][i * rows : (i + 1) * rows, :] = ref[...]
 
 
-def order_kernel(rows, me_ref, mine_ref, other_ref, tokens_ref, grads_ref, turned_ref, scratch):
+def order_kernel(rows, me_ref, mine_ref, other_ref, tokens_ref, grads_ref, scratch):
     me = me_ref[0]
     share = rows // 2
     n = mine_ref.shape[0] // rows
@@ -62,10 +62,11 @@
                     half * share : (half + 1) * share
                 ]
         parts = [scratch[half, k ^ me] for k in range(scratch.shape[1])]
-        rows_in_order = jnp.concatenate(parts, axis=0)
-        out[...] = rows_in_order.astype(BF16)
-        if half == 0:
-            turned_ref[...] = rows_in_order.T.astype(BF16)
+        out[...] = jnp.concatenate(parts, axis=0).astype(BF16)
+
+
+def turn_kernel(tokens_ref, after_ref, turned_ref):
+    turned_ref[...] = tokens_ref[...].astype(F32).T.astype(BF16)
 
 
 def weights_copies(sources, wanted, targets, sems):
@@ -288,11 +289,11 @@
         name="join",
     )(mine, *others, fetched)
     far = exchange(near, "col", n_col, 1)
-    tokens, grads, turned = pl.pallas_call(
+    tokens, grads = pl.pallas_call(
         functools.partial(order_kernel, 2 * share),
-        out_shape=[vmem((total, depth), BF16)] * 2 + [vmem((depth, total), BF16)],
+        out_shape=[vmem((total, depth), BF16)] * 2,
         in_specs=[SMEM] + [VMEM] * 2,
-        out_specs=[VMEM] * 3,
+        out_specs=[VMEM] * 2,
         scratch_shapes=[vmem((2, n_row, own, depth), F32)],
         compiler_params=PARAMS,
         name="order",
@@ -352,7 +353,15 @@
 
     keep_one, sends, (gate_two,) = forward(*one, gate_one, up_one, down_one, ((0, *two),), me)
     got_one = to_others(sends)
-    keep_two, sends, (up_two,) = forward(*two, gate_two, None, None, ((1, *two),), me)
+    turned = pl.pallas_call(
+        turn_kernel,
+        out_shape=vmem((depth, total), BF16),
+        in_specs=[VMEM, HBM],
+        out_specs=VMEM,
+        compiler_params=PARAMS,
+        name="turn",
+    )(tokens, keep_one)
+    keep_two, sends, (up_two,) = forward(*two, gate_two, None, None, ((1, *two),), turned)
     mine_one, sends = swiglu(one[1], keep_one, got_one, sends, me)
     got_two = to_others(sends)
     keep_three, sends, (gate_three, up_three, gate_four, up_four, down_four) = forward(

time: 76.3 us -> 76.4 us (level)
  no operation moved by 1% of the time
where the time goes in v5:
time: 76.4 us; the launch traced here: 76.2 us
  Pallas kernels  46.4 us (61%)
  starting transfers between devices  24.3 us (32%)
  waiting for transfers between devices  3.84 us (5%)
  between operations  0.9 us (1%)
    ppermute x20, starting transfers between devices, exchange(): return lax.ppermute(x, axis, [(i, i ^ offset) for i in range(size)])  24.3 us
    pallas_call x4, Pallas kernels, backward(): pl.pallas_call(functools.partial(backward_kernel, n_row, start, width, sh...  21.6 us
    pallas_call x4, Pallas kernels, forward(): pl.pallas_call(functools.partial(forward_kernel, start, width, given, wan...  15 us
    pallas_call x1, Pallas kernels, per_device(): pl.pallas_call(functools.partial(fetch_kernel, wanted), out_shape=held(wa...  4.75 us
    ppermute x20, waiting for transfers between devices, exchange(): return lax.ppermute(x, axis, [(i, i ^ offset) for i in range(size)])  3.84 us
    pallas_call x1, Pallas kernels, per_device(): pl.pallas_call(functools.partial(input_kernel, n_row, ((three[1], shift),...  3.47 us
  transfers between devices with their start and end apart: 20, of which 5 were waited for; matrix products, arithmetic and copies ran while one was open for 0% of the time, Pallas kernels for 51%

profile of v5, /device:TPU:0, one launch (start us, length us, event | category | flops | bytes accessed | tf_op | source)
XLA Modules:
  0.0 76.2 jit_solution(5728379317805859913)
XLA Ops:
  1.4 5.1 %collective-permute-start.2 = (bf16[16,2048]{1,0:T(8,128)(2,1)S(1)}, bf16[16,2048]{1,0:T(8,128)(2,1)S(1)}, u32[]{:S(2)}, u32[]{:S(2)}) collective-permute-start(bf16[16,2048]{1,0:T(8,128)(2,1)S(1)} %pair.1.refs_0_), channel_id=1, source_target_pairs={{0,6},{1,7},{2,4},{3,5},{4,2},{5,3},{6,0},{7,1},{8,14},{9,15},{10,... | collective-permute-start | bytes 196616 | tf_op jit(solution)/shard_map/ppermute | solution.py:24
  7.2 4.8 %fetch.1 = (bf16[2048,1024]{1,0:T(8,128)(2,1)S(1)}, bf16[2048,1024]{1,0:T(8,128)(2,1)S(1)}, bf16[1024,2048]{1,0:T(8,128)(2,1)S(1)}, f32[8,128]{1,0:T(8,128)S(1)}) custom-call(s32[1]{0:T(128)} %bitcast.me_ref.refs_6_.after_ref, bf16[2048,3584]{1,0:T(8,128)(2,1)} %refs_3_.5, bf16[2048,3584]{1,0:T(8,128)(2,1)} %refs_4_.3, bf16[3584,2048]{1,0:T(8,128)(2,1)} %refs_5_.3), custom_call_target="tpu_custom_call" | custom-call | tf_op jit(solution)/shard_map/fetch/pallas_call | solution.py:273
  12.3 1.5 %collective-permute-done.3.other_ref = bf16[64,2048]{1,0:T(8,128)(2,1)S(1)} collective-permute-done((bf16[64,2048]{1,0:T(8,128)(2,1)S(1)}, bf16[64,2048]{1,0:T(8,128)(2,1)S(1)}, u32[]{:S(2)}, u32[]{:S(2)}) %collective-permute-start.3) | collective-permute-done | bytes 262176 | tf_op jit(solution)/shard_map/ppermute | solution.py:24
  13.9 2.9 %forward.4 = (f32[16,3072]{1,0:T(8,128)S(1)}, bf16[16,3072]{1,0:T(8,128)(2,1)S(1)}, bf16[16,3072]{1,0:T(8,128)(2,1)S(1)}, bf16[16,3072]{1,0:T(8,128)(2,1)S(1)}, bf16[2048,1024]{1,0:T(8,128)(2,1)S(1)}) custom-call(s32[1]{0:T(128)} %bitcast.me_ref.refs_6_.after_ref, bf16[64,2048]{1,0:T(8,128)(2,1)S(1)} %get-tuple-element.64.tokens_ref, ...), custom_call_target="tpu_custom_call" | custom-call | tf_op jit(solution)/shard_map/forward/pallas_call | solution.py:310
  16.8 1.6 %collective-permute-start.4 = (bf16[16,3072]{1,0:T(8,128)(2,1)S(1)}, bf16[16,3072]{1,0:T(8,128)(2,1)S(1)}, u32[]{:S(2)}, u32[]{:S(2)}) collective-permute-start(bf16[16,3072]{1,0:T(8,128)(2,1)S(1)} %get-tuple-element.70), channel_id=1, source_target_pairs={{0,8},{8,0},{16,24},{24,16},{1,9},{9,1},{17,25},{25,17},{2,10},{10... | collective-permute-start | bytes 294920 | tf_op jit(solution)/shard_map/ppermute | solution.py:24
  18.4 1.5 %collective-permute-start.5 = (bf16[16,3072]{1,0:T(8,128)(2,1)S(1)}, bf16[16,3072]{1,0:T(8,128)(2,1)S(1)}, u32[]{:S(2)}, u32[]{:S(2)}) collective-permute-start(bf16[16,3072]{1,0:T(8,128)(2,1)S(1)} %get-tuple-element.71), channel_id=1, source_target_pairs={{0,16},{8,24},{16,0},{24,8},{1,17},{9,25},{17,1},{25,9},{2,18},{10... | collective-permute-start | bytes 294920 | tf_op jit(solution)/shard_map/ppermute | solution.py:24
  20.6 4.5 %forward.5 = (f32[16,3072]{1,0:T(8,128)S(1)}, bf16[16,3072]{1,0:T(8,128)(2,1)S(1)}, bf16[16,3072]{1,0:T(8,128)(2,1)S(1)}, bf16[16,3072]{1,0:T(8,128)(2,1)S(1)}, bf16[2048,1024]{1,0:T(8,128)(2,1)S(1)}) custom-call(s32[1]{0:T(128)} %bitcast.me_ref.refs_6_.after_ref, bf16[64,2048]{1,0:T(8,128)(2,1)S(1)} %get-tuple-element.64.tokens_ref, ...), custom_call_target="tpu_custom_call" | custom-call | tf_op jit(solution)/shard_map/forward/pallas_call | solution.py:310
  25.5 1.2 %collective-permute-start.7 = (bf16[16,6144]{1,0:T(8,128)(2,1)S(1)}, bf16[16,6144]{1,0:T(8,128)(2,1)S(1)}, u32[]{:S(2)}, u32[]{:S(2)}) collective-permute-start(bf16[16,6144]{1,0:T(8,128)(2,1)S(1)} %get-tuple-element.78), channel_id=1, source_target_pairs={{0,8},{8,0},{16,24},{24,16},{1,9},{9,1},{17,25},{25,17},{2,10},{10... | collective-permute-start | bytes 589832 | tf_op jit(solution)/shard_map/ppermute | solution.py:24
  26.7 1.5 %collective-permute-start.8 = (bf16[16,6144]{1,0:T(8,128)(2,1)S(1)}, bf16[16,6144]{1,0:T(8,128)(2,1)S(1)}, u32[]{:S(2)}, u32[]{:S(2)}) collective-permute-start(bf16[16,6144]{1,0:T(8,128)(2,1)S(1)} %get-tuple-element.79), channel_id=1, source_target_pairs={{0,16},{8,24},{16,0},{24,8},{1,17},{9,25},{17,1},{25,9},{2,18},{10... | collective-permute-start | bytes 589832 | tf_op jit(solution)/shard_map/ppermute | solution.py:24
  29.1 6.9 %forward.6 = (f32[16,3840]{1,0:T(8,128)S(1)}, bf16[16,3840]{1,0:T(8,128)(2,1)S(1)}, bf16[16,3840]{1,0:T(8,128)(2,1)S(1)}, bf16[16,3840]{1,0:T(8,128)(2,1)S(1)}, ...) custom-call(s32[1]{0:T(128)} %bitcast.me_ref.refs_6_.after_ref, ...), custom_call_target="tpu_custom_call" | custom-call | tf_op jit(solution)/shard_map/forward/pallas_call | solution.py:310
  36.0 0.8 %collective-permute-done.8.refs_1_.refs_2_ = bf16[16,6144]{1,0:T(8,128)(2,1)S(1)} collective-permute-done((bf16[16,6144]{1,0:T(8,128)(2,1)S(1)}, bf16[16,6144]{1,0:T(8,128)(2,1)S(1)}, u32[]{:S(2)}, u32[]{:S(2)}) %collective-permute-start.8) | collective-permute-done | bytes 196640 | tf_op jit(solution)/shard_map/ppermute | solution.py:24
  36.9 1.3 %collective-permute-start.10 = (bf16[16,6912]{1,0:T(8,128)(2,1)S(1)}, bf16[16,6912]{1,0:T(8,128)(2,1)S(1)}, u32[]{:S(2)}, u32[]{:S(2)}) collective-permute-start(bf16[16,6912]{1,0:T(8,128)(2,1)S(1)} %get-tuple-element.88), channel_id=1, source_target_pairs={{0,8},{8,0},{16,24},{24,16},{1,9},{9,1},{17,25},{25,17},{2,10},{10... | collective-permute-start | bytes 663560 | tf_op jit(solution)/shard_map/ppermute | solution.py:24
  38.2 0.8 %collective-permute-start.11 = (bf16[16,6912]{1,0:T(8,128)(2,1)S(1)}, bf16[16,6912]{1,0:T(8,128)(2,1)S(1)}, u32[]{:S(2)}, u32[]{:S(2)}) collective-permute-start(bf16[16,6912]{1,0:T(8,128)(2,1)S(1)} %get-tuple-element.89), channel_id=1, source_target_pairs={{0,16},{8,24},{16,0},{24,8},{1,17},{9,25},{17,1},{25,9},{2,18},{10... | collective-permute-start | bytes 663560 | tf_op jit(solution)/shard_map/ppermute | solution.py:24
  39.0 1.4 %collective-permute-start.12 = (bf16[16,6912]{1,0:T(8,128)(2,1)S(1)}, bf16[16,6912]{1,0:T(8,128)(2,1)S(1)}, u32[]{:S(2)}, u32[]{:S(2)}) collective-permute-start(bf16[16,6912]{1,0:T(8,128)(2,1)S(1)} %get-tuple-element.90), channel_id=1, source_target_pairs={{0,24},{8,16},{16,8},{24,0},{1,25},{9,17},{17,9},{25,1},{2,26},{10... | collective-permute-start | bytes 663560 | tf_op jit(solution)/shard_map/ppermute | solution.py:24
  41.3 6.1 %backward_one.1 = (bf16[2048,3584]{1,0:T(8,128)(2,1)}, bf16[2048,3584]{1,0:T(8,128)(2,1)}, bf16[3584,2048]{1,0:T(8,128)(2,1)}, f32[2048,64]{1,0:T(8,128)S(1)}) custom-call(s32[1]{0:T(128)} %bitcast.me_ref.refs_6_.after_ref, bf16[2048,64]{1,0:T(8,128)(2,1)S(1)} %turn.1.refs_4_.turned_ref, bf16[64,2048]{1,0:T(8,128)(2,1)S(1)} %get-tuple-element.65.grads_ref, ...), custom_call_target="tpu_custom_call" | custom-call | tf_op jit(solution)/shard_map/backward_one/pallas_call | solution.py:337
  47.5 0.9 %collective-permute-done.11.refs_1_.refs_2_ = bf16[16,6912]{1,0:T(8,128)(2,1)S(1)} collective-permute-done((bf16[16,6912]{1,0:T(8,128)(2,1)S(1)}, bf16[16,6912]{1,0:T(8,128)(2,1)S(1)}, u32[]{:S(2)}, u32[]{:S(2)}) %collective-permute-start.11) | collective-permute-done | bytes 221216 | tf_op jit(solution)/shard_map/ppermute | solution.py:24
  48.5 1.6 %collective-permute-start.15 = (bf16[16,6912]{1,0:T(8,128)(2,1)S(1)}, bf16[16,6912]{1,0:T(8,128)(2,1)S(1)}, u32[]{:S(2)}, u32[]{:S(2)}) collective-permute-start(bf16[16,6912]{1,0:T(8,128)(2,1)S(1)} %get-tuple-element.96), channel_id=1, source_target_pairs={{0,24},{8,16},{16,8},{24,0},{1,25},{9,17},{17,9},{25,1},{2,26},{10... | collective-permute-start | bytes 663560 | tf_op jit(solution)/shard_map/ppermute | solution.py:24
  50.7 1.4 %collective-permute-start.13 = (bf16[16,6912]{1,0:T(8,128)(2,1)S(1)}, bf16[16,6912]{1,0:T(8,128)(2,1)S(1)}, u32[]{:S(2)}, u32[]{:S(2)}) collective-permute-start(bf16[16,6912]{1,0:T(8,128)(2,1)S(1)} %get-tuple-element.96), channel_id=1, source_target_pairs={{0,8},{8,0},{16,24},{24,16},{1,9},{9,1},{17,25},{25,17},{2,10},{10... | collective-permute-start | bytes 663560 | tf_op jit(solution)/shard_map/ppermute | solution.py:24
  52.1 6.0 %backward_two.1 = (bf16[2048,3584]{1,0:T(8,128)(2,1)}, bf16[2048,3584]{1,0:T(8,128)(2,1)}, bf16[3584,2048]{1,0:T(8,128)(2,1)}, f32[2048,64]{1,0:T(8,128)S(1)}) custom-call(s32[1]{0:T(128)} %bitcast.me_ref.refs_6_.after_ref, bf16[2048,64]{1,0:T(8,128)(2,1)S(1)} %turn.1.refs_4_.turned_ref, ...), custom_call_target="tpu_custom_call", output_to_operand_aliasing={{0}: (10, {}), {1}: (11, {}), {2}: (12, {})} | custom-call | tf_op jit(solution)/shard_map/backward_two/pallas_call | solution.py:337
  58.2 3.5 %input_grad.1.refs_7_ = f32[64,2048]{1,0:T(8,128)S(1)} custom-call(s32[1]{0:T(128)} %bitcast.me_ref.refs_6_.after_ref, bf16[16,3840]{1,0:T(8,128)(2,1)S(1)} %get-tuple-element.95.refs_10_.refs_0_, bf16[16,6912]{1,0:T(8,128)(2,1)S(1)} %collective-permute-done.13.refs_0_.refs_1_, bf16[16,6912]{1,0:T(8,128)(2,1)S(1)} %collective-permute-done.14.refs_1_.refs_2_, ...), custom_call_target="tpu_custom_call" | custom-call | tf_op jit(solution)/shard_map/input_grad/pallas_call | solution.py:391
  61.8 2.4 %weight_grads_early.1 = (bf16[2048,3584]{1,0:T(8,128)(2,1)}, bf16[2048,3584]{1,0:T(8,128)(2,1)}, bf16[3584,2048]{1,0:T(8,128)(2,1)}) custom-call(s32[1]{0:T(128)} %bitcast.me_ref.refs_6_.after_ref, bf16[2048,64]{1,0:T(8,128)(2,1)S(1)} %turn.1.refs_4_.turned_ref, ...), custom_call_target="tpu_custom_call", output_to_operand_aliasing={{0}: (7, {}), {1}: (8, {}), {2}: (9, {})} | custom-call | tf_op jit(solution)/shard_map/weight_grads_early/pallas_call | solution.py:337
  64.3 1.3 %collective-permute-start.17 = (f32[8,2048]{1,0:T(8,128)S(1)}, f32[8,2048]{1,0:T(8,128)S(1)}, u32[]{:S(2)}, u32[]{:S(2)}) collective-permute-start(f32[8,2048]{1,0:T(8,128)S(1)} %get-tuple-element.122), channel_id=1, source_target_pairs={{0,2},{1,3},{2,0},{3,1},{4,6},{5,7},{6,4},{7,5},{8,10},{9,11},{10,... | collective-permute-start | bytes 196616 | tf_op jit(solution)/shard_map/ppermute | solution.py:24
  65.6 2.5 %collective-permute-start.19 = (f32[8,2048]{1,0:T(8,128)S(1)}, f32[8,2048]{1,0:T(8,128)S(1)}, u32[]{:S(2)}, u32[]{:S(2)}) collective-permute-start(f32[8,2048]{1,0:T(8,128)S(1)} %get-tuple-element.123), channel_id=1, source_target_pairs={{0,6},{1,7},{2,4},{3,5},{4,2},{5,3},{6,0},{7,1},{8,14},{9,15},{10,... | collective-permute-start | bytes 196616 | tf_op jit(solution)/shard_map/ppermute | solution.py:24
  68.5 7.0 %weight_grads.1 = (bf16[2048,3584]{1,0:T(8,128)(2,1)}, bf16[2048,3584]{1,0:T(8,128)(2,1)}, bf16[3584,2048]{1,0:T(8,128)(2,1)}) custom-call(s32[1]{0:T(128)} %bitcast.me_ref.refs_6_.after_ref, bf16[2048,64]{1,0:T(8,128)(2,1)S(1)} %turn.1.refs_4_.turned_ref, ...), custom_call_target="tpu_custom_call", output_to_operand_aliasing={{0}: (7, {}), {1}: (8, {}), {2}: (9, {})} | custom-call | tf_op jit(solution)/shard_map/weight_grads/pallas_call | solution.py:337
  (38 shorter events, 6.8 us)
Async XLA Ops:
  1.4 10.5 %collective-permute-start.2 = (bf16[16,2048]{1,0:T(8,128)(2,1)S(1)}, bf16[16,2048]{1,0:T(8,128)(2,1)S(1)}, u32[]{:S(2)}, u32[]{:S(2)}) collective-permute-start(bf16[16,2048]{1,0:T(8,128)(2,1)S(1)} %pair.1.refs_0_), channel_id=1, source_target_pairs={{0,6},{1,7},{2,4},{3,5},{4,2},{5,3},{6,0},{7,1},{8,14},{9,15},{10,... | collective-permute-start | bytes 196616 | tf_op jit(solution)/shard_map/ppermute | solution.py:24
  6.6 5.6 %collective-permute-start.1 = (bf16[16,2048]{1,0:T(8,128)(2,1)S(1)}, bf16[16,2048]{1,0:T(8,128)(2,1)S(1)}, u32[]{:S(2)}, u32[]{:S(2)}) collective-permute-start(bf16[16,2048]{1,0:T(8,128)(2,1)S(1)} %pair.1.refs_0_), channel_id=1, source_target_pairs={{0,4},{1,5},{2,6},{3,7},{4,0},{5,1},{6,2},{7,3},{8,12},{9,13},{10,... | collective-permute-start | bytes 196616 | tf_op jit(solution)/shard_map/ppermute | solution.py:24
  6.6 5.6 %collective-permute-start = (bf16[16,2048]{1,0:T(8,128)(2,1)S(1)}, bf16[16,2048]{1,0:T(8,128)(2,1)S(1)}, u32[]{:S(2)}, u32[]{:S(2)}) collective-permute-start(bf16[16,2048]{1,0:T(8,128)(2,1)S(1)} %pair.1.refs_0_), channel_id=1, source_target_pairs={{0,2},{1,3},{2,0},{3,1},{4,6},{5,7},{6,4},{7,5},{8,10},{9,11},{10,... | collective-permute-start | bytes 196616 | tf_op jit(solution)/shard_map/ppermute | solution.py:24
  12.2 1.6 %collective-permute-start.3 = (bf16[64,2048]{1,0:T(8,128)(2,1)S(1)}, bf16[64,2048]{1,0:T(8,128)(2,1)S(1)}, u32[]{:S(2)}, u32[]{:S(2)}) collective-permute-start(bf16[64,2048]{1,0:T(8,128)(2,1)S(1)} %join.1.mine_ref), channel_id=1, source_target_pairs={{0,1},{1,0},{2,3},{3,2},{4,5},{5,4},{6,7},{7,6},{8,9},{9,8},{10,11... | collective-permute-start | bytes 786440 | tf_op jit(solution)/shard_map/ppermute | solution.py:24
  16.8 8.2 %collective-permute-start.4 = (bf16[16,3072]{1,0:T(8,128)(2,1)S(1)}, bf16[16,3072]{1,0:T(8,128)(2,1)S(1)}, u32[]{:S(2)}, u32[]{:S(2)}) collective-permute-start(bf16[16,3072]{1,0:T(8,128)(2,1)S(1)} %get-tuple-element.70), channel_id=1, source_target_pairs={{0,8},{8,0},{16,24},{24,16},{1,9},{9,1},{17,25},{25,17},{2,10},{10... | collective-permute-start | bytes 294920 | tf_op jit(solution)/shard_map/ppermute | solution.py:24
  18.4 6.7 %collective-permute-start.5 = (bf16[16,3072]{1,0:T(8,128)(2,1)S(1)}, bf16[16,3072]{1,0:T(8,128)(2,1)S(1)}, u32[]{:S(2)}, u32[]{:S(2)}) collective-permute-start(bf16[16,3072]{1,0:T(8,128)(2,1)S(1)} %get-tuple-element.71), channel_id=1, source_target_pairs={{0,16},{8,24},{16,0},{24,8},{1,17},{9,25},{17,1},{25,9},{2,18},{10... | collective-permute-start | bytes 294920 | tf_op jit(solution)/shard_map/ppermute | solution.py:24
  19.9 5.5 %collective-permute-start.6 = (bf16[16,3072]{1,0:T(8,128)(2,1)S(1)}, bf16[16,3072]{1,0:T(8,128)(2,1)S(1)}, u32[]{:S(2)}, u32[]{:S(2)}) collective-permute-start(bf16[16,3072]{1,0:T(8,128)(2,1)S(1)} %get-tuple-element.72), channel_id=1, source_target_pairs={{0,24},{8,16},{16,8},{24,0},{1,25},{9,17},{17,9},{25,1},{2,26},{10... | collective-permute-start | bytes 294920 | tf_op jit(solution)/shard_map/ppermute | solution.py:24
  25.5 10.4 %collective-permute-start.7 = (bf16[16,6144]{1,0:T(8,128)(2,1)S(1)}, bf16[16,6144]{1,0:T(8,128)(2,1)S(1)}, u32[]{:S(2)}, u32[]{:S(2)}) collective-permute-start(bf16[16,6144]{1,0:T(8,128)(2,1)S(1)} %get-tuple-element.78), channel_id=1, source_target_pairs={{0,8},{8,0},{16,24},{24,16},{1,9},{9,1},{17,25},{25,17},{2,10},{10... | collective-permute-start | bytes 589832 | tf_op jit(solution)/shard_map/ppermute | solution.py:24
  26.7 10.0 %collective-permute-start.8 = (bf16[16,6144]{1,0:T(8,128)(2,1)S(1)}, bf16[16,6144]{1,0:T(8,128)(2,1)S(1)}, u32[]{:S(2)}, u32[]{:S(2)}) collective-permute-start(bf16[16,6144]{1,0:T(8,128)(2,1)S(1)} %get-tuple-element.79), channel_id=1, source_target_pairs={{0,16},{8,24},{16,0},{24,8},{1,17},{9,25},{17,1},{25,9},{2,18},{10... | collective-permute-start | bytes 589832 | tf_op jit(solution)/shard_map/ppermute | solution.py:24
  28.3 8.5 %collective-permute-start.9 = (bf16[16,6144]{1,0:T(8,128)(2,1)S(1)}, bf16[16,6144]{1,0:T(8,128)(2,1)S(1)}, u32[]{:S(2)}, u32[]{:S(2)}) collective-permute-start(bf16[16,6144]{1,0:T(8,128)(2,1)S(1)} %get-tuple-element.80), channel_id=1, source_target_pairs={{0,24},{8,16},{16,8},{24,0},{1,25},{9,17},{17,9},{25,1},{2,26},{10... | collective-permute-start | bytes 589832 | tf_op jit(solution)/shard_map/ppermute | solution.py:24
  36.9 10.5 %collective-permute-start.10 = (bf16[16,6912]{1,0:T(8,128)(2,1)S(1)}, bf16[16,6912]{1,0:T(8,128)(2,1)S(1)}, u32[]{:S(2)}, u32[]{:S(2)}) collective-permute-start(bf16[16,6912]{1,0:T(8,128)(2,1)S(1)} %get-tuple-element.88), channel_id=1, source_target_pairs={{0,8},{8,0},{16,24},{24,16},{1,9},{9,1},{17,25},{25,17},{2,10},{10... | collective-permute-start | bytes 663560 | tf_op jit(solution)/shard_map/ppermute | solution.py:24
  38.2 10.2 %collective-permute-start.11 = (bf16[16,6912]{1,0:T(8,128)(2,1)S(1)}, bf16[16,6912]{1,0:T(8,128)(2,1)S(1)}, u32[]{:S(2)}, u32[]{:S(2)}) collective-permute-start(bf16[16,6912]{1,0:T(8,128)(2,1)S(1)} %get-tuple-element.89), channel_id=1, source_target_pairs={{0,16},{8,24},{16,0},{24,8},{1,17},{9,25},{17,1},{25,9},{2,18},{10... | collective-permute-start | bytes 663560 | tf_op jit(solution)/shard_map/ppermute | solution.py:24
  39.0 9.3 %collective-permute-start.12 = (bf16[16,6912]{1,0:T(8,128)(2,1)S(1)}, bf16[16,6912]{1,0:T(8,128)(2,1)S(1)}, u32[]{:S(2)}, u32[]{:S(2)}) collective-permute-start(bf16[16,6912]{1,0:T(8,128)(2,1)S(1)} %get-tuple-element.90), channel_id=1, source_target_pairs={{0,24},{8,16},{16,8},{24,0},{1,25},{9,17},{17,9},{25,1},{2,26},{10... | collective-permute-start | bytes 663560 | tf_op jit(solution)/shard_map/ppermute | solution.py:24
  48.5 9.6 %collective-permute-start.15 = (bf16[16,6912]{1,0:T(8,128)(2,1)S(1)}, bf16[16,6912]{1,0:T(8,128)(2,1)S(1)}, u32[]{:S(2)}, u32[]{:S(2)}) collective-permute-start(bf16[16,6912]{1,0:T(8,128)(2,1)S(1)} %get-tuple-element.96), channel_id=1, source_target_pairs={{0,24},{8,16},{16,8},{24,0},{1,25},{9,17},{17,9},{25,1},{2,26},{10... | collective-permute-start | bytes 663560 | tf_op jit(solution)/shard_map/ppermute | solution.py:24
  50.2 7.9 %collective-permute-start.14 = (bf16[16,6912]{1,0:T(8,128)(2,1)S(1)}, bf16[16,6912]{1,0:T(8,128)(2,1)S(1)}, u32[]{:S(2)}, u32[]{:S(2)}) collective-permute-start(bf16[16,6912]{1,0:T(8,128)(2,1)S(1)} %get-tuple-element.96), channel_id=1, source_target_pairs={{0,16},{8,24},{16,0},{24,8},{1,17},{9,25},{17,1},{25,9},{2,18},{10... | collective-permute-start | bytes 663560 | tf_op jit(solution)/shard_map/ppermute | solution.py:24
  50.7 7.4 %collective-permute-start.13 = (bf16[16,6912]{1,0:T(8,128)(2,1)S(1)}, bf16[16,6912]{1,0:T(8,128)(2,1)S(1)}, u32[]{:S(2)}, u32[]{:S(2)}) collective-permute-start(bf16[16,6912]{1,0:T(8,128)(2,1)S(1)} %get-tuple-element.96), channel_id=1, source_target_pairs={{0,8},{8,0},{16,24},{24,16},{1,9},{9,1},{17,25},{25,17},{2,10},{10... | collective-permute-start | bytes 663560 | tf_op jit(solution)/shard_map/ppermute | solution.py:24
  61.7 2.5 %collective-permute-start.16 = (f32[4,8,2048]{2,1,0:T(8,128)S(1)}, f32[4,8,2048]{2,1,0:T(8,128)S(1)}, u32[]{:S(2)}, u32[]{:S(2)}) collective-permute-start(f32[4,8,2048]{2,1,0:T(8,128)S(1)} %slice_bitcast_fusion), channel_id=1, source_target_pairs={{0,1},{1,0},{2,3},{3,2},{4,5},{5,4},{6,7},{7,6},{8,9},{9,8},{10,11... | collective-permute-start | bytes 786440 | tf_op jit(solution)/shard_map/ppermute | solution.py:24
  64.3 11.2 %collective-permute-start.17 = (f32[8,2048]{1,0:T(8,128)S(1)}, f32[8,2048]{1,0:T(8,128)S(1)}, u32[]{:S(2)}, u32[]{:S(2)}) collective-permute-start(f32[8,2048]{1,0:T(8,128)S(1)} %get-tuple-element.122), channel_id=1, source_target_pairs={{0,2},{1,3},{2,0},{3,1},{4,6},{5,7},{6,4},{7,5},{8,10},{9,11},{10,... | collective-permute-start | bytes 196616 | tf_op jit(solution)/shard_map/ppermute | solution.py:24
  65.6 10.0 %collective-permute-start.19 = (f32[8,2048]{1,0:T(8,128)S(1)}, f32[8,2048]{1,0:T(8,128)S(1)}, u32[]{:S(2)}, u32[]{:S(2)}) collective-permute-start(f32[8,2048]{1,0:T(8,128)S(1)} %get-tuple-element.123), channel_id=1, source_target_pairs={{0,6},{1,7},{2,4},{3,5},{4,2},{5,3},{6,0},{7,1},{8,14},{9,15},{10,... | collective-permute-start | bytes 196616 | tf_op jit(solution)/shard_map/ppermute | solution.py:24
  68.0 7.5 %collective-permute-start.18 = (f32[8,2048]{1,0:T(8,128)S(1)}, f32[8,2048]{1,0:T(8,128)S(1)}, u32[]{:S(2)}, u32[]{:S(2)}) collective-permute-start(f32[8,2048]{1,0:T(8,128)S(1)} %get-tuple-element.124), channel_id=1, source_target_pairs={{0,4},{1,5},{2,6},{3,7},{4,0},{5,1},{6,2},{7,3},{8,12},{9,13},{10,... | collective-permute-start | bytes 196616 | tf_op jit(solution)/shard_map/ppermute | solution.py:24

commit v6 on v4

--- a/solution.py
+++ b/solution.py
@@ -180,7 +180,7 @@
             others = [r[:, shift + j * width : shift + (j + 1) * width] for r in pieces]
             products.append((ref, jnp.concatenate([mine_ref[:, cols]] + others, axis=0).T))
     own = refs[0].shape[0]
-    for at, size in tiles(sum_ref.shape[0], 512):
+    for at, size in tiles(sum_ref.shape[0], 2048):
         rows = slice(at, at + size)
         part = sum_ref[rows, :]
         for ref, grads in products:

time: 76.3 us -> 76.4 us (level)
  transfers between devices with their start and end apart: 20 -> 20, of which waited for: 5 -> 5; matrix products, arithmetic and copies ran while one was open for 0% -> 0% of each run, Pallas kernels for 51% -> 50%
where the time goes in v6:
time: 76.4 us; the launch traced here: 76.2 us
  Pallas kernels  46.4 us (61%)
  starting transfers between devices  24.3 us (32%)
  waiting for transfers between devices  3.85 us (5%)
  between operations  0.89 us (1%)
    ppermute x20, starting transfers between devices, exchange(): return lax.ppermute(x, axis, [(i, i ^ offset) for i in range(size)])  24.3 us
    pallas_call x4, Pallas kernels, backward(): pl.pallas_call(functools.partial(backward_kernel, n_row, start, width, sh...  21.6 us
    pallas_call x4, Pallas kernels, forward(): pl.pallas_call(functools.partial(forward_kernel, start, width, given, wan...  15 us
    pallas_call x1, Pallas kernels, per_device(): pl.pallas_call(functools.partial(fetch_kernel, wanted), out_shape=held(wa...  4.75 us
    ppermute x20, waiting for transfers between devices, exchange(): return lax.ppermute(x, axis, [(i, i ^ offset) for i in range(size)])  3.85 us
    pallas_call x1, Pallas kernels, per_device(): pl.pallas_call(functools.partial(input_kernel, n_row, ((three[1], shift),...  3.53 us
  transfers between devices with their start and end apart: 20, of which 5 were waited for; matrix products, arithmetic and copies ran while one was open for 0% of the time, Pallas kernels for 50%

profile of v6, /device:TPU:0, one launch (start us, length us, event | category | flops | bytes accessed | tf_op | source)
XLA Modules:
  0.0 76.2 jit_solution(7325616415746202748)
XLA Ops:
  1.4 5.1 %collective-permute-start.2 = (bf16[16,2048]{1,0:T(8,128)(2,1)S(1)}, bf16[16,2048]{1,0:T(8,128)(2,1)S(1)}, u32[]{:S(2)}, u32[]{:S(2)}) collective-permute-start(bf16[16,2048]{1,0:T(8,128)(2,1)S(1)} %pair.1.refs_0_), channel_id=1, source_target_pairs={{0,6},{1,7},{2,4},{3,5},{4,2},{5,3},{6,0},{7,1},{8,14},{9,15},{10,... | collective-permute-start | bytes 196616 | tf_op jit(solution)/shard_map/ppermute | solution.py:24
  7.2 4.8 %fetch.1 = (bf16[2048,1024]{1,0:T(8,128)(2,1)S(1)}, bf16[2048,1024]{1,0:T(8,128)(2,1)S(1)}, bf16[1024,2048]{1,0:T(8,128)(2,1)S(1)}, f32[8,128]{1,0:T(8,128)S(1)}) custom-call(s32[1]{0:T(128)} %bitcast.me_ref.refs_6_.refs_4_.after_ref, bf16[2048,3584]{1,0:T(8,128)(2,1)} %refs_3_.5, bf16[2048,3584]{1,0:T(8,128)(2,1)} %refs_4_.3, bf16[3584,2048]{1,0:T(8,128)(2,1)} %refs_5_.3), custom_call_target="tpu_custom_call" | custom-call | tf_op jit(solution)/shard_map/fetch/pallas_call | solution.py:272
  12.3 1.5 %collective-permute-done.3.other_ref = bf16[64,2048]{1,0:T(8,128)(2,1)S(1)} collective-permute-done((bf16[64,2048]{1,0:T(8,128)(2,1)S(1)}, bf16[64,2048]{1,0:T(8,128)(2,1)S(1)}, u32[]{:S(2)}, u32[]{:S(2)}) %collective-permute-start.3) | collective-permute-done | bytes 262176 | tf_op jit(solution)/shard_map/ppermute | solution.py:24
  14.1 2.9 %forward.4 = (f32[16,3072]{1,0:T(8,128)S(1)}, bf16[16,3072]{1,0:T(8,128)(2,1)S(1)}, bf16[16,3072]{1,0:T(8,128)(2,1)S(1)}, bf16[16,3072]{1,0:T(8,128)(2,1)S(1)}, bf16[2048,1024]{1,0:T(8,128)(2,1)S(1)}) custom-call(s32[1]{0:T(128)} %bitcast.me_ref.refs_6_.refs_4_.after_ref, bf16[64,2048]{1,0:T(8,128)(2,1)S(1)} %get-tuple-element.67.tokens_ref, ...), custom_call_target="tpu_custom_call" | custom-call | tf_op jit(solution)/shard_map/forward/pallas_call | solution.py:309
  17.0 1.6 %collective-permute-start.4 = (bf16[16,3072]{1,0:T(8,128)(2,1)S(1)}, bf16[16,3072]{1,0:T(8,128)(2,1)S(1)}, u32[]{:S(2)}, u32[]{:S(2)}) collective-permute-start(bf16[16,3072]{1,0:T(8,128)(2,1)S(1)} %get-tuple-element.72), channel_id=1, source_target_pairs={{0,8},{8,0},{16,24},{24,16},{1,9},{9,1},{17,25},{25,17},{2,10},{10... | collective-permute-start | bytes 294920 | tf_op jit(solution)/shard_map/ppermute | solution.py:24
  18.5 1.5 %collective-permute-start.5 = (bf16[16,3072]{1,0:T(8,128)(2,1)S(1)}, bf16[16,3072]{1,0:T(8,128)(2,1)S(1)}, u32[]{:S(2)}, u32[]{:S(2)}) collective-permute-start(bf16[16,3072]{1,0:T(8,128)(2,1)S(1)} %get-tuple-element.73), channel_id=1, source_target_pairs={{0,16},{8,24},{16,0},{24,8},{1,17},{9,25},{17,1},{25,9},{2,18},{10... | collective-permute-start | bytes 294920 | tf_op jit(solution)/shard_map/ppermute | solution.py:24
  20.5 4.5 %forward.5 = (f32[16,3072]{1,0:T(8,128)S(1)}, bf16[16,3072]{1,0:T(8,128)(2,1)S(1)}, bf16[16,3072]{1,0:T(8,128)(2,1)S(1)}, bf16[16,3072]{1,0:T(8,128)(2,1)S(1)}, bf16[2048,1024]{1,0:T(8,128)(2,1)S(1)}) custom-call(s32[1]{0:T(128)} %bitcast.me_ref.refs_6_.refs_4_.after_ref, bf16[64,2048]{1,0:T(8,128)(2,1)S(1)} %get-tuple-element.67.tokens_ref, ...), custom_call_target="tpu_custom_call" | custom-call | tf_op jit(solution)/shard_map/forward/pallas_call | solution.py:309
  25.7 1.0 %collective-permute-start.7 = (bf16[16,6144]{1,0:T(8,128)(2,1)S(1)}, bf16[16,6144]{1,0:T(8,128)(2,1)S(1)}, u32[]{:S(2)}, u32[]{:S(2)}) collective-permute-start(bf16[16,6144]{1,0:T(8,128)(2,1)S(1)} %get-tuple-element.80), channel_id=1, source_target_pairs={{0,8},{8,0},{16,24},{24,16},{1,9},{9,1},{17,25},{25,17},{2,10},{10... | collective-permute-start | bytes 589832 | tf_op jit(solution)/shard_map/ppermute | solution.py:24
  26.7 1.5 %collective-permute-start.8 = (bf16[16,6144]{1,0:T(8,128)(2,1)S(1)}, bf16[16,6144]{1,0:T(8,128)(2,1)S(1)}, u32[]{:S(2)}, u32[]{:S(2)}) collective-permute-start(bf16[16,6144]{1,0:T(8,128)(2,1)S(1)} %get-tuple-element.81), channel_id=1, source_target_pairs={{0,16},{8,24},{16,0},{24,8},{1,17},{9,25},{17,1},{25,9},{2,18},{10... | collective-permute-start | bytes 589832 | tf_op jit(solution)/shard_map/ppermute | solution.py:24
  28.2 1.0 %collective-permute-start.9 = (bf16[16,6144]{1,0:T(8,128)(2,1)S(1)}, bf16[16,6144]{1,0:T(8,128)(2,1)S(1)}, u32[]{:S(2)}, u32[]{:S(2)}) collective-permute-start(bf16[16,6144]{1,0:T(8,128)(2,1)S(1)} %get-tuple-element.82), channel_id=1, source_target_pairs={{0,24},{8,16},{16,8},{24,0},{1,25},{9,17},{17,9},{25,1},{2,26},{10... | collective-permute-start | bytes 589832 | tf_op jit(solution)/shard_map/ppermute | solution.py:24
  29.3 6.9 %forward.6 = (f32[16,3840]{1,0:T(8,128)S(1)}, bf16[16,3840]{1,0:T(8,128)(2,1)S(1)}, bf16[16,3840]{1,0:T(8,128)(2,1)S(1)}, bf16[16,3840]{1,0:T(8,128)(2,1)S(1)}, ...) custom-call(s32[1]{0:T(128)} %bitcast.me_ref.refs_6_.refs_4_.after_r, ...), custom_call_target="tpu_custom_call" | custom-call | tf_op jit(solution)/shard_map/forward/pallas_call | solution.py:309
  36.9 1.3 %collective-permute-start.10 = (bf16[16,6912]{1,0:T(8,128)(2,1)S(1)}, bf16[16,6912]{1,0:T(8,128)(2,1)S(1)}, u32[]{:S(2)}, u32[]{:S(2)}) collective-permute-start(bf16[16,6912]{1,0:T(8,128)(2,1)S(1)} %get-tuple-element.90), channel_id=1, source_target_pairs={{0,8},{8,0},{16,24},{24,16},{1,9},{9,1},{17,25},{25,17},{2,10},{10... | collective-permute-start | bytes 663560 | tf_op jit(solution)/shard_map/ppermute | solution.py:24
  38.2 0.9 %collective-permute-start.11 = (bf16[16,6912]{1,0:T(8,128)(2,1)S(1)}, bf16[16,6912]{1,0:T(8,128)(2,1)S(1)}, u32[]{:S(2)}, u32[]{:S(2)}) collective-permute-start(bf16[16,6912]{1,0:T(8,128)(2,1)S(1)} %get-tuple-element.91), channel_id=1, source_target_pairs={{0,16},{8,24},{16,0},{24,8},{1,17},{9,25},{17,1},{25,9},{2,18},{10... | collective-permute-start | bytes 663560 | tf_op jit(solution)/shard_map/ppermute | solution.py:24
  39.1 1.4 %collective-permute-start.12 = (bf16[16,6912]{1,0:T(8,128)(2,1)S(1)}, bf16[16,6912]{1,0:T(8,128)(2,1)S(1)}, u32[]{:S(2)}, u32[]{:S(2)}) collective-permute-start(bf16[16,6912]{1,0:T(8,128)(2,1)S(1)} %get-tuple-element.92), channel_id=1, source_target_pairs={{0,24},{8,16},{16,8},{24,0},{1,25},{9,17},{17,9},{25,1},{2,26},{10... | collective-permute-start | bytes 663560 | tf_op jit(solution)/shard_map/ppermute | solution.py:24
  41.3 6.1 %backward_one.1 = (bf16[2048,3584]{1,0:T(8,128)(2,1)}, bf16[2048,3584]{1,0:T(8,128)(2,1)}, bf16[3584,2048]{1,0:T(8,128)(2,1)}, f32[2048,64]{1,0:T(8,128)S(1)}) custom-call(s32[1]{0:T(128)} %bitcast.me_ref.refs_6_.refs_4_.after_ref, bf16[2048,64]{1,0:T(8,128)(2,1)S(1)} %get-tuple-element.65.turned_ref, bf16[64,2048]{1,0:T(8,128)(2,1)S(1)} %get-tuple-element.66.grads_ref, ...), custom_call_target="tpu_custom_call" | custom-call | tf_op jit(solution)/shard_map/backward_one/pallas_call | solution.py:336
  47.4 0.9 %collective-permute-done.11.refs_1_.refs_2_ = bf16[16,6912]{1,0:T(8,128)(2,1)S(1)} collective-permute-done((bf16[16,6912]{1,0:T(8,128)(2,1)S(1)}, bf16[16,6912]{1,0:T(8,128)(2,1)S(1)}, u32[]{:S(2)}, u32[]{:S(2)}) %collective-permute-start.11) | collective-permute-done | bytes 221216 | tf_op jit(solution)/shard_map/ppermute | solution.py:24
  48.5 1.6 %collective-permute-start.15 = (bf16[16,6912]{1,0:T(8,128)(2,1)S(1)}, bf16[16,6912]{1,0:T(8,128)(2,1)S(1)}, u32[]{:S(2)}, u32[]{:S(2)}) collective-permute-start(bf16[16,6912]{1,0:T(8,128)(2,1)S(1)} %get-tuple-element.98), channel_id=1, source_target_pairs={{0,24},{8,16},{16,8},{24,0},{1,25},{9,17},{17,9},{25,1},{2,26},{10... | collective-permute-start | bytes 663560 | tf_op jit(solution)/shard_map/ppermute | solution.py:24
  50.7 1.4 %collective-permute-start.13 = (bf16[16,6912]{1,0:T(8,128)(2,1)S(1)}, bf16[16,6912]{1,0:T(8,128)(2,1)S(1)}, u32[]{:S(2)}, u32[]{:S(2)}) collective-permute-start(bf16[16,6912]{1,0:T(8,128)(2,1)S(1)} %get-tuple-element.98), channel_id=1, source_target_pairs={{0,8},{8,0},{16,24},{24,16},{1,9},{9,1},{17,25},{25,17},{2,10},{10... | collective-permute-start | bytes 663560 | tf_op jit(solution)/shard_map/ppermute | solution.py:24
  52.0 6.0 %backward_two.1 = (bf16[2048,3584]{1,0:T(8,128)(2,1)}, bf16[2048,3584]{1,0:T(8,128)(2,1)}, bf16[3584,2048]{1,0:T(8,128)(2,1)}, f32[2048,64]{1,0:T(8,128)S(1)}) custom-call(s32[1]{0:T(128)} %bitcast.me_ref.refs_6_.refs_4_.after_ref, bf16[2048,64]{1,0:T(8,128)(2,1)S(1)} %get-tuple-element.65.turned_ref, ...), custom_call_target="tpu_custom_call", output_to_operand_aliasing={{0}: (10, {}), {1}: (11, {}), {2}: (12, {})} | custom-call | tf_op jit(solution)/shard_map/backward_two/pallas_call | solution.py:336
  58.2 3.5 %input_grad.1.refs_7_ = f32[64,2048]{1,0:T(8,128)S(1)} custom-call(s32[1]{0:T(128)} %bitcast.me_ref.refs_6_.refs_4_.after_ref, bf16[16,3840]{1,0:T(8,128)(2,1)S(1)} %get-tuple-element.97.refs_10_.refs_0_, bf16[16,6912]{1,0:T(8,128)(2,1)S(1)} %collective-permute-done.13.refs_0_.refs_1_, bf16[16,6912]{1,0:T(8,128)(2,1)S(1)} %collective-permute-done.14.refs_1_.refs_2_, ...), custom_call_target="tpu_custom_call" | custom-call | tf_op jit(solution)/shard_map/input_grad/pallas_call | solution.py:382
  61.8 2.4 %weight_grads_early.1 = (bf16[2048,3584]{1,0:T(8,128)(2,1)}, bf16[2048,3584]{1,0:T(8,128)(2,1)}, bf16[3584,2048]{1,0:T(8,128)(2,1)}) custom-call(s32[1]{0:T(128)} %bitcast.me_ref.refs_6_.refs_4_.after_ref, bf16[2048,64]{1,0:T(8,128)(2,1)S(1)} %get-tuple-element.65.turned_ref, ...), custom_call_target="tpu_custom_call", output_to_operand_aliasing={{0}: (7, {}), {1}: (8, {}), {2}: (9, {})} | custom-call | tf_op jit(solution)/shard_map/weight_grads_early/pallas_call | solution.py:336
  64.3 1.3 %collective-permute-start.17 = (f32[8,2048]{1,0:T(8,128)S(1)}, f32[8,2048]{1,0:T(8,128)S(1)}, u32[]{:S(2)}, u32[]{:S(2)}) collective-permute-start(f32[8,2048]{1,0:T(8,128)S(1)} %get-tuple-element.124), channel_id=1, source_target_pairs={{0,2},{1,3},{2,0},{3,1},{4,6},{5,7},{6,4},{7,5},{8,10},{9,11},{10,... | collective-permute-start | bytes 196616 | tf_op jit(solution)/shard_map/ppermute | solution.py:24
  65.6 2.4 %collective-permute-start.19 = (f32[8,2048]{1,0:T(8,128)S(1)}, f32[8,2048]{1,0:T(8,128)S(1)}, u32[]{:S(2)}, u32[]{:S(2)}) collective-permute-start(f32[8,2048]{1,0:T(8,128)S(1)} %get-tuple-element.125), channel_id=1, source_target_pairs={{0,6},{1,7},{2,4},{3,5},{4,2},{5,3},{6,0},{7,1},{8,14},{9,15},{10,... | collective-permute-start | bytes 196616 | tf_op jit(solution)/shard_map/ppermute | solution.py:24
  68.5 7.0 %weight_grads.1 = (bf16[2048,3584]{1,0:T(8,128)(2,1)}, bf16[2048,3584]{1,0:T(8,128)(2,1)}, bf16[3584,2048]{1,0:T(8,128)(2,1)}) custom-call(s32[1]{0:T(128)} %bitcast.me_ref.refs_6_.refs_4_.after_ref, bf16[2048,64]{1,0:T(8,128)(2,1)S(1)} %get-tuple-element.65.turned_ref, ...), custom_call_target="tpu_custom_call", output_to_operand_aliasing={{0}: (7, {}), {1}: (8, {}), {2}: (9, {})} | custom-call | tf_op jit(solution)/shard_map/weight_grads/pallas_call | solution.py:336
  (37 shorter events, 6.8 us)
Async XLA Ops:
  1.4 10.5 %collective-permute-start.2 = (bf16[16,2048]{1,0:T(8,128)(2,1)S(1)}, bf16[16,2048]{1,0:T(8,128)(2,1)S(1)}, u32[]{:S(2)}, u32[]{:S(2)}) collective-permute-start(bf16[16,2048]{1,0:T(8,128)(2,1)S(1)} %pair.1.refs_0_), channel_id=1, source_target_pairs={{0,6},{1,7},{2,4},{3,5},{4,2},{5,3},{6,0},{7,1},{8,14},{9,15},{10,... | collective-permute-start | bytes 196616 | tf_op jit(solution)/shard_map/ppermute | solution.py:24
  6.6 5.6 %collective-permute-start.1 = (bf16[16,2048]{1,0:T(8,128)(2,1)S(1)}, bf16[16,2048]{1,0:T(8,128)(2,1)S(1)}, u32[]{:S(2)}, u32[]{:S(2)}) collective-permute-start(bf16[16,2048]{1,0:T(8,128)(2,1)S(1)} %pair.1.refs_0_), channel_id=1, source_target_pairs={{0,4},{1,5},{2,6},{3,7},{4,0},{5,1},{6,2},{7,3},{8,12},{9,13},{10,... | collective-permute-start | bytes 196616 | tf_op jit(solution)/shard_map/ppermute | solution.py:24
  6.6 5.6 %collective-permute-start = (bf16[16,2048]{1,0:T(8,128)(2,1)S(1)}, bf16[16,2048]{1,0:T(8,128)(2,1)S(1)}, u32[]{:S(2)}, u32[]{:S(2)}) collective-permute-start(bf16[16,2048]{1,0:T(8,128)(2,1)S(1)} %pair.1.refs_0_), channel_id=1, source_target_pairs={{0,2},{1,3},{2,0},{3,1},{4,6},{5,7},{6,4},{7,5},{8,10},{9,11},{10,... | collective-permute-start | bytes 196616 | tf_op jit(solution)/shard_map/ppermute | solution.py:24
  12.2 1.6 %collective-permute-start.3 = (bf16[64,2048]{1,0:T(8,128)(2,1)S(1)}, bf16[64,2048]{1,0:T(8,128)(2,1)S(1)}, u32[]{:S(2)}, u32[]{:S(2)}) collective-permute-start(bf16[64,2048]{1,0:T(8,128)(2,1)S(1)} %join.1.mine_ref), channel_id=1, source_target_pairs={{0,1},{1,0},{2,3},{3,2},{4,5},{5,4},{6,7},{7,6},{8,9},{9,8},{10,11... | collective-permute-start | bytes 786440 | tf_op jit(solution)/shard_map/ppermute | solution.py:24
  17.0 8.0 %collective-permute-start.4 = (bf16[16,3072]{1,0:T(8,128)(2,1)S(1)}, bf16[16,3072]{1,0:T(8,128)(2,1)S(1)}, u32[]{:S(2)}, u32[]{:S(2)}) collective-permute-start(bf16[16,3072]{1,0:T(8,128)(2,1)S(1)} %get-tuple-element.72), channel_id=1, source_target_pairs={{0,8},{8,0},{16,24},{24,16},{1,9},{9,1},{17,25},{25,17},{2,10},{10... | collective-permute-start | bytes 294920 | tf_op jit(solution)/shard_map/ppermute | solution.py:24
  18.5 6.5 %collective-permute-start.5 = (bf16[16,3072]{1,0:T(8,128)(2,1)S(1)}, bf16[16,3072]{1,0:T(8,128)(2,1)S(1)}, u32[]{:S(2)}, u32[]{:S(2)}) collective-permute-start(bf16[16,3072]{1,0:T(8,128)(2,1)S(1)} %get-tuple-element.73), channel_id=1, source_target_pairs={{0,16},{8,24},{16,0},{24,8},{1,17},{9,25},{17,1},{25,9},{2,18},{10... | collective-permute-start | bytes 294920 | tf_op jit(solution)/shard_map/ppermute | solution.py:24
  20.1 5.5 %collective-permute-start.6 = (bf16[16,3072]{1,0:T(8,128)(2,1)S(1)}, bf16[16,3072]{1,0:T(8,128)(2,1)S(1)}, u32[]{:S(2)}, u32[]{:S(2)}) collective-permute-start(bf16[16,3072]{1,0:T(8,128)(2,1)S(1)} %get-tuple-element.74), channel_id=1, source_target_pairs={{0,24},{8,16},{16,8},{24,0},{1,25},{9,17},{17,9},{25,1},{2,26},{10... | collective-permute-start | bytes 294920 | tf_op jit(solution)/shard_map/ppermute | solution.py:24
  25.7 10.4 %collective-permute-start.7 = (bf16[16,6144]{1,0:T(8,128)(2,1)S(1)}, bf16[16,6144]{1,0:T(8,128)(2,1)S(1)}, u32[]{:S(2)}, u32[]{:S(2)}) collective-permute-start(bf16[16,6144]{1,0:T(8,128)(2,1)S(1)} %get-tuple-element.80), channel_id=1, source_target_pairs={{0,8},{8,0},{16,24},{24,16},{1,9},{9,1},{17,25},{25,17},{2,10},{10... | collective-permute-start | bytes 589832 | tf_op jit(solution)/shard_map/ppermute | solution.py:24
  26.7 10.0 %collective-permute-start.8 = (bf16[16,6144]{1,0:T(8,128)(2,1)S(1)}, bf16[16,6144]{1,0:T(8,128)(2,1)S(1)}, u32[]{:S(2)}, u32[]{:S(2)}) collective-permute-start(bf16[16,6144]{1,0:T(8,128)(2,1)S(1)} %get-tuple-element.81), channel_id=1, source_target_pairs={{0,16},{8,24},{16,0},{24,8},{1,17},{9,25},{17,1},{25,9},{2,18},{10... | collective-permute-start | bytes 589832 | tf_op jit(solution)/shard_map/ppermute | solution.py:24
  28.2 8.5 %collective-permute-start.9 = (bf16[16,6144]{1,0:T(8,128)(2,1)S(1)}, bf16[16,6144]{1,0:T(8,128)(2,1)S(1)}, u32[]{:S(2)}, u32[]{:S(2)}) collective-permute-start(bf16[16,6144]{1,0:T(8,128)(2,1)S(1)} %get-tuple-element.82), channel_id=1, source_target_pairs={{0,24},{8,16},{16,8},{24,0},{1,25},{9,17},{17,9},{25,1},{2,26},{10... | collective-permute-start | bytes 589832 | tf_op jit(solution)/shard_map/ppermute | solution.py:24
  36.9 10.5 %collective-permute-start.10 = (bf16[16,6912]{1,0:T(8,128)(2,1)S(1)}, bf16[16,6912]{1,0:T(8,128)(2,1)S(1)}, u32[]{:S(2)}, u32[]{:S(2)}) collective-permute-start(bf16[16,6912]{1,0:T(8,128)(2,1)S(1)} %get-tuple-element.90), channel_id=1, source_target_pairs={{0,8},{8,0},{16,24},{24,16},{1,9},{9,1},{17,25},{25,17},{2,10},{10... | collective-permute-start | bytes 663560 | tf_op jit(solution)/shard_map/ppermute | solution.py:24
  38.2 10.2 %collective-permute-start.11 = (bf16[16,6912]{1,0:T(8,128)(2,1)S(1)}, bf16[16,6912]{1,0:T(8,128)(2,1)S(1)}, u32[]{:S(2)}, u32[]{:S(2)}) collective-permute-start(bf16[16,6912]{1,0:T(8,128)(2,1)S(1)} %get-tuple-element.91), channel_id=1, source_target_pairs={{0,16},{8,24},{16,0},{24,8},{1,17},{9,25},{17,1},{25,9},{2,18},{10... | collective-permute-start | bytes 663560 | tf_op jit(solution)/shard_map/ppermute | solution.py:24
  39.1 9.3 %collective-permute-start.12 = (bf16[16,6912]{1,0:T(8,128)(2,1)S(1)}, bf16[16,6912]{1,0:T(8,128)(2,1)S(1)}, u32[]{:S(2)}, u32[]{:S(2)}) collective-permute-start(bf16[16,6912]{1,0:T(8,128)(2,1)S(1)} %get-tuple-element.92), channel_id=1, source_target_pairs={{0,24},{8,16},{16,8},{24,0},{1,25},{9,17},{17,9},{25,1},{2,26},{10... | collective-permute-start | bytes 663560 | tf_op jit(solution)/shard_map/ppermute | solution.py:24
  48.5 9.6 %collective-permute-start.15 = (bf16[16,6912]{1,0:T(8,128)(2,1)S(1)}, bf16[16,6912]{1,0:T(8,128)(2,1)S(1)}, u32[]{:S(2)}, u32[]{:S(2)}) collective-permute-start(bf16[16,6912]{1,0:T(8,128)(2,1)S(1)} %get-tuple-element.98), channel_id=1, source_target_pairs={{0,24},{8,16},{16,8},{24,0},{1,25},{9,17},{17,9},{25,1},{2,26},{10... | collective-permute-start | bytes 663560 | tf_op jit(solution)/shard_map/ppermute | solution.py:24
  50.1 7.9 %collective-permute-start.14 = (bf16[16,6912]{1,0:T(8,128)(2,1)S(1)}, bf16[16,6912]{1,0:T(8,128)(2,1)S(1)}, u32[]{:S(2)}, u32[]{:S(2)}) collective-permute-start(bf16[16,6912]{1,0:T(8,128)(2,1)S(1)} %get-tuple-element.98), channel_id=1, source_target_pairs={{0,16},{8,24},{16,0},{24,8},{1,17},{9,25},{17,1},{25,9},{2,18},{10... | collective-permute-start | bytes 663560 | tf_op jit(solution)/shard_map/ppermute | solution.py:24
  50.7 7.4 %collective-permute-start.13 = (bf16[16,6912]{1,0:T(8,128)(2,1)S(1)}, bf16[16,6912]{1,0:T(8,128)(2,1)S(1)}, u32[]{:S(2)}, u32[]{:S(2)}) collective-permute-start(bf16[16,6912]{1,0:T(8,128)(2,1)S(1)} %get-tuple-element.98), channel_id=1, source_target_pairs={{0,8},{8,0},{16,24},{24,16},{1,9},{9,1},{17,25},{25,17},{2,10},{10... | collective-permute-start | bytes 663560 | tf_op jit(solution)/shard_map/ppermute | solution.py:24
  61.7 2.5 %collective-permute-start.16 = (f32[4,8,2048]{2,1,0:T(8,128)S(1)}, f32[4,8,2048]{2,1,0:T(8,128)S(1)}, u32[]{:S(2)}, u32[]{:S(2)}) collective-permute-start(f32[4,8,2048]{2,1,0:T(8,128)S(1)} %slice_bitcast_fusion), channel_id=1, source_target_pairs={{0,1},{1,0},{2,3},{3,2},{4,5},{5,4},{6,7},{7,6},{8,9},{9,8},{10,11... | collective-permute-start | bytes 786440 | tf_op jit(solution)/shard_map/ppermute | solution.py:24
  64.3 11.2 %collective-permute-start.17 = (f32[8,2048]{1,0:T(8,128)S(1)}, f32[8,2048]{1,0:T(8,128)S(1)}, u32[]{:S(2)}, u32[]{:S(2)}) collective-permute-start(f32[8,2048]{1,0:T(8,128)S(1)} %get-tuple-element.124), channel_id=1, source_target_pairs={{0,2},{1,3},{2,0},{3,1},{4,6},{5,7},{6,4},{7,5},{8,10},{9,11},{10,... | collective-permute-start | bytes 196616 | tf_op jit(solution)/shard_map/ppermute | solution.py:24
  65.6 9.9 %collective-permute-start.19 = (f32[8,2048]{1,0:T(8,128)S(1)}, f32[8,2048]{1,0:T(8,128)S(1)}, u32[]{:S(2)}, u32[]{:S(2)}) collective-permute-start(f32[8,2048]{1,0:T(8,128)S(1)} %get-tuple-element.125), channel_id=1, source_target_pairs={{0,6},{1,7},{2,4},{3,5},{4,2},{5,3},{6,0},{7,1},{8,14},{9,15},{10,... | collective-permute-start | bytes 196616 | tf_op jit(solution)/shard_map/ppermute | solution.py:24
  68.0 7.5 %collective-permute-start.18 = (f32[8,2048]{1,0:T(8,128)S(1)}, f32[8,2048]{1,0:T(8,128)S(1)}, u32[]{:S(2)}, u32[]{:S(2)}) collective-permute-start(f32[8,2048]{1,0:T(8,128)S(1)} %get-tuple-element.126), channel_id=1, source_target_pairs={{0,4},{1,5},{2,6},{3,7},{4,0},{5,1},{6,2},{7,3},{8,12},{9,13},{10,... | collective-permute-start | bytes 196616 | tf_op jit(solution)/shard_map/ppermute | solution.py:24
